TPU v7x, 32 devices: a whole 2x2x4 slice. The times are simulated.
32 devices in a mesh: ctx: 8 (over z, x), exp: 4 (over y, core).
Axes of the slice: x: 2, y: 2, z: 4, core: 2. Of those that a mesh axis runs over, the one named last changes fastest.
Arguments:
- residual: bfloat16 [4, 1024, 2048], P('exp', 'ctx'), may hold values from -6 to 6
- query_heads: bfloat16 [4, 1024, 2048], P('exp', 'ctx'), may hold values from -6.5 to 6.5
- key_heads: bfloat16 [4, 1024, 256], P('exp', 'ctx'), may hold values from -6 to 6
- value_heads: bfloat16 [4, 1024, 256], P('exp', 'ctx'), may hold values from -6 to 6
- norm_gain: float32 [2048], replicated, may hold values from 0.1 to 1.9
- chosen_experts: int32 [4, 1024, 8], P('exp', 'ctx'), may hold values from 0 to 31, all different within a row; in each aligned block of 128 rows (0 to 127, 128 to 255, ..., all dimensions but the last counted through in order) at most 36 rows name the same one
- route_weights: float32 [4, 1024, 8], P('exp', 'ctx'), may hold values from 0.05 to 1
- gate_weight: bfloat16 [32, 2048, 768], P(('ctx', 'exp')), may hold values from -0.125 to 0.125
- up_weight: bfloat16 [32, 2048, 768], P(('ctx', 'exp')), may hold values from -0.125 to 0.125
- down_weight: bfloat16 [32, 768, 2048], P(('ctx', 'exp')), may hold values from -0.21875 to 0.21875
- cotangent: bfloat16 [4, 1024, 2048], P('exp', 'ctx'), may hold values from -6 to 6
Outputs:
- layer_out: bfloat16 [4, 1024, 2048], P('exp', 'ctx')
- residual_gradient: bfloat16 [4, 1024, 2048], P('exp', 'ctx')
- query_gradient: bfloat16 [4, 1024, 2048], P('exp', 'ctx')
- key_gradient: bfloat16 [4, 1024, 256], P('exp', 'ctx')
- value_gradient: bfloat16 [4, 1024, 256], P('exp', 'ctx')
- route_gradient: float32 [4, 1024, 8], P('exp', 'ctx')
Inputs may be any that keep to these rules, and one draw needn't show every extreme that they name: `chosen_experts`: among the rows of one device no expert is named by more than 36 rows, a bound that some block reaches; the 8 experts of a row differ.
All inputs are finite; a program needn't handle non-finite values.
Results may differ from a plain program's by a relative error of at most 0.025.
Values may be sent and summed in bfloat16 or wider, within the bound.
No kernel may reach another device: no remote copies, remote signals or barrier semaphores. Data moves between devices by JAX's collectives and lax.ppermute only.
A program may use at most 192 MiB of HBM per device.

v0:
```python
import jax
import jax.numpy as jnp
from jax import lax
from jax.sharding import PartitionSpec as P

H = 16
KVH = 2
DH = 128
TOPK = 8


NEG = -1e30
EPSILON = 1e-06


def place_rows(begin_row, row_count):
    row_index = begin_row + jnp.arange(row_count, dtype=jnp.int32)
    return row_index


def over_keys(key_local, value_local, visit, start_state):
    return visit(
        start_state,
        (
            lax.all_gather(key_local, "ctx", axis=0, tiled=True),
            lax.all_gather(value_local, "ctx", axis=0, tiled=True),
        ),
        jnp.int32(0),
    )


def to_experts(rows_out):
    return lax.all_to_all(rows_out, ("ctx", "exp"), split_axis=0, concat_axis=0, tiled=True)


def from_experts(rows_back):
    return lax.all_to_all(rows_back, ("ctx", "exp"), split_axis=0, concat_axis=0, tiled=True)


def forward_tile(state, query_half, query_place, key_block, value_block, key_place, score_scale):
    run_max, run_sum, run_acc = state
    scores = (
        jnp.einsum("ikgd,jkd->kgij", query_half, key_block, preferred_element_type=jnp.float32)
        * score_scale
    )
    allowed = key_place[None, :] <= query_place[:, None]
    scores = jnp.where(allowed, scores, NEG)
    new_max = jnp.maximum(run_max, jnp.max(scores, axis=-1))
    weights = jnp.where(allowed, jnp.exp(scores - new_max[..., None]), 0.0)
    run_sum = jnp.sum(weights, axis=-1)
    run_acc = jnp.einsum(
        "kgij,jkd->kgid",
        weights.astype(jnp.bfloat16),
        value_block,
        preferred_element_type=jnp.float32,
    )
    return (new_max, run_sum, run_acc)


def backward_tile(
    query_acc,
    query_half,
    query_place,
    grad_half,
    log_half,
    dot_half,
    key_block,
    value_block,
    key_place,
    score_scale,
):
    scores = (
        jnp.einsum("ikgd,jkd->kgij", query_half, key_block, preferred_element_type=jnp.float32)
        * score_scale
    )
    allowed = key_place[None, :] <= query_place[:, None]
    weights = jnp.where(allowed, jnp.exp(scores - log_half[..., None]), 0.0)
    value_part = jnp.einsum(
        "kgij,ikgd->jkd",
        weights.astype(jnp.bfloat16),
        grad_half,
        preferred_element_type=jnp.float32,
    )
    grad_weights = jnp.einsum(
        "ikgd,jkd->kgij", grad_half, value_block, preferred_element_type=jnp.float32
    )
    grad_scores = (weights * (grad_weights - dot_half[..., None])).astype(jnp.bfloat16)
    query_acc = (
        jnp.einsum("kgij,jkd->kgid", grad_scores, key_block, preferred_element_type=jnp.float32)
        * score_scale
    )
    key_part = (
        jnp.einsum("kgij,ikgd->jkd", grad_scores, query_half, preferred_element_type=jnp.float32)
        * score_scale
    )
    return (query_acc, key_part, value_part)


def per_device(
    residual,
    query_heads,
    key_heads,
    value_heads,
    norm_gain,
    chosen_experts,
    route_weights,
    gate_weight,
    up_weight,
    down_weight,
    cotangent,
):
    shard_rows = residual.shape[1]
    width = residual.shape[2]
    kv_width = key_heads.shape[2]
    query_width = query_heads.shape[2]
    group_size = H // KVH
    half_rows = shard_rows // 2
    ctx_count = lax.axis_size("ctx")
    seq_rows = shard_rows * ctx_count
    score_scale = DH ** (-0.5)
    ctx_index = lax.axis_index("ctx")
    packed = jnp.concatenate([query_heads[0], key_heads[0], value_heads[0]], axis=1)
    query_local = packed[:, :query_width].reshape(shard_rows, KVH, group_size, DH)
    key_local = packed[:, query_width : query_width + kv_width]
    value_local = packed[:, query_width + kv_width :]
    query_place = place_rows(ctx_index * shard_rows, shard_rows)

    def forward_visit(state, piece, begin_row):
        key_rows, value_rows = piece
        row_count = key_rows.shape[0]
        key_block = key_rows.reshape(row_count, KVH, DH)
        value_block = value_rows.reshape(row_count, KVH, DH)
        key_place = place_rows(begin_row, row_count)
        updated = []
        for which_half in range(2):
            query_half = query_local[which_half * half_rows : (which_half + 1) * half_rows]
            place_half = query_place[which_half * half_rows : (which_half + 1) * half_rows]
            updated.append(
                lax.cond(
                    jnp.min(key_place) <= jnp.max(place_half),
                    lambda inner: forward_tile(
                        inner,
                        query_half,
                        place_half,
                        key_block,
                        value_block,
                        key_place,
                        score_scale,
                    ),
                    lambda inner: inner,
                    state[which_half],
                )
            )
        return tuple(updated)

    start_half = (
        jnp.full((KVH, group_size, half_rows), NEG, jnp.float32),
        jnp.zeros((KVH, group_size, half_rows), jnp.float32),
        jnp.zeros((KVH, group_size, half_rows, DH), jnp.float32),
    )
    halves = over_keys(key_local, value_local, forward_visit, (start_half, start_half))
    attended = jnp.concatenate(
        [acc_half / sum_half[..., None] for max_half, sum_half, acc_half in halves], axis=2
    )
    log_sum = jnp.concatenate(
        [max_half + jnp.log(sum_half) for max_half, sum_half, acc_half in halves], axis=2
    )
    attended_local = (
        jnp.transpose(attended, (2, 0, 1, 3)).reshape(shard_rows, query_width).astype(jnp.bfloat16)
    )
    hidden = (residual[0].astype(jnp.float32) + attended_local.astype(jnp.float32)).astype(
        jnp.bfloat16
    )
    hidden_float = hidden.astype(jnp.float32)
    inverse = lax.rsqrt(jnp.mean(hidden_float * hidden_float, axis=-1, keepdims=True) + EPSILON)
    normed = (hidden_float * inverse * norm_gain).astype(jnp.bfloat16)
    expert_count = ctx_count * lax.axis_size("exp")
    capacity = (9 * shard_rows * TOPK + 8 * expert_count - 1) // (8 * expert_count)
    chosen_flat = chosen_experts[0].reshape(-1)
    onehot_hits = (
        chosen_flat[:, None] == jnp.arange(expert_count, dtype=jnp.int32)[None, :]
    ).astype(jnp.int32)
    earlier = jnp.cumsum(onehot_hits, axis=0) - onehot_hits
    slot_index = jnp.sum(earlier * onehot_hits, axis=1)
    target = chosen_flat * capacity + slot_index
    share_raw = route_weights[0]
    route_total = jnp.sum(share_raw, axis=-1, keepdims=True)
    route_share = share_raw / route_total
    cot_float = cotangent[0].astype(jnp.float32)

    def spread(row_values):
        filled = (
            jnp.zeros((expert_count * capacity, width), jnp.bfloat16).at[target].set(row_values)
        )
        return filled.reshape(expert_count, capacity, width)

    gate_mat = gate_weight[0]
    up_mat = up_weight[0]
    down_mat = down_weight[0]
    incoming = to_experts(spread(jnp.repeat(normed, TOPK, axis=0))).reshape(-1, width)
    gate_act = jnp.dot(incoming, gate_mat, preferred_element_type=jnp.float32)
    up_act = jnp.dot(incoming, up_mat, preferred_element_type=jnp.float32)
    activation = (jax.nn.silu(gate_act) * up_act).astype(jnp.bfloat16)
    produced = jnp.dot(activation, down_mat, preferred_element_type=jnp.float32).astype(
        jnp.bfloat16
    )
    returned = from_experts(produced.reshape(expert_count, capacity, width)).reshape(-1, width)
    picked = returned[target].reshape(shard_rows, TOPK, width)
    moe_sum = jnp.sum(route_share[:, :, None] * picked.astype(jnp.float32), axis=1)
    layer_out = (hidden_float + moe_sum).astype(jnp.bfloat16)
    route_dot = jnp.sum(picked.astype(jnp.float32) * cot_float[:, None, :], axis=-1)
    route_gradient = (
        route_dot - jnp.sum(route_share * route_dot, axis=-1, keepdims=True)
    ) / route_total
    out_cot = (
        (route_share[:, :, None] * cot_float[:, None, :]).astype(jnp.bfloat16).reshape(-1, width)
    )
    cot_in = to_experts(spread(out_cot)).reshape(-1, width)
    act_cot = lax.dot_general(
        cot_in, down_mat, (((1,), (1,)), ((), ())), preferred_element_type=jnp.float32
    )
    sigma_gate = jax.nn.sigmoid(gate_act)
    gate_cot = (act_cot * up_act * sigma_gate * (1.0 + gate_act * (1.0 - sigma_gate))).astype(
        jnp.bfloat16
    )
    up_cot = (act_cot * gate_act * sigma_gate).astype(jnp.bfloat16)
    row_cot = (
        lax.dot_general(
            gate_cot, gate_mat, (((1,), (1,)), ((), ())), preferred_element_type=jnp.float32
        )
        + lax.dot_general(
            up_cot, up_mat, (((1,), (1,)), ((), ())), preferred_element_type=jnp.float32
        )
    ).astype(jnp.bfloat16)
    cot_back = from_experts(row_cot.reshape(expert_count, capacity, width)).reshape(-1, width)
    normed_cot = jnp.sum(
        cot_back[target].reshape(shard_rows, TOPK, width).astype(jnp.float32), axis=1
    )
    gained = norm_gain * normed_cot
    hidden_cot = inverse * gained - hidden_float * inverse**3 * jnp.mean(
        hidden_float * gained, axis=-1, keepdims=True
    )
    residual_gradient = (cot_float + hidden_cot).astype(jnp.bfloat16)
    grad_local = residual_gradient.reshape(shard_rows, KVH, group_size, DH)
    attended_rows = attended_local.reshape(shard_rows, KVH, group_size, DH)
    row_dot = jnp.einsum(
        "ikgd,ikgd->kgi", grad_local, attended_rows, preferred_element_type=jnp.float32
    )

    def backward_visit(state, piece, begin_row):
        query_accs, key_total, value_total = state
        key_rows, value_rows = piece
        row_count = key_rows.shape[0]
        key_block = key_rows.reshape(row_count, KVH, DH)
        value_block = value_rows.reshape(row_count, KVH, DH)
        key_place = place_rows(begin_row, row_count)
        empty_block = jnp.zeros((row_count, KVH, DH), jnp.float32)
        key_sum = empty_block
        value_sum = empty_block
        new_accs = []
        for which_half in range(2):
            lower = which_half * half_rows
            upper = lower + half_rows
            query_half = query_local[lower:upper]
            place_half = query_place[lower:upper]
            grad_half = grad_local[lower:upper]
            log_half = log_sum[:, :, lower:upper]
            dot_half = row_dot[:, :, lower:upper]
            query_acc, key_part, value_part = lax.cond(
                jnp.min(key_place) <= jnp.max(place_half),
                lambda inner: backward_tile(
                    inner,
                    query_half,
                    place_half,
                    grad_half,
                    log_half,
                    dot_half,
                    key_block,
                    value_block,
                    key_place,
                    score_scale,
                ),
                lambda inner: (inner, empty_block, empty_block),
                query_accs[which_half],
            )
            new_accs.append(query_acc)
            key_sum = key_sum + key_part
            value_sum = value_sum + value_part
        key_total = key_sum.reshape(row_count, -1)
        value_total = value_sum.reshape(row_count, -1)
        return (tuple(new_accs), key_total, value_total)

    empty_query = jnp.zeros((KVH, group_size, half_rows, DH), jnp.float32)
    empty_keys = jnp.zeros((seq_rows, kv_width), jnp.float32)
    query_accs, key_total, value_total = over_keys(
        key_local, value_local, backward_visit, ((empty_query, empty_query), empty_keys, empty_keys)
    )
    key_own, value_own = (
        lax.psum_scatter(
            key_total.astype(jnp.bfloat16), "ctx", scatter_dimension=0, tiled=True
        ).astype(jnp.float32),
        lax.psum_scatter(
            value_total.astype(jnp.bfloat16), "ctx", scatter_dimension=0, tiled=True
        ).astype(jnp.float32),
    )
    query_grad = jnp.transpose(jnp.concatenate(query_accs, axis=2), (2, 0, 1, 3)).reshape(
        shard_rows, query_width
    )
    grads_packed = jnp.concatenate(
        [
            query_grad.astype(jnp.bfloat16),
            key_own.astype(jnp.bfloat16),
            value_own.astype(jnp.bfloat16),
        ],
        axis=1,
    )
    query_gradient = grads_packed[:, :query_width]
    key_gradient = grads_packed[:, query_width : query_width + kv_width]
    value_gradient = grads_packed[:, query_width + kv_width :]
    return (
        layer_out[None],
        residual_gradient[None],
        query_gradient[None],
        key_gradient[None],
        value_gradient[None],
        route_gradient[None],
    )


def solution(mesh):
    in_specs = (
        P("exp", "ctx", None),
        P("exp", "ctx", None),
        P("exp", "ctx", None),
        P("exp", "ctx", None),
        P(),
        P("exp", "ctx", None),
        P("exp", "ctx", None),
        P(("ctx", "exp"), None, None),
        P(("ctx", "exp"), None, None),
        P(("ctx", "exp"), None, None),
        P("exp", "ctx", None),
    )
    out_specs = (
        P("exp", "ctx", None),
        P("exp", "ctx", None),
        P("exp", "ctx", None),
        P("exp", "ctx", None),
        P("exp", "ctx", None),
        P("exp", "ctx", None),
    )
    return jax.shard_map(
        per_device, mesh=mesh, in_specs=in_specs, out_specs=out_specs, check_vma=False
    )
```

profile of v0, /device:TPU:0, one launch (start us, length us, event | category | flops | bytes accessed | tf_op | source)
XLA Modules:
  0.0 781.4 jit_solution(3407579729371419643)
XLA Ops:
  12.3 30.7 %all-gather = bf16[1,1024,256]{1,2,0:T(8,128)(2,1)} all-gather(bf16[1,128,256]{1,2,0:T(8,128)(2,1)S(1)} %copy.64), channel_id=2, replica_groups=mesh['ctx'=8,'exp'=4] {'ctx'}, dimensions={1}, use_global_device_ids=true | all-gather | bytes 589824 | tf_op jit(solution)/shard_map/all_gather | solution.py:25
  44.0 28.6 %all-gather.1 = bf16[1,1024,256]{1,2,0:T(8,128)(2,1)} all-gather(bf16[1,128,256]{1,2,0:T(8,128)(2,1)S(1)} %copy.65), channel_id=3, replica_groups=mesh['ctx'=8,'exp'=4] {'ctx'}, dimensions={1}, use_global_device_ids=true | all-gather | bytes 589824 | tf_op jit(solution)/shard_map/all_gather | solution.py:26
  77.4 8.5 %conditional.4 = (f32[2,8,64]{2,1,0:T(8,128)}, f32[2,8,64]{2,1,0:T(8,128)}, f32[2,8,64,128]{3,2,1,0:T(8,128)S(1)}, f32[2,8,64]{2,1,0:T(8,128)S(1)}) conditional(s32[]{:T(128)} %convert_element_type.215, () %tuple.44, (s32[1024]{0:T(1024)S(1)}, s32[64]{0:T(128)}, bf16[1024,2,128]{0,2,1:T(8,128)(2,1)}, bf16[64,2,8,128]{3,2,1,0:T(8,128)(2,1)}, ...), branch_computations={%region_1.0_spmd, %region_2.5_spmd} | conditional | flops 550566912 | bytes 16814396 | solution.py:139
  78.1 2.1 fusion
  80.8 2.6 fusion.2
  86.7 8.0 %conditional.5 = (f32[2,8,64]{2,1,0:T(8,128)}, f32[2,8,64]{2,1,0:T(8,128)}, f32[2,8,64,128]{3,2,1,0:T(8,128)S(1)}, f32[2,8,64]{2,1,0:T(8,128)S(1)}) conditional(s32[]{:T(128)} %convert_element_type.216, () %tuple.46, (s32[1024]{0:T(1024)S(1)}, s32[64]{0:T(128)S(1)}, bf16[1024,2,128]{0,2,1:T(8,128)(2,1)}, bf16[64,2,8,128]{3,2,1,0:T(8,128)(2,1)S(1)}, ...), branch_computations={%region_6.7_spmd, %region_7.10_spmd} | conditional | flops 550566912 | bytes 16814396 | solution.py:139
  86.8 2.0 fusion.13
  89.4 2.6 fusion.15
  100.5 15.7 %reduce-window.6 = s32[32,8,128]{2,1,0:T(8,128)S(1)} reduce-window(s32[32,8,128]{2,1,0:T(8,128)} %fusion.131, s32[]{:T(128)} %constant.40.clone.1), window={size=1x1x128 pad=0_0x0_0x127_0}, to_apply=%region_11.0 | reduce-window | flops 4161536 | bytes 262148 | tf_op jit(solution)/shard_map/reduce-window
  124.5 2.0 fusion.114
  126.6 9.8 %scatter_custom_fusion = bf16[1152,2048]{1,0:T(8,128)(2,1)} fusion(s32[1024]{0:T(1024)S(1)} %bitcast.311, bf16[]{:T(256)} %constant.48.clone.1, bf16[128,2048]{1,0:T(8,128)(2,1)} %fusion.114), kind=kCustom, calls=%fused_computation.106 | custom fusion | bytes 5242882 | tf_op jit(solution)/shard_map/scatter | solution.py:193
  136.4 7.2 reshape.371
  143.6 3.9 all-to-all-start
  148.4 2.7 convert_bitcast_fusion
  151.1 10.2 %scatter_custom_fusion.1 = bf16[1152,2048]{1,0:T(8,128)(2,1)} fusion(s32[1024]{0:T(1024)S(1)} %bitcast.312, f32[128,2048]{1,0:T(8,128)} %get-tuple-element.205, f32[1024]{0:T(1024)S(1)} %div.68, bf16[]{:T(256)} %constant.48.clone.1), kind=kCustom, calls=%fused_computation.105 | custom fusion | flops 4194304 | bytes 5771266 | tf_op jit(solution)/shard_map/scatter | solution.py:193
  161.3 7.2 reshape.375
  168.5 96.2 %all-to-all-done = bf16[32,36,2048]{2,1,0:T(8,128)(2,1)} async-done(((bf16[32,36,2048]{2,1,0:T(8,128)(2,1)}), bf16[32,36,2048]{2,1,0:T(8,128)(2,1)}, u32[]{:S(2)}, u32[]{:S(2)}) %all-to-all-start) | async-done | bytes 4718624 | tf_op jit(solution)/shard_map/all_to_all | solution.py:33
  264.7 5.2 all-to-all-start.2
  270.0 7.3 reshape.372
  277.3 9.1 %fusion.93 = f32[1152,768]{1,0:T(8,128)} fusion(bf16[1152,2048]{1,0:T(8,128)(2,1)} %reshape.372, bf16[1,2048,768]{2,1,0:T(8,128)(2,1)} %param.27), kind=kOutput, calls=%fused_computation.118 | convolution fusion | flops 3623878656 | bytes 11403264 | tf_op jit(solution)/shard_map/dot_general | solution.py:202
  286.4 5.6 fusion.97
  292.0 95.2 %all-to-all-done.2 = bf16[32,36,2048]{2,1,0:T(8,128)(2,1)} async-done(((bf16[32,36,2048]{2,1,0:T(8,128)(2,1)}), bf16[32,36,2048]{2,1,0:T(8,128)(2,1)}, u32[]{:S(2)}, u32[]{:S(2)}) %all-to-all-start.2) | async-done | bytes 4718624 | tf_op jit(solution)/shard_map/all_to_all | solution.py:33
  387.2 7.2 reshape.376
  394.4 6.8 fusion.89
  401.3 8.2 %fusion.95 = f32[1152,2048]{1,0:T(8,128)} fusion(bf16[1,2048,768]{2,1,0:T(8,128)(2,1)S(1)} %copy-done, f32[1152,768]{1,0:T(8,128)S(1)} %copy-done.47, f32[1152,768]{1,0:T(8,128)S(1)} %fusion.89, f32[1152,768]{1,0:T(8,128)S(1)} %copy-done.48), kind=kOutput, calls=%fused_computation.120 | convolution fusion | flops 3632726016 | bytes 23199744 | tf_op jit(solution)/shard_map/dot_general | solution.py:228
  409.5 8.0 %add_convert_fusion = bf16[1152,2048]{1,0:T(8,128)(2,1)} fusion(f32[1152,2048]{1,0:T(8,128)} %fusion.95, bf16[1,2048,768]{2,1,0:T(8,128)(2,1)S(1)} %copy-done.45, f32[1152,768]{1,0:T(8,128)S(1)} %fusion.89, f32[1152,768]{1,0:T(8,128)S(1)} %copy-done.47), kind=kOutput, calls=%fused_computation.98 | convolution fusion | flops 3633905664 | bytes 24379392 | tf_op jit(solution)/shard_map/dot_general | solution.py:231
  417.5 17.4 %reshape.377 = bf16[32,36,2048]{2,1,0:T(8,128)(2,1)} reshape(bf16[1152,2048]{1,0:T(8,128)(2,1)} %add_convert_fusion) | data formatting | bytes 9437184 | tf_op jit(solution)/shard_map/reshape | solution.py:235
  434.9 5.1 all-to-all-start.3
  440.0 8.7 %convolution_convert_fusion = bf16[1152,2048]{1,0:T(8,128)(2,1)} fusion(bf16[1,768,2048]{2,1,0:T(8,128)(2,1)S(1)} %copy-done.46, f32[1152,768]{1,0:T(8,128)} %fusion.93, f32[1152,768]{1,0:T(8,128)} %fusion.97), kind=kOutput, calls=%fused_computation.104 | convolution fusion | flops 3631546368 | bytes 14942208 | tf_op jit(solution)/shard_map/dot_general | solution.py:204
  448.7 7.2 reshape.373
  456.0 101.2 %all-to-all-done.3 = bf16[32,36,2048]{2,1,0:T(8,128)(2,1)} async-done(((bf16[32,36,2048]{2,1,0:T(8,128)(2,1)}), bf16[32,36,2048]{2,1,0:T(8,128)(2,1)}, u32[]{:S(2)}, u32[]{:S(2)}) %all-to-all-start.3) | async-done | bytes 4718624 | tf_op jit(solution)/shard_map/all_to_all | solution.py:37
  557.2 5.1 all-to-all-start.1
  564.8 7.3 reshape.378
  572.1 11.8 %gather_fusion.1 = bf16[1024,2048]{1,0:T(8,128)(2,1)} fusion(bf16[1152,2048]{1,0:T(8,128)(2,1)} %reshape.378, s32[1024]{0:T(1024)S(1)} %broadcast_clamp_fusion), kind=kCustom, calls=%fused_computation.1 | custom fusion | bytes 8392704 | tf_op jit(solution)/shard_map/gather | solution.py:237
  583.9 5.2 convert_reduce_fusion
  592.8 8.8 %conditional.6 = (f32[1024,2,128]{2,0,1:T(8,128)S(1)}, f32[1024,2,128]{2,0,1:T(8,128)S(1)}, bf16[2,8,64,128]{3,2,1,0:T(8,128)(2,1)S(1)}) conditional(s32[]{:T(128)} %convert_element_type.215, () %tuple.48, (s32[1024]{0:T(1024)S(1)}, s32[64]{0:T(128)}, bf16[1024,2,128]{0,2,1:T(8,128)(2,1)S(1)}, bf16[64,2,8,128]{3,2,1,0:T(8,128)(2,1)S(1)}, ...), branch_computations={%region_20.21_spmd, %region_21.22_spmd} | conditional | flops 1353253888 | bytes 25129240 | solution.py:269
  596.0 2.2 fusion.27
  602.7 9.0 %conditional.7 = (f32[1024,2,128]{2,0,1:T(8,128)}, f32[1024,2,128]{2,0,1:T(8,128)S(1)}, bf16[2,8,64,128]{3,2,1,0:T(8,128)(2,1)S(1)}) conditional(s32[]{:T(128)} %convert_element_type.216, () %tuple.50, (s32[1024]{0:T(1024)S(1)}, s32[64]{0:T(128)}, bf16[1024,2,128]{0,2,1:T(8,128)(2,1)S(1)}, bf16[64,2,8,128]{3,2,1,0:T(8,128)(2,1)S(1)}, ...), branch_computations={%region_22.23_spmd, %region_23.24_spmd} | conditional | flops 1353253888 | bytes 27252076 | solution.py:269
  607.5 1.9 fusion.68
  611.7 2.3 copy_bitcast_fusion
  615.3 69.1 %all-to-all-done.1 = bf16[32,36,2048]{2,1,0:T(8,128)(2,1)} async-done(((bf16[32,36,2048]{2,1,0:T(8,128)(2,1)}), bf16[32,36,2048]{2,1,0:T(8,128)(2,1)}, u32[]{:S(2)}, u32[]{:S(2)}) %all-to-all-start.1) | async-done | bytes 4718624 | tf_op jit(solution)/shard_map/all_to_all | solution.py:37
  684.4 7.3 reshape.374
  691.7 11.8 %gather_fusion = bf16[1024,2048]{1,0:T(8,128)(2,1)} fusion(bf16[1152,2048]{1,0:T(8,128)(2,1)} %reshape.374, s32[1024]{0:T(1024)S(1)} %broadcast_clamp_fusion), kind=kCustom, calls=%fused_computation | custom fusion | bytes 8392704 | tf_op jit(solution)/shard_map/gather | solution.py:208
  703.5 2.1 copy_bitcast_fusion.1
  705.7 5.9 fusion.81
  714.8 2.1 convert_element_type.257
  716.9 3.6 fusion.111
  720.4 53.9 %reduce-scatter.3.cloned.1.call-done = bf16[128,256]{1,0:T(8,128)(2,1)} async-done(((bf16[1024,256]{1,0:T(8,128)(2,1)}), bf16[128,256]{1,0:T(8,128)(2,1)}) %reduce-scatter.3.cloned.1.call-update) | async-done | bytes 65552 | tf_op jit(solution)/shard_map/reduce_scatter | solution.py:299
  (181 shorter events, 57.2 us)
Async XLA Ops:
  7.2 279.2 %copy-start = (bf16[1,2048,768]{2,1,0:T(8,128)(2,1)S(1)}, bf16[1,2048,768]{2,1,0:T(8,128)(2,1)}, u32[]{:S(2)}) copy-start(bf16[1,2048,768]{2,1,0:T(8,128)(2,1)} %param.26) | copy-start | bytes 9437188
  11.3 74.6 %copy-start.39 = (s32[64]{0:T(128)}, s32[64]{0:T(128)S(1)}, u32[]{:S(2)}) copy-start(s32[64]{0:T(128)S(1)} %get-tuple-element.211) | copy-start | bytes 772
  78.1 6.0 copy-start.26
  86.8 5.9 copy-start.27
  94.7 5.1 copy-start.32
  94.7 3.3 copy-start.8
  94.7 29.8 %copy-start.29 = (f32[2048]{0:T(1024)S(1)}, f32[2048]{0:T(1024)}, u32[]{:S(2)}) copy-start(f32[2048]{0:T(1024)} %param.23) | copy-start | bytes 24580
  143.6 4.0 copy-start.34
  143.6 121.2 %all-to-all-start = ((bf16[32,36,2048]{2,1,0:T(8,128)(2,1)}), bf16[32,36,2048]{2,1,0:T(8,128)(2,1)}, u32[]{:S(2)}, u32[]{:S(2)}) async-start(bf16[32,36,2048]{2,1,0:T(8,128)(2,1)} %reshape.371), calls=%async_computation | async-start | bytes 10485760 | tf_op jit(solution)/shard_map/all_to_all | solution.py:33
  264.7 122.4 %all-to-all-start.2 = ((bf16[32,36,2048]{2,1,0:T(8,128)(2,1)}), bf16[32,36,2048]{2,1,0:T(8,128)(2,1)}, u32[]{:S(2)}, u32[]{:S(2)}) async-start(bf16[32,36,2048]{2,1,0:T(8,128)(2,1)} %reshape.375), calls=%async_computation.2 | async-start | bytes 10485760 | tf_op jit(solution)/shard_map/all_to_all | solution.py:33
  277.3 9.1 %copy-start.11 = (bf16[1152,2048]{1,0:T(8,128)(2,1)S(1)}, bf16[1152,2048]{1,0:T(8,128)(2,1)}, u32[]{:S(2)}) copy-start(bf16[1152,2048]{1,0:T(8,128)(2,1)} %reshape.372) | copy-start | bytes 14155780
  394.4 6.9 copy-start.47
  394.4 6.9 copy-start.48
  401.3 8.2 %copy-start.45 = (bf16[1,2048,768]{2,1,0:T(8,128)(2,1)S(1)}, bf16[1,2048,768]{2,1,0:T(8,128)(2,1)}, u32[]{:S(2)}) copy-start(bf16[1,2048,768]{2,1,0:T(8,128)(2,1)} %param.27) | copy-start | bytes 9437188
  434.9 5.1 copy-start.46
  434.9 122.3 %all-to-all-start.3 = ((bf16[32,36,2048]{2,1,0:T(8,128)(2,1)}), bf16[32,36,2048]{2,1,0:T(8,128)(2,1)}, u32[]{:S(2)}, u32[]{:S(2)}) async-start(bf16[32,36,2048]{2,1,0:T(8,128)(2,1)} %reshape.377), calls=%async_computation.3 | async-start | bytes 10485760 | tf_op jit(solution)/shard_map/all_to_all | solution.py:37
  455.9 106.4 %copy-start.14 = (f32[16,8,16,128]{3,1,2,0:T(8,128)S(1)}, f32[16,8,16,128]{3,1,2,0:T(8,128)}, u32[]{:S(2)}) copy-start(f32[16,8,16,128]{3,1,2,0:T(8,128)} %get-tuple-element.204) | copy-start | bytes 3145732
  455.9 107.6 %copy-start.9 = (bf16[1,128,2048]{2,1,0:T(8,128)(2,1)S(1)}, bf16[1,128,2048]{2,1,0:T(8,128)(2,1)}, u32[]{:S(2)}) copy-start(bf16[1,128,2048]{2,1,0:T(8,128)(2,1)} %param.19) | copy-start | bytes 1572868
  557.2 127.2 %all-to-all-start.1 = ((bf16[32,36,2048]{2,1,0:T(8,128)(2,1)}), bf16[32,36,2048]{2,1,0:T(8,128)(2,1)}, u32[]{:S(2)}, u32[]{:S(2)}) async-start(bf16[32,36,2048]{2,1,0:T(8,128)(2,1)} %reshape.373), calls=%async_computation.1 | async-start | bytes 10485760 | tf_op jit(solution)/shard_map/all_to_all | solution.py:37
  562.3 158.1 %reduce-scatter.5.cloned.1.call-start = ((), (), s32[]{:S(2)}) async-start(), calls=%async_computation.7 | async-start | bytes 589824 | tf_op jit(solution)/shard_map/reduce_scatter | solution.py:302
  583.9 5.5 copy-start.7
  583.9 5.7 copy-start.12
  583.9 5.7 copy-start.13
  583.9 5.8 copy-start.18
  583.9 5.8 copy-start.20
  583.9 5.8 copy-start.37
  583.9 5.8 copy-start.41
  589.1 3.6 copy-start.2
  589.2 2.3 copy-start.10
  589.4 3.4 copy-start.3
  589.4 3.4 copy-start.16
  589.4 3.4 copy-start.25
  589.4 3.4 copy-start.31
  589.6 3.2 copy-start.43
  601.6 1.0 copy-start.22
  602.6 11.5 %copy-start.5 = (f32[128,2,8,128]{3,2,1,0:T(8,128)S(1)}, f32[128,2,8,128]{3,2,1,0:T(8,128)}, u32[]{:S(2)}) copy-start(f32[128,2,8,128]{3,2,1,0:T(8,128)} %copy-done.4) | copy-start | bytes 3145732
  602.7 1.7 copy-start.40
  602.7 1.8 copy-start.33
  602.7 3.3 copy-start.28
  611.7 80.0 %copy-start.24 = (bf16[2,8,64,128]{3,2,1,0:T(8,128)(2,1)}, bf16[2,8,64,128]{3,2,1,0:T(8,128)(2,1)S(1)}, u32[]{:S(2)}) copy-start(bf16[2,8,64,128]{3,2,1,0:T(8,128)(2,1)S(1)} %get-tuple-element.129) | copy-start | bytes 786436
  611.7 3.5 copy-start.36
  614.0 160.3 %reduce-scatter.3.cloned.1.call-start = ((), (), s32[]{:S(2)}) async-start(), calls=%async_computation.6 | async-start | bytes 589824 | tf_op jit(solution)/shard_map/reduce_scatter | solution.py:299
  691.7 14.0 %copy-start.6 = (f32[128,2048]{1,0:T(8,128)S(1)}, f32[128,2048]{1,0:T(8,128)}, u32[]{:S(2)}) copy-start(f32[128,2048]{1,0:T(8,128)} %get-tuple-element.205) | copy-start | bytes 3145732
  705.6 6.9 copy-start.23
  705.6 11.2 %copy-start.38 = (f32[128]{0:T(128)S(1)}, f32[128]{0:T(128)}, u32[]{:S(2)}) copy-start(f32[128]{0:T(128)} %get-tuple-element.209) | copy-start | bytes 1540
  705.6 11.2 %copy-start.42 = (f32[128]{0:T(128)S(1)}, f32[128]{0:T(128)}, u32[]{:S(2)}) copy-start(f32[128]{0:T(128)} %get-tuple-element.208) | copy-start | bytes 1540
  705.6 11.2 %copy-start.44 = (f32[128]{0:T(128)S(1)}, f32[128]{0:T(128)}, u32[]{:S(2)}) copy-start(f32[128]{0:T(128)} %copy-done.43) | copy-start | bytes 1540
  712.5 61.9 %copy-start.1 = (bf16[1,2048,768]{2,1,0:T(8,128)(2,1)S(1)}, bf16[1,2048,768]{2,1,0:T(8,128)(2,1)}, u32[]{:S(2)}) copy-start(bf16[1,2048,768]{2,1,0:T(8,128)(2,1)} %param.26) | copy-start | bytes 9437188
  (7 other events, 5.4 us)
Sparse Core Ops, SparseCore 0:
  614.2 76.7 reduce-scatter.4
  711.7 62.6 reduce-scatter.2
where the time goes:
time: 791 us; the launch traced here: 781 us
  waiting for transfers between devices  416 us (53%)
  local copies, waits for them, and re-layouts  130 us (16%)
  other arithmetic  73.6 us (9%)
  matrix products  66.5 us (8%)
  blocking collectives  59.3 us (7%)
  starting transfers between devices  19.4 us (2%)
  between operations  16.2 us (2%)
    all_to_all x2, waiting for transfers between devices, to_experts(): lax.all_to_all(rows_out, ('ctx', 'exp'), split_axis=0, concat_axis=0, til...  191 us
    all_to_all x2, waiting for transfers between devices, from_experts(): lax.all_to_all(rows_back, ('ctx', 'exp'), split_axis=0, concat_axis=0, ti...  170 us
    reduce_scatter x1, waiting for transfers between devices, per_device(): lax.psum_scatter(key_total.astype(jnp.bfloat16), 'ctx', scatter_dimension...  53.9 us
    all_gather x1, blocking collectives, over_keys(): lax.all_gather(key_local, 'ctx', axis=0, tiled=True)  30.7 us
    all_gather x1, blocking collectives, over_keys(): lax.all_gather(value_local, 'ctx', axis=0, tiled=True)  28.6 us
    another operation x3, other arithmetic  17.9 us
    reshape x1, local copies, waits for them, and re-layouts, per_device(): row_cot.reshape(expert_count, capacity, width)  17.4 us
  transfers between devices with their start and end apart: 6, of which 5 were waited for; matrix products, arithmetic and copies ran while one was open for 19% of the time, Pallas kernels for 0%

commit v1 on v0

v1 whole, which is shorter than its diff:
```python
import jax
import jax.numpy as jnp
from jax import lax
from jax.sharding import Mesh, PartitionSpec as P

H = 16
KVH = 2
DH = 128
TOPK = 8

NEG = -1e30
EPSILON = 1e-06
F32 = jnp.float32
BF16 = jnp.bfloat16


def dot_f32(a, b, dims):
    return lax.dot_general(a, b, (dims, ((), ())), preferred_element_type=F32)


def flip_axis(value, name):
    return lax.ppermute(value, name, [(0, 1), (1, 0)])


def flip_xy(value):
    return lax.ppermute(value, ("x", "y"), [(i, 3 - i) for i in range(4)])


def ring_up(value):
    size = lax.axis_size("z")
    return lax.ppermute(value, "z", [(i, (i + 1) % size) for i in range(size)])


def to_chips(blocks):
    return [
        blocks[0],
        flip_axis(blocks[1], "y"),
        flip_axis(blocks[2], "x"),
        flip_xy(blocks[3]),
    ]


def three_parts(value):
    high = value.astype(BF16)
    rest = value - high.astype(F32)
    middle = rest.astype(BF16)
    low = (rest - middle.astype(F32)).astype(BF16)
    return high, middle, low


def per_device(
    residual,
    query_heads,
    key_heads,
    value_heads,
    norm_gain,
    chosen_experts,
    route_weights,
    gate_weight,
    up_weight,
    down_weight,
    cotangent,
):
    rows = residual.shape[1]
    width = residual.shape[2]
    kv_width = key_heads.shape[2]
    group = H // KVH
    planes = lax.axis_size("z")
    experts = planes * 8
    scale = DH ** (-0.5)
    capacity = (9 * rows * TOPK + 8 * experts - 1) // (8 * experts)
    capacity = (capacity + 3) // 4 * 4
    chip_rows = 2 * capacity
    z_index = lax.axis_index("z")
    x_index = lax.axis_index("x")
    y_index = lax.axis_index("y")
    core_index = lax.axis_index("core")

    chosen = chosen_experts[0]
    share_raw = route_weights[0]
    route_total = jnp.sum(share_raw, axis=-1, keepdims=True)
    route_share = share_raw / route_total
    hits = chosen[:, :, None] == jnp.arange(experts, dtype=jnp.int32)
    hit = jnp.any(hits, axis=1)
    share_table = jnp.sum(jnp.where(hits, route_share[:, :, None], 0.0), axis=1)
    below = (jnp.arange(rows)[:, None] > jnp.arange(rows)[None, :]).astype(BF16)
    earlier = dot_f32(below, hit.astype(BF16), ((1,), (0,)))
    slot_table = jnp.where(hit, earlier, -1.0)
    cot_own = cotangent[0]
    cot_float = cot_own.astype(F32)
    payload = jnp.concatenate(
        [cot_own, slot_table.astype(BF16)] + list(three_parts(share_table)), axis=1
    )

    kv_own = jnp.concatenate([key_heads[0], value_heads[0]], axis=1)
    ctx_count = planes * 2
    kv_blocks = [kv_own]
    for step in range(1, ctx_count):
        kv_blocks.append(
            lax.ppermute(
                kv_own, ("z", "x"), [(i, (i + step) % ctx_count) for i in range(ctx_count)]
            )
        )
    kv_all = jnp.concatenate(kv_blocks, axis=0)
    ctx_index = z_index * 2 + x_index
    key_all = kv_all[:, :kv_width].reshape(-1, KVH, DH)
    value_all = kv_all[:, kv_width:].reshape(-1, KVH, DH)
    key_block_place = jnp.mod(ctx_index - jnp.arange(ctx_count, dtype=jnp.int32), ctx_count)
    key_place = (key_block_place[:, None] * rows + jnp.arange(rows, dtype=jnp.int32)).reshape(-1)
    query_place = ctx_index * rows + jnp.arange(rows, dtype=jnp.int32)
    allowed = key_place[None, :] <= query_place[:, None]

    def own_columns(table):
        plane = lax.dynamic_slice_in_dim(table, z_index * 8, 8, axis=1)
        columns = []
        for chip in range(4):
            at = ((x_index ^ (chip >> 1)) * 2 + (y_index ^ (chip & 1))) * 2 + core_index
            columns.append(lax.dynamic_slice_in_dim(plane, at, 1, axis=1)[:, 0])
        return jnp.stack(columns)

    slot_ids = jnp.arange(capacity, dtype=F32)
    pick_steps = []
    share_steps = []
    cot_steps = []
    block = payload
    for step in range(planes):
        if step:
            block = ring_up(block)
        both = [block, flip_axis(block, "core")]
        picks = []
        shares = []
        for which, part in enumerate(both):
            slots = own_columns(part[:, width : width + experts].astype(F32))
            share = own_columns(
                part[:, width + experts : width + 2 * experts].astype(F32)
                + part[:, width + 2 * experts : width + 3 * experts].astype(F32)
                + part[:, width + 3 * experts :].astype(F32)
            )
            pick = slots[:, None, :] == slot_ids[None, :, None]
            empty = jnp.zeros_like(pick)
            picks.append(
                jnp.concatenate([pick, empty] if which == 0 else [empty, pick], axis=2)
            )
            shares.append(jnp.sum(jnp.where(pick, share[:, None, :], 0.0), axis=2))
        pick = jnp.stack(picks, axis=1).reshape(4 * chip_rows, 2 * rows).astype(BF16)
        share_rows = jnp.stack(shares, axis=1).reshape(4 * chip_rows, 1)
        pick_steps.append(pick)
        share_steps.append(share_rows)
        tokens = jnp.concatenate([part[:, :width] for part in both], axis=0)
        sent = (dot_f32(pick, tokens, ((1,), (0,))) * share_rows).astype(BF16)
        arrived = to_chips([sent[q * chip_rows : (q + 1) * chip_rows] for q in range(4)])
        cot_steps.append(jnp.concatenate(arrived, axis=0))

    query = query_heads[0].reshape(rows, KVH, group, DH)
    scores = (
        jnp.einsum("ikgd,jkd->kgij", query, key_all, preferred_element_type=F32) * scale
    )
    scores = jnp.where(allowed, scores, NEG)
    row_max = jnp.max(scores, axis=-1, keepdims=True)
    weights = jnp.exp(scores - row_max)
    row_sum = jnp.sum(weights, axis=-1, keepdims=True)
    attended = (
        jnp.einsum("kgij,jkd->kgid", weights.astype(BF16), value_all, preferred_element_type=F32)
        / row_sum
    )
    log_sum = row_max + jnp.log(row_sum)
    attended = jnp.transpose(attended, (2, 0, 1, 3)).reshape(rows, width).astype(BF16)
    hidden = (residual[0].astype(F32) + attended.astype(F32)).astype(BF16)
    hidden_float = hidden.astype(F32)
    inverse = lax.rsqrt(jnp.mean(hidden_float * hidden_float, axis=-1, keepdims=True) + EPSILON)
    normed = (hidden_float * inverse * norm_gain).astype(BF16)

    normed_steps = []
    block = normed
    for step in range(planes):
        if step:
            block = ring_up(block)
        tokens = jnp.concatenate([block, flip_axis(block, "core")], axis=0)
        sent = dot_f32(pick_steps[step], tokens, ((1,), (0,))).astype(BF16)
        arrived = to_chips([sent[q * chip_rows : (q + 1) * chip_rows] for q in range(4)])
        normed_steps.append(jnp.concatenate(arrived, axis=0))

    gate_mat = gate_weight[0]
    up_mat = up_weight[0]
    down_mat = down_weight[0]
    order = list(range(1, planes)) + [0]
    produced_steps = {}
    row_cot_steps = {}
    dot_steps = [None] * planes
    for step in order:
        incoming = normed_steps[step]
        cot_in = cot_steps[step]
        gate_act = dot_f32(incoming, gate_mat, ((1,), (0,)))
        up_act = dot_f32(incoming, up_mat, ((1,), (0,)))
        act_cot = dot_f32(cot_in, down_mat, ((1,), (1,)))
        sigma = jax.nn.sigmoid(gate_act)
        gate_cot = (act_cot * up_act * sigma * (1.0 + gate_act * (1.0 - sigma))).astype(BF16)
        up_cot = (act_cot * gate_act * sigma).astype(BF16)
        row_cot_steps[step] = (
            dot_f32(gate_cot, gate_mat, ((1,), (1,))) + dot_f32(up_cot, up_mat, ((1,), (1,)))
        ).astype(BF16)
        activation = (gate_act * sigma * up_act).astype(BF16)
        produced = dot_f32(activation, down_mat, ((1,), (0,))).astype(BF16)
        produced_steps[step] = produced
        dot_steps[step] = jnp.sum(produced.astype(F32) * cot_in.astype(F32), axis=1)

    def bring_back(result_steps, weighted):
        total = None
        for step in order:
            result = result_steps[step]
            arrived = to_chips([result[q * chip_rows : (q + 1) * chip_rows] for q in range(4)])
            back = jnp.concatenate(arrived, axis=0)
            pick = pick_steps[step]
            if weighted:
                exact = pick.astype(F32) * share_steps[step]
                high = exact.astype(BF16)
                low = (exact - high.astype(F32)).astype(BF16)
                both = dot_f32(high, back, ((0,), (0,))) + dot_f32(low, back, ((0,), (0,)))
            else:
                both = dot_f32(pick, back, ((0,), (0,)))
            part = both[:rows] + flip_axis(both[rows:].astype(BF16), "core").astype(F32)
            if total is None:
                total = part
            else:
                total = ring_up(total.astype(BF16)).astype(F32) + part
        return total

    normed_cot = bring_back(row_cot_steps, False)
    gained = norm_gain * normed_cot
    hidden_cot = inverse * gained - hidden_float * inverse**3 * jnp.mean(
        hidden_float * gained, axis=-1, keepdims=True
    )
    residual_gradient = (cot_float + hidden_cot).astype(BF16)

    grad = residual_gradient.reshape(rows, KVH, group, DH)
    row_dot = jnp.einsum(
        "ikgd,ikgd->kgi", grad, attended.reshape(rows, KVH, group, DH), preferred_element_type=F32
    )
    scores = (
        jnp.einsum("ikgd,jkd->kgij", query, key_all, preferred_element_type=F32) * scale
    )
    weights = jnp.where(allowed, jnp.exp(scores - log_sum), 0.0)
    value_part = jnp.einsum(
        "kgij,ikgd->jkd", weights.astype(BF16), grad, preferred_element_type=F32
    )
    grad_weights = jnp.einsum("ikgd,jkd->kgij", grad, value_all, preferred_element_type=F32)
    grad_scores = (weights * (grad_weights - row_dot[..., None])).astype(BF16)
    query_gradient = (
        jnp.einsum("kgij,jkd->ikgd", grad_scores, key_all, preferred_element_type=F32) * scale
    )
    query_gradient = query_gradient.reshape(rows, width).astype(BF16)
    key_part = (
        jnp.einsum("kgij,ikgd->jkd", grad_scores, query, preferred_element_type=F32) * scale
    )
    kv_part = jnp.concatenate(
        [key_part.reshape(-1, kv_width), value_part.reshape(-1, kv_width)], axis=1
    )
    kv_total = kv_part[:rows]
    kv_low = kv_part.astype(BF16)
    for step in range(1, ctx_count):
        kv_total = kv_total + lax.ppermute(
            kv_low[step * rows : (step + 1) * rows],
            ("z", "x"),
            [(i, (i - step) % ctx_count) for i in range(ctx_count)],
        ).astype(F32)
    kv_total = kv_total.astype(BF16)
    key_gradient = kv_total[:, :kv_width]
    value_gradient = kv_total[:, kv_width:]

    moe_sum = bring_back(produced_steps, True)
    layer_out = (hidden_float + moe_sum).astype(BF16)

    products = jnp.stack(dot_steps).reshape(planes, 2, 2, 2, capacity)
    products = products[jnp.mod(z_index - jnp.arange(planes, dtype=jnp.int32), planes)]
    for axis, index in ((1, x_index), (2, y_index), (3, core_index)):
        products = jnp.where(index == 1, jnp.flip(products, axis), products)
    products = lax.all_to_all(
        products.reshape(experts, capacity), ("z", "x", "y", "core"), 0, 0, tiled=True
    )
    weighted_dot = jnp.sum(
        jnp.where(
            slot_table[:, :, None] == slot_ids[None, None, :], products[None], 0.0
        ),
        axis=2,
    )
    route_dot = jnp.sum(jnp.where(hits, weighted_dot[:, None, :], 0.0), axis=2) / route_share
    route_gradient = (
        route_dot - jnp.sum(route_share * route_dot, axis=-1, keepdims=True)
    ) / route_total
    return (
        layer_out[None],
        residual_gradient[None],
        query_gradient[None],
        key_gradient[None],
        value_gradient[None],
        route_gradient[None],
    )


def solution(mesh):
    fine = Mesh(
        mesh.devices.reshape(mesh.shape["ctx"] // 2, 2, mesh.shape["exp"] // 2, 2),
        ("z", "x", "y", "core"),
    )
    tokens = P(("y", "core"), ("z", "x"), None)
    expert = P(("z", "x", "y", "core"), None, None)
    return jax.shard_map(
        per_device,
        mesh=fine,
        in_specs=(tokens,) * 4 + (P(),) + (tokens,) * 2 + (expert,) * 3 + (tokens,),
        out_specs=(tokens,) * 6,
        check_vma=False,
    )
```

time: 791 us -> 469 us (0.59)
  waiting for transfers between devices: 416 us -> 136 us
  starting transfers between devices: 19.4 us -> 94.4 us
  blocking collectives: 59.3 us -> 0 us
  local copies, waits for them, and re-layouts: 130 us -> 86.9 us
  other arithmetic: 73.6 us -> 50.4 us
  matrix products: 66.5 us -> 89.3 us
  between operations: 16.2 us -> 3.13 us
    all_to_all x4 -> x1, waiting for transfers between devices: 362 us -> 0.01 us  [per_device(): lax.all_to_all(products.reshape(experts, capacity), ('z', 'x', 'y', 'core...]
    ppermute x0 -> x90, waiting for transfers between devices: none -> 136 us  [the longest x16 52.7 us: flip_xy(): return lax.ppermute(value, ('x', 'y'), [(i, 3 - i) for i in range(4)])]
    ppermute x0 -> x90, starting transfers between devices: none -> 89.8 us  [the longest x48 40.1 us: flip_axis(): return lax.ppermute(value, name, [(0, 1), (1, 0)])]
    reshape x8 -> x6, local copies, waits for them, and re-layouts: 68.1 us -> 5.29 us  [the longest x1 2.61 us: per_device(): value_part.reshape(-1, kv_width)]
    all_gather x2 -> x0, blocking collectives: 59.3 us -> none  [the longest x1 30.7 us: over_keys(): lax.all_gather(key_local, 'ctx', axis=0, tiled=True)]
    reduce_scatter x2 -> x0, waiting for transfers between devices: 53.9 us -> none  [the longest x1 53.9 us: per_device(): lax.psum_scatter(key_total.astype(jnp.bfloat16), 'ctx', scatter_dimension...]
    slice x3 -> x33, local copies, waits for them, and re-layouts: 3.14 us -> 33.3 us  [the longest x8 13.9 us: bring_back(): result[q * chip_rows:(q + 1) * chip_rows]]
    gather x2 -> x1, local copies, waits for them, and re-layouts: 23.6 us -> 0.7 us  [per_device(): products[jnp.mod(z_index - jnp.arange(planes, dtype=jnp.int32), planes)]]
  transfers between devices with their start and end apart: 6 -> 91, of which waited for: 5 -> 36; matrix products, arithmetic and copies ran while one was open for 19% -> 40% of each run, Pallas kernels for 0% -> 0%
where the time goes in v1:
time: 469 us; the launch traced here: 460 us
  waiting for transfers between devices  136 us (29%)
  starting transfers between devices  94.4 us (20%)
  matrix products  89.3 us (19%)
  local copies, waits for them, and re-layouts  86.9 us (19%)
  other arithmetic  50.4 us (11%)
    dot_general x45, matrix products, dot_f32(): return lax.dot_general(a, b, (dims, ((), ())), preferred_element_type=F32)  73.5 us
    ppermute x16, waiting for transfers between devices, flip_xy(): return lax.ppermute(value, ('x', 'y'), [(i, 3 - i) for i in range(4)])  52.7 us
    ppermute x12, waiting for transfers between devices, ring_up(): return lax.ppermute(value, 'z', [(i, (i + 1) % size) for i in range(size)])  51.8 us
    ppermute x48, starting transfers between devices, flip_axis(): return lax.ppermute(value, name, [(0, 1), (1, 0)])  40.1 us
    unnamed x227, local copies, waits for them, and re-layouts  25.6 us
    ppermute x48, waiting for transfers between devices, flip_axis(): return lax.ppermute(value, name, [(0, 1), (1, 0)])  19.3 us
    ppermute x16, starting transfers between devices, flip_xy(): return lax.ppermute(value, ('x', 'y'), [(i, 3 - i) for i in range(4)])  17.9 us
    slice x8, local copies, waits for them, and re-layouts, bring_back(): result[q * chip_rows:(q + 1) * chip_rows]  13.9 us
  transfers between devices with their start and end apart: 91, of which 36 were waited for; matrix products, arithmetic and copies ran while one was open for 40% of the time, Pallas kernels for 0%

profile of v1, /device:TPU:0, one launch (start us, length us, event | category | flops | bytes accessed | tf_op | source)
XLA Modules:
  0.0 460.1 jit_solution(18002329725907931675)
XLA Ops:
  3.4 2.9 collective-permute-start
  7.9 2.6 collective-permute-start.2
  11.7 2.6 collective-permute-start.4
  47.5 2.5 copy.111
  54.2 7.1 %fusion.7 = bf16[2,8,128,1024]{2,3,1,0:T(8,128)(2,1)} fusion(f32[2,1024,128,8]{2,1,3,0:T(8,128)} %copy-done.1, f32[2,8,128]{2,1,0:T(8,128)S(1)} %log_add_fusion, pred[128,1024]{0,1:T(8,128)(4,1)S(1)} %broadcast_compare_fusion), kind=kLoop, calls=%fused_computation.12 | loop fusion | flops 8388608 | bytes 12722176 | tf_op jit(solution)/shard_map/convert_element_type | solution.py:244
  61.3 6.8 %copy.125 = bf16[2,8,128,1024]{3,1,0,2:T(8,128)(2,1)} copy(bf16[2,8,128,1024]{2,3,1,0:T(8,128)(2,1)} %fusion.7) | data formatting | bytes 8388608 | tf_op jit(solution)/shard_map/convert_element_type | solution.py:244
  85.4 5.7 %collective-permute-done.78 = bf16[72,2048]{1,0:T(8,128)(2,1)S(1)} collective-permute-done((bf16[72,2048]{1,0:T(8,128)(2,1)S(1)}, bf16[72,2048]{1,0:T(8,128)(2,1)S(1)}, u32[]{:S(2)}, u32[]{:S(2)}) %collective-permute-start.78) | collective-permute-done | bytes 294944 | tf_op jit(solution)/shard_map/ppermute | solution.py:26
  97.5 5.0 %collective-permute-done.47 = bf16[72,2048]{1,0:T(8,128)(2,1)S(1)} collective-permute-done((bf16[72,2048]{1,0:T(8,128)(2,1)S(1)}, bf16[72,2048]{1,0:T(8,128)(2,1)S(1)}, u32[]{:S(2)}, u32[]{:S(2)}) %collective-permute-start.47) | collective-permute-done | bytes 294944 | tf_op jit(solution)/shard_map/ppermute | solution.py:26
  105.6 2.3 multiply_reduce_fusion.3
  107.9 2.4 fusion.316
  112.6 3.3 fusion.27
  145.2 3.0 collective-permute-done.81
  152.2 2.6 collective-permute-done.53
  155.6 5.3 %collective-permute-done.54 = bf16[72,2048]{1,0:T(8,128)(2,1)S(1)} collective-permute-done((bf16[72,2048]{1,0:T(8,128)(2,1)S(1)}, bf16[72,2048]{1,0:T(8,128)(2,1)S(1)}, u32[]{:S(2)}, u32[]{:S(2)}) %collective-permute-start.54) | collective-permute-done | bytes 294944 | tf_op jit(solution)/shard_map/ppermute | solution.py:26
  167.4 3.2 collective-permute-done.13
  173.6 2.2 multiply_reduce_fusion.2
  175.9 2.4 fusion.310
  180.7 3.3 fusion.33
  214.6 2.4 collective-permute-done.57
  223.8 5.2 %collective-permute-done.62 = bf16[72,2048]{1,0:T(8,128)(2,1)S(1)} collective-permute-done((bf16[72,2048]{1,0:T(8,128)(2,1)S(1)}, bf16[72,2048]{1,0:T(8,128)(2,1)S(1)}, u32[]{:S(2)}, u32[]{:S(2)}) %collective-permute-start.62) | collective-permute-done | bytes 294944 | tf_op jit(solution)/shard_map/ppermute | solution.py:26
  231.2 3.3 collective-permute-done.23
  235.6 3.4 collective-permute-done.25
  244.9 2.4 fusion.312
  248.9 3.0 fusion.31
  267.3 2.4 collective-permute-done.28
  272.8 2.3 convolution_add_fusion.2
  275.1 2.9 collective-permute-done.63
  279.4 3.6 collective-permute-done.65
  302.1 3.5 collective-permute-done.70
  305.5 2.2 multiply_reduce_fusion
  309.3 4.6 %all-to-all-start = ((f32[32,1,36]{2,1,0:T(1,128)}), f32[32,1,36]{2,1,0:T(1,128)S(1)}, u32[]{:S(2)}, u32[]{:S(2)}) async-start(f32[32,1,36]{2,1,0:T(1,128)} %bitcast.64), calls=%async_computation | async-start | bytes 32768 | tf_op jit(solution)/shard_map/all_to_all | solution.py:277
  313.9 2.4 fusion.314
  329.7 4.6 collective-permute-done.40
  334.3 2.7 collective-permute-start.73
  341.8 4.0 collective-permute-done.73
  352.1 10.5 %collective-permute-done.18 = bf16[128,2048]{1,0:T(8,128)(2,1)S(1)} collective-permute-done((bf16[128,2048]{1,0:T(8,128)(2,1)S(1)}, bf16[128,2048]{1,0:T(8,128)(2,1)S(1)}, u32[]{:S(2)}, u32[]{:S(2)}) %collective-permute-start.18) | collective-permute-done | bytes 524320 | tf_op jit(solution)/shard_map/ppermute | solution.py:31
  362.9 10.9 %collective-permute-done.67 = bf16[128,2048]{1,0:T(8,128)(2,1)S(1)} collective-permute-done((bf16[128,2048]{1,0:T(8,128)(2,1)S(1)}, bf16[128,2048]{1,0:T(8,128)(2,1)S(1)}, u32[]{:S(2)}, u32[]{:S(2)}) %collective-permute-start.67) | collective-permute-done | bytes 524320 | tf_op jit(solution)/shard_map/ppermute | solution.py:31
  374.4 10.6 %collective-permute-done.30 = bf16[128,2048]{1,0:T(8,128)(2,1)S(1)} collective-permute-done((bf16[128,2048]{1,0:T(8,128)(2,1)S(1)}, bf16[128,2048]{1,0:T(8,128)(2,1)S(1)}, u32[]{:S(2)}, u32[]{:S(2)}) %collective-permute-start.30) | collective-permute-done | bytes 524320 | tf_op jit(solution)/shard_map/ppermute | solution.py:31
  385.3 10.9 %collective-permute-done.75 = bf16[128,2048]{1,0:T(8,128)(2,1)S(1)} collective-permute-done((bf16[128,2048]{1,0:T(8,128)(2,1)S(1)}, bf16[128,2048]{1,0:T(8,128)(2,1)S(1)}, u32[]{:S(2)}, u32[]{:S(2)}) %collective-permute-start.75) | collective-permute-done | bytes 524320 | tf_op jit(solution)/shard_map/ppermute | solution.py:31
  396.7 8.9 %collective-permute-done.42 = bf16[128,2048]{1,0:T(8,128)(2,1)S(1)} collective-permute-done((bf16[128,2048]{1,0:T(8,128)(2,1)S(1)}, bf16[128,2048]{1,0:T(8,128)(2,1)S(1)}, u32[]{:S(2)}, u32[]{:S(2)}) %collective-permute-start.42) | collective-permute-done | bytes 524320 | tf_op jit(solution)/shard_map/ppermute | solution.py:31
  411.1 2.6 copy.127
  413.8 2.5 copy.139
  417.8 6.5 %fusion.1 = bf16[2,8,128,1024]{2,3,1,0:T(8,128)(2,1)S(1)} fusion(f32[2,1024,128,8]{2,1,3,0:T(8,128)} %copy-done.1, f32[2,8,128]{2,1,0:T(8,128)S(1)} %multiply_reduce_fusion.4, f32[2,8,128]{2,1,0:T(8,128)S(1)} %log_add_fusion, pred[128,1024]{0,1:T(8,128)(4,1)S(1)} %broadcast_compare_fusion, bf16[1024,2,128,1]{0,2,3,1:T(8,128)(2,1)} %bitcast.336, ...), kind=kOutput, calls=%fused_computation.3 | convolution fusion | flops 549453824 | bytes 13778944 | tf_op jit(solution)/shard_map/ikgd,jkd->kgij/dot_general | solution.py:246
  424.4 2.5 fusion.103
  426.8 2.5 copy.126
  432.0 2.5 collective-permute-start.83
  435.6 3.0 collective-permute-start.86
  446.2 9.8 %collective-permute-done.86 = bf16[128,512]{1,0:T(8,128)(2,1)} collective-permute-done((bf16[128,512]{1,0:T(8,128)(2,1)}, bf16[128,512]{1,0:T(8,128)(2,1)}, u32[]{:S(2)}, u32[]{:S(2)}) %collective-permute-start.86) | collective-permute-done | bytes 131104 | tf_op jit(solution)/shard_map/ppermute | solution.py:261
  (585 shorter events, 252.9 us)
Async XLA Ops:
  3.4 21.3 %collective-permute-start = (bf16[128,512]{0,1:T(8,128)(2,1)S(1)}, bf16[128,512]{0,1:T(8,128)(2,1)}, u32[]{:S(2)}, u32[]{:S(2)}) collective-permute-start(bf16[128,512]{0,1:T(8,128)(2,1)S(1)} %get-tuple-element.173), channel_id=1, source_target_pairs={{0,4},{4,8},{8,12},{12,16},{16,20},{20,24},{24,28},{28,0},{1,5},{5... | collective-permute-start | bytes 393224 | tf_op jit(solution)/shard_map/ppermute | solution.py:100
  6.3 21.3 %collective-permute-start.1 = (bf16[128,512]{0,1:T(8,128)(2,1)S(1)}, bf16[128,512]{0,1:T(8,128)(2,1)}, u32[]{:S(2)}, u32[]{:S(2)}) collective-permute-start(bf16[128,512]{0,1:T(8,128)(2,1)S(1)} %get-tuple-element.173), channel_id=1, source_target_pairs={{0,8},{4,12},{8,16},{12,20},{16,24},{20,28},{24,0},{28,4},{1,9},{5... | collective-permute-start | bytes 393224 | tf_op jit(solution)/shard_map/ppermute | solution.py:100
  7.9 22.8 %collective-permute-start.2 = (bf16[128,512]{0,1:T(8,128)(2,1)S(1)}, bf16[128,512]{0,1:T(8,128)(2,1)}, u32[]{:S(2)}, u32[]{:S(2)}) collective-permute-start(bf16[128,512]{0,1:T(8,128)(2,1)S(1)} %get-tuple-element.173), channel_id=1, source_target_pairs={{0,12},{4,16},{8,20},{12,24},{16,28},{20,0},{24,4},{28,8},{1,13},{... | collective-permute-start | bytes 393224 | tf_op jit(solution)/shard_map/ppermute | solution.py:100
  10.5 22.5 %collective-permute-start.3 = (bf16[128,512]{0,1:T(8,128)(2,1)S(1)}, bf16[128,512]{0,1:T(8,128)(2,1)}, u32[]{:S(2)}, u32[]{:S(2)}) collective-permute-start(bf16[128,512]{0,1:T(8,128)(2,1)S(1)} %get-tuple-element.173), channel_id=1, source_target_pairs={{0,16},{4,20},{8,24},{12,28},{16,0},{20,4},{24,8},{28,12},{1,17},{... | collective-permute-start | bytes 393224 | tf_op jit(solution)/shard_map/ppermute | solution.py:100
  11.7 22.8 %collective-permute-start.4 = (bf16[128,512]{0,1:T(8,128)(2,1)S(1)}, bf16[128,512]{0,1:T(8,128)(2,1)}, u32[]{:S(2)}, u32[]{:S(2)}) collective-permute-start(bf16[128,512]{0,1:T(8,128)(2,1)S(1)} %get-tuple-element.173), channel_id=1, source_target_pairs={{0,20},{4,24},{8,28},{12,0},{16,4},{20,8},{24,12},{28,16},{1,21},{... | collective-permute-start | bytes 393224 | tf_op jit(solution)/shard_map/ppermute | solution.py:100
  30.7 44.8 %collective-permute-start.7 = (bf16[128,2176]{1,0:T(8,128)(2,1)}, bf16[128,2176]{1,0:T(8,128)(2,1)}, u32[]{:S(2)}, u32[]{:S(2)}) collective-permute-start(bf16[128,2176]{1,0:T(8,128)(2,1)} %concatenate.111), channel_id=1, source_target_pairs={{0,8},{8,16},{16,24},{24,0},{1,9},{9,17},{17,25},{25,1},{2,10},{10... | collective-permute-start | bytes 1671176 | tf_op jit(solution)/shard_map/ppermute | solution.py:31
  32.9 35.2 %collective-permute-start.43 = (bf16[128,2176]{1,0:T(8,128)(2,1)}, bf16[128,2176]{1,0:T(8,128)(2,1)}, u32[]{:S(2)}, u32[]{:S(2)}) collective-permute-start(bf16[128,2176]{1,0:T(8,128)(2,1)} %concatenate.111), channel_id=1, source_target_pairs={{0,1},{1,0},{2,3},{3,2},{4,5},{5,4},{6,7},{7,6},{8,9},{9,8},{10,11... | collective-permute-start | bytes 1671176 | tf_op jit(solution)/shard_map/ppermute | solution.py:22
  53.4 41.4 %collective-permute-start.9 = (bf16[128,2048]{1,0:T(8,128)(2,1)}, bf16[128,2048]{1,0:T(8,128)(2,1)}, u32[]{:S(2)}, u32[]{:S(2)}) collective-permute-start(bf16[128,2048]{1,0:T(8,128)(2,1)} %fusion.139), channel_id=1, source_target_pairs={{0,8},{8,16},{16,24},{24,0},{1,9},{9,17},{17,25},{25,1},{2,10},{10... | collective-permute-start | bytes 1572872 | tf_op jit(solution)/shard_map/ppermute | solution.py:31
  53.7 27.4 %collective-permute-start.44 = (bf16[128,2048]{1,0:T(8,128)(2,1)}, bf16[128,2048]{1,0:T(8,128)(2,1)}, u32[]{:S(2)}, u32[]{:S(2)}) collective-permute-start(bf16[128,2048]{1,0:T(8,128)(2,1)} %fusion.139), channel_id=1, source_target_pairs={{0,1},{1,0},{2,3},{3,2},{4,5},{5,4},{6,7},{7,6},{8,9},{9,8},{10,11... | collective-permute-start | bytes 1572872 | tf_op jit(solution)/shard_map/ppermute | solution.py:22
  81.1 37.1 %collective-permute-start.8 = (bf16[128,2176]{1,0:T(8,128)(2,1)}, bf16[128,2176]{1,0:T(8,128)(2,1)}, u32[]{:S(2)}, u32[]{:S(2)}) collective-permute-start(bf16[128,2176]{1,0:T(8,128)(2,1)} %collective-permute-done.7), channel_id=1, source_target_pairs={{0,1},{1,0},{2,3},{3,2},{4,5},{5,4},{6,7},{7,6},{8,9},{9,8},{10,11... | collective-permute-start | bytes 1671176 | tf_op jit(solution)/shard_map/ppermute | solution.py:22
  94.8 28.0 %collective-permute-start.19 = (bf16[128,2176]{1,0:T(8,128)(2,1)}, bf16[128,2176]{1,0:T(8,128)(2,1)}, u32[]{:S(2)}, u32[]{:S(2)}) collective-permute-start(bf16[128,2176]{1,0:T(8,128)(2,1)} %collective-permute-done.7), channel_id=1, source_target_pairs={{0,8},{8,16},{16,24},{24,0},{1,9},{9,17},{17,25},{25,1},{2,10},{10... | collective-permute-start | bytes 1671176 | tf_op jit(solution)/shard_map/ppermute | solution.py:31
  97.4 34.7 %collective-permute-start.10 = (bf16[128,2048]{1,0:T(8,128)(2,1)}, bf16[128,2048]{1,0:T(8,128)(2,1)}, u32[]{:S(2)}, u32[]{:S(2)}) collective-permute-start(bf16[128,2048]{1,0:T(8,128)(2,1)} %collective-permute-done.9), channel_id=1, source_target_pairs={{0,1},{1,0},{2,3},{3,2},{4,5},{5,4},{6,7},{7,6},{8,9},{9,8},{10,11... | collective-permute-start | bytes 1572872 | tf_op jit(solution)/shard_map/ppermute | solution.py:22
  110.4 24.5 %collective-permute-start.48 = (bf16[72,2048]{1,0:T(8,128)(2,1)}, bf16[72,2048]{1,0:T(8,128)(2,1)}, u32[]{:S(2)}, u32[]{:S(2)}) collective-permute-start(bf16[72,2048]{1,0:T(8,128)(2,1)} %get-tuple-element.155), channel_id=1, source_target_pairs={{0,2},{2,0},{1,3},{3,1},{4,6},{6,4},{5,7},{7,5},{8,10},{10,8},{9,1... | collective-permute-start | bytes 884744 | tf_op jit(solution)/shard_map/ppermute | solution.py:22
  112.0 23.9 %collective-permute-start.49 = (bf16[72,2048]{1,0:T(8,128)(2,1)}, bf16[72,2048]{1,0:T(8,128)(2,1)}, u32[]{:S(2)}, u32[]{:S(2)}) collective-permute-start(bf16[72,2048]{1,0:T(8,128)(2,1)} %get-tuple-element.154), channel_id=1, source_target_pairs={{0,4},{4,0},{1,5},{5,1},{2,6},{6,2},{3,7},{7,3},{8,12},{12,8},{9,1... | collective-permute-start | bytes 884744 | tf_op jit(solution)/shard_map/ppermute | solution.py:22
  118.2 19.3 %collective-permute-start.50 = (bf16[72,2048]{1,0:T(8,128)(2,1)}, bf16[72,2048]{1,0:T(8,128)(2,1)}, u32[]{:S(2)}, u32[]{:S(2)}) collective-permute-start(bf16[72,2048]{1,0:T(8,128)(2,1)} %get-tuple-element.153), channel_id=1, source_target_pairs={{0,6},{2,4},{4,2},{6,0},{1,7},{3,5},{5,3},{7,1},{8,14},{10,12},{12... | collective-permute-start | bytes 884744 | tf_op jit(solution)/shard_map/ppermute | solution.py:26
  122.8 17.6 %collective-permute-start.79 = (bf16[72,2048]{1,0:T(8,128)(2,1)}, bf16[72,2048]{1,0:T(8,128)(2,1)S(1)}, u32[]{:S(2)}, u32[]{:S(2)}) collective-permute-start(bf16[72,2048]{1,0:T(8,128)(2,1)} %get-tuple-element.123), channel_id=1, source_target_pairs={{0,2},{2,0},{1,3},{3,1},{4,6},{6,4},{5,7},{7,5},{8,10},{10,8},{9,1... | collective-permute-start | bytes 884744 | tf_op jit(solution)/shard_map/ppermute | solution.py:22
  137.5 17.2 %collective-permute-start.53 = (bf16[72,2048]{1,0:T(8,128)(2,1)S(1)}, bf16[72,2048]{1,0:T(8,128)(2,1)S(1)}, u32[]{:S(2)}, u32[]{:S(2)}) collective-permute-start(bf16[72,2048]{1,0:T(8,128)(2,1)S(1)} %get-tuple-element.102), channel_id=1, source_target_pairs={{0,4},{4,0},{1,5},{5,1},{2,6},{6,2},{3,7},{7,3},{8,12},{12,8},{9,1... | collective-permute-start | bytes 884744 | tf_op jit(solution)/shard_map/ppermute | solution.py:22
  140.5 20.5 %collective-permute-start.54 = (bf16[72,2048]{1,0:T(8,128)(2,1)S(1)}, bf16[72,2048]{1,0:T(8,128)(2,1)S(1)}, u32[]{:S(2)}, u32[]{:S(2)}) collective-permute-start(bf16[72,2048]{1,0:T(8,128)(2,1)S(1)} %get-tuple-element.101), channel_id=1, source_target_pairs={{0,6},{2,4},{4,2},{6,0},{1,7},{3,5},{5,3},{7,1},{8,14},{10,12},{12... | collective-permute-start | bytes 884744 | tf_op jit(solution)/shard_map/ppermute | solution.py:26
  144.4 20.3 %collective-permute-start.21 = (bf16[128,2048]{1,0:T(8,128)(2,1)}, bf16[128,2048]{1,0:T(8,128)(2,1)}, u32[]{:S(2)}, u32[]{:S(2)}) collective-permute-start(bf16[128,2048]{1,0:T(8,128)(2,1)} %collective-permute-done.9), channel_id=1, source_target_pairs={{0,8},{8,16},{16,24},{24,0},{1,9},{9,17},{17,25},{25,1},{2,10},{10... | collective-permute-start | bytes 1572872 | tf_op jit(solution)/shard_map/ppermute | solution.py:31
  148.3 38.0 %collective-permute-start.20 = (bf16[128,2176]{1,0:T(8,128)(2,1)}, bf16[128,2176]{1,0:T(8,128)(2,1)}, u32[]{:S(2)}, u32[]{:S(2)}) collective-permute-start(bf16[128,2176]{1,0:T(8,128)(2,1)} %collective-permute-done.19), channel_id=1, source_target_pairs={{0,1},{1,0},{2,3},{3,2},{4,5},{5,4},{6,7},{7,6},{8,9},{9,8},{10,11... | collective-permute-start | bytes 1671176 | tf_op jit(solution)/shard_map/ppermute | solution.py:22
  150.6 15.7 %collective-permute-start.11 = (bf16[72,2048]{1,0:T(8,128)(2,1)S(1)}, bf16[72,2048]{1,0:T(8,128)(2,1)S(1)}, u32[]{:S(2)}, u32[]{:S(2)}) collective-permute-start(bf16[72,2048]{1,0:T(8,128)(2,1)S(1)} %get-tuple-element.135), channel_id=1, source_target_pairs={{0,2},{2,0},{1,3},{3,1},{4,6},{6,4},{5,7},{7,5},{8,10},{10,8},{9,1... | collective-permute-start | bytes 884744 | tf_op jit(solution)/shard_map/ppermute | solution.py:22
  164.7 26.9 %collective-permute-start.31 = (bf16[128,2176]{1,0:T(8,128)(2,1)}, bf16[128,2176]{1,0:T(8,128)(2,1)}, u32[]{:S(2)}, u32[]{:S(2)}) collective-permute-start(bf16[128,2176]{1,0:T(8,128)(2,1)} %collective-permute-done.19), channel_id=1, source_target_pairs={{0,8},{8,16},{16,24},{24,0},{1,9},{9,17},{17,25},{25,1},{2,10},{10... | collective-permute-start | bytes 1671176 | tf_op jit(solution)/shard_map/ppermute | solution.py:31
  166.3 34.5 %collective-permute-start.22 = (bf16[128,2048]{1,0:T(8,128)(2,1)}, bf16[128,2048]{1,0:T(8,128)(2,1)}, u32[]{:S(2)}, u32[]{:S(2)}) collective-permute-start(bf16[128,2048]{1,0:T(8,128)(2,1)} %collective-permute-done.21), channel_id=1, source_target_pairs={{0,1},{1,0},{2,3},{3,2},{4,5},{5,4},{6,7},{7,6},{8,9},{9,8},{10,11... | collective-permute-start | bytes 1572872 | tf_op jit(solution)/shard_map/ppermute | solution.py:22
  178.3 25.3 %collective-permute-start.14 = (bf16[72,2048]{1,0:T(8,128)(2,1)}, bf16[72,2048]{1,0:T(8,128)(2,1)}, u32[]{:S(2)}, u32[]{:S(2)}) collective-permute-start(bf16[72,2048]{1,0:T(8,128)(2,1)} %get-tuple-element.131), channel_id=1, source_target_pairs={{0,2},{2,0},{1,3},{3,1},{4,6},{6,4},{5,7},{7,5},{8,10},{10,8},{9,1... | collective-permute-start | bytes 884744 | tf_op jit(solution)/shard_map/ppermute | solution.py:22
  180.0 24.6 %collective-permute-start.15 = (bf16[72,2048]{1,0:T(8,128)(2,1)}, bf16[72,2048]{1,0:T(8,128)(2,1)}, u32[]{:S(2)}, u32[]{:S(2)}) collective-permute-start(bf16[72,2048]{1,0:T(8,128)(2,1)} %get-tuple-element.130), channel_id=1, source_target_pairs={{0,4},{4,0},{1,5},{5,1},{2,6},{6,2},{3,7},{7,3},{8,12},{12,8},{9,1... | collective-permute-start | bytes 884744 | tf_op jit(solution)/shard_map/ppermute | solution.py:22
  186.3 19.2 %collective-permute-start.16 = (bf16[72,2048]{1,0:T(8,128)(2,1)}, bf16[72,2048]{1,0:T(8,128)(2,1)}, u32[]{:S(2)}, u32[]{:S(2)}) collective-permute-start(bf16[72,2048]{1,0:T(8,128)(2,1)} %get-tuple-element.129), channel_id=1, source_target_pairs={{0,6},{2,4},{4,2},{6,0},{1,7},{3,5},{5,3},{7,1},{8,14},{10,12},{12... | collective-permute-start | bytes 884744 | tf_op jit(solution)/shard_map/ppermute | solution.py:26
  191.6 17.5 %collective-permute-start.55 = (bf16[72,2048]{1,0:T(8,128)(2,1)}, bf16[72,2048]{1,0:T(8,128)(2,1)S(1)}, u32[]{:S(2)}, u32[]{:S(2)}) collective-permute-start(bf16[72,2048]{1,0:T(8,128)(2,1)} %get-tuple-element.99), channel_id=1, source_target_pairs={{0,2},{2,0},{1,3},{3,1},{4,6},{6,4},{5,7},{7,5},{8,10},{10,8},{9,1... | collective-permute-start | bytes 884744 | tf_op jit(solution)/shard_map/ppermute | solution.py:22
  210.7 18.3 %collective-permute-start.62 = (bf16[72,2048]{1,0:T(8,128)(2,1)S(1)}, bf16[72,2048]{1,0:T(8,128)(2,1)S(1)}, u32[]{:S(2)}, u32[]{:S(2)}) collective-permute-start(bf16[72,2048]{1,0:T(8,128)(2,1)S(1)} %get-tuple-element.109), channel_id=1, source_target_pairs={{0,6},{2,4},{4,2},{6,0},{1,7},{3,5},{5,3},{7,1},{8,14},{10,12},{12... | collective-permute-start | bytes 884744 | tf_op jit(solution)/shard_map/ppermute | solution.py:26
  217.0 37.2 %collective-permute-start.32 = (bf16[128,2176]{1,0:T(8,128)(2,1)}, bf16[128,2176]{1,0:T(8,128)(2,1)}, u32[]{:S(2)}, u32[]{:S(2)}) collective-permute-start(bf16[128,2176]{1,0:T(8,128)(2,1)} %collective-permute-done.31), channel_id=1, source_target_pairs={{0,1},{1,0},{2,3},{3,2},{4,5},{5,4},{6,7},{7,6},{8,9},{9,8},{10,11... | collective-permute-start | bytes 1671176 | tf_op jit(solution)/shard_map/ppermute | solution.py:22
  229.0 28.7 %collective-permute-start.34 = (bf16[128,2048]{1,0:T(8,128)(2,1)}, bf16[128,2048]{1,0:T(8,128)(2,1)}, u32[]{:S(2)}, u32[]{:S(2)}) collective-permute-start(bf16[128,2048]{1,0:T(8,128)(2,1)} %collective-permute-done.33), channel_id=1, source_target_pairs={{0,1},{1,0},{2,3},{3,2},{4,5},{5,4},{6,7},{7,6},{8,9},{9,8},{10,11... | collective-permute-start | bytes 1572872 | tf_op jit(solution)/shard_map/ppermute | solution.py:22
  234.5 52.4 %collective-permute-start.17 = (bf16[128,2048]{1,0:T(8,128)(2,1)}, bf16[128,2048]{1,0:T(8,128)(2,1)}, u32[]{:S(2)}, u32[]{:S(2)}) collective-permute-start(bf16[128,2048]{1,0:T(8,128)(2,1)} %slice.757), channel_id=1, source_target_pairs={{0,1},{1,0},{2,3},{3,2},{4,5},{5,4},{6,7},{7,6},{8,9},{9,8},{10,11... | collective-permute-start | bytes 1572872 | tf_op jit(solution)/shard_map/ppermute | solution.py:22
  235.5 53.9 %collective-permute-start.58 = (bf16[128,2048]{1,0:T(8,128)(2,1)}, bf16[128,2048]{1,0:T(8,128)(2,1)}, u32[]{:S(2)}, u32[]{:S(2)}) collective-permute-start(bf16[128,2048]{1,0:T(8,128)(2,1)} %slice.753), channel_id=1, source_target_pairs={{0,1},{1,0},{2,3},{3,2},{4,5},{5,4},{6,7},{7,6},{8,9},{9,8},{10,11... | collective-permute-start | bytes 1572872 | tf_op jit(solution)/shard_map/ppermute | solution.py:22
  247.3 17.8 %collective-permute-start.26 = (bf16[72,2048]{1,0:T(8,128)(2,1)}, bf16[72,2048]{1,0:T(8,128)(2,1)}, u32[]{:S(2)}, u32[]{:S(2)}) collective-permute-start(bf16[72,2048]{1,0:T(8,128)(2,1)} %get-tuple-element.139), channel_id=1, source_target_pairs={{0,2},{2,0},{1,3},{3,1},{4,6},{6,4},{5,7},{7,5},{8,10},{10,8},{9,1... | collective-permute-start | bytes 884744 | tf_op jit(solution)/shard_map/ppermute | solution.py:22
  278.0 16.2 %collective-permute-start.35 = (bf16[72,2048]{1,0:T(8,128)(2,1)S(1)}, bf16[72,2048]{1,0:T(8,128)(2,1)S(1)}, u32[]{:S(2)}, u32[]{:S(2)}) collective-permute-start(bf16[72,2048]{1,0:T(8,128)(2,1)S(1)} %copy-done.51), channel_id=1, source_target_pairs={{0,2},{2,0},{1,3},{3,1},{4,6},{6,4},{5,7},{7,5},{8,10},{10,8},{9,1... | collective-permute-start | bytes 884744 | tf_op jit(solution)/shard_map/ppermute | solution.py:22
  294.5 54.0 %collective-permute-start.66 = (bf16[128,2048]{1,0:T(8,128)(2,1)}, bf16[128,2048]{1,0:T(8,128)(2,1)}, u32[]{:S(2)}, u32[]{:S(2)}) collective-permute-start(bf16[128,2048]{1,0:T(8,128)(2,1)} %slice.752), channel_id=1, source_target_pairs={{0,1},{1,0},{2,3},{3,2},{4,5},{5,4},{6,7},{7,6},{8,9},{9,8},{10,11... | collective-permute-start | bytes 1572872 | tf_op jit(solution)/shard_map/ppermute | solution.py:22
  295.7 52.8 %collective-permute-start.59 = (bf16[128,2048]{1,0:T(8,128)(2,1)}, bf16[128,2048]{1,0:T(8,128)(2,1)}, u32[]{:S(2)}, u32[]{:S(2)}) collective-permute-start(bf16[128,2048]{1,0:T(8,128)(2,1)} %fusion.152), channel_id=1, source_target_pairs={{0,8},{8,16},{16,24},{24,0},{1,9},{9,17},{17,25},{25,1},{2,10},{10... | collective-permute-start | bytes 1572872 | tf_op jit(solution)/shard_map/ppermute | solution.py:31
  309.3 16.8 %all-to-all-start = ((f32[32,1,36]{2,1,0:T(1,128)}), f32[32,1,36]{2,1,0:T(1,128)S(1)}, u32[]{:S(2)}, u32[]{:S(2)}) async-start(f32[32,1,36]{2,1,0:T(1,128)} %bitcast.64), calls=%async_computation | async-start | bytes 32768 | tf_op jit(solution)/shard_map/all_to_all | solution.py:277
  341.3 55.4 %collective-permute-start.51 = (bf16[128,2048]{1,0:T(8,128)(2,1)S(1)}, bf16[128,2048]{1,0:T(8,128)(2,1)S(1)}, u32[]{:S(2)}, u32[]{:S(2)}) collective-permute-start(bf16[128,2048]{1,0:T(8,128)(2,1)S(1)} %copy-done.31), channel_id=1, source_target_pairs={{0,1},{1,0},{2,3},{3,2},{4,5},{5,4},{6,7},{7,6},{8,9},{9,8},{10,11... | collective-permute-start | bytes 1572872 | tf_op jit(solution)/shard_map/ppermute | solution.py:22
  345.9 16.7 %collective-permute-start.18 = (bf16[128,2048]{1,0:T(8,128)(2,1)S(1)}, bf16[128,2048]{1,0:T(8,128)(2,1)S(1)}, u32[]{:S(2)}, u32[]{:S(2)}) collective-permute-start(bf16[128,2048]{1,0:T(8,128)(2,1)S(1)} %copy-done.35), channel_id=1, source_target_pairs={{0,8},{8,16},{16,24},{24,0},{1,9},{9,17},{17,25},{25,1},{2,10},{10... | collective-permute-start | bytes 1572872 | tf_op jit(solution)/shard_map/ppermute | solution.py:31
  348.5 36.5 %collective-permute-start.41 = (bf16[128,2048]{1,0:T(8,128)(2,1)S(1)}, bf16[128,2048]{1,0:T(8,128)(2,1)S(1)}, u32[]{:S(2)}, u32[]{:S(2)}) collective-permute-start(bf16[128,2048]{1,0:T(8,128)(2,1)S(1)} %slice.755), channel_id=1, source_target_pairs={{0,1},{1,0},{2,3},{3,2},{4,5},{5,4},{6,7},{7,6},{8,9},{9,8},{10,11... | collective-permute-start | bytes 1572872 | tf_op jit(solution)/shard_map/ppermute | solution.py:22
  348.6 25.2 %collective-permute-start.74 = (bf16[128,2048]{1,0:T(8,128)(2,1)S(1)}, bf16[128,2048]{1,0:T(8,128)(2,1)S(1)}, u32[]{:S(2)}, u32[]{:S(2)}) collective-permute-start(bf16[128,2048]{1,0:T(8,128)(2,1)S(1)} %slice.751), channel_id=1, source_target_pairs={{0,1},{1,0},{2,3},{3,2},{4,5},{5,4},{6,7},{7,6},{8,9},{9,8},{10,11... | collective-permute-start | bytes 1572872 | tf_op jit(solution)/shard_map/ppermute | solution.py:22
  350.6 23.2 %collective-permute-start.67 = (bf16[128,2048]{1,0:T(8,128)(2,1)S(1)}, bf16[128,2048]{1,0:T(8,128)(2,1)S(1)}, u32[]{:S(2)}, u32[]{:S(2)}) collective-permute-start(bf16[128,2048]{1,0:T(8,128)(2,1)S(1)} %fusion.151), channel_id=1, source_target_pairs={{0,8},{8,16},{16,24},{24,0},{1,9},{9,17},{17,25},{25,1},{2,10},{10... | collective-permute-start | bytes 1572872 | tf_op jit(solution)/shard_map/ppermute | solution.py:31
  362.8 22.3 %collective-permute-start.30 = (bf16[128,2048]{1,0:T(8,128)(2,1)S(1)}, bf16[128,2048]{1,0:T(8,128)(2,1)S(1)}, u32[]{:S(2)}, u32[]{:S(2)}) collective-permute-start(bf16[128,2048]{1,0:T(8,128)(2,1)S(1)} %fusion.157), channel_id=1, source_target_pairs={{0,8},{8,16},{16,24},{24,0},{1,9},{9,17},{17,25},{25,1},{2,10},{10... | collective-permute-start | bytes 1572872 | tf_op jit(solution)/shard_map/ppermute | solution.py:31
  374.1 22.2 %collective-permute-start.75 = (bf16[128,2048]{1,0:T(8,128)(2,1)S(1)}, bf16[128,2048]{1,0:T(8,128)(2,1)S(1)}, u32[]{:S(2)}, u32[]{:S(2)}) collective-permute-start(bf16[128,2048]{1,0:T(8,128)(2,1)S(1)} %fusion.149), channel_id=1, source_target_pairs={{0,8},{8,16},{16,24},{24,0},{1,9},{9,17},{17,25},{25,1},{2,10},{10... | collective-permute-start | bytes 1572872 | tf_op jit(solution)/shard_map/ppermute | solution.py:31
  385.2 20.4 %collective-permute-start.42 = (bf16[128,2048]{1,0:T(8,128)(2,1)S(1)}, bf16[128,2048]{1,0:T(8,128)(2,1)S(1)}, u32[]{:S(2)}, u32[]{:S(2)}) collective-permute-start(bf16[128,2048]{1,0:T(8,128)(2,1)S(1)} %fusion.155), channel_id=1, source_target_pairs={{0,8},{8,16},{16,24},{24,0},{1,9},{9,17},{17,25},{25,1},{2,10},{10... | collective-permute-start | bytes 1572872 | tf_op jit(solution)/shard_map/ppermute | solution.py:31
  435.6 20.4 %collective-permute-start.86 = (bf16[128,512]{1,0:T(8,128)(2,1)}, bf16[128,512]{1,0:T(8,128)(2,1)}, u32[]{:S(2)}, u32[]{:S(2)}) collective-permute-start(bf16[128,512]{1,0:T(8,128)(2,1)} %get-tuple-element.164), channel_id=1, source_target_pairs={{0,16},{4,20},{8,24},{12,28},{16,0},{20,4},{24,8},{28,12},{1,17},{... | collective-permute-start | bytes 393224 | tf_op jit(solution)/shard_map/ppermute | solution.py:261
  438.6 19.0 %collective-permute-start.87 = (bf16[128,512]{1,0:T(8,128)(2,1)S(1)}, bf16[128,512]{1,0:T(8,128)(2,1)}, u32[]{:S(2)}, u32[]{:S(2)}) collective-permute-start(bf16[128,512]{1,0:T(8,128)(2,1)S(1)} %get-tuple-element.163), channel_id=1, source_target_pairs={{0,12},{4,16},{8,20},{12,24},{16,28},{20,0},{24,4},{28,8},{1,13},{... | collective-permute-start | bytes 393224 | tf_op jit(solution)/shard_map/ppermute | solution.py:261
  440.0 17.6 %collective-permute-start.88 = (bf16[128,512]{1,0:T(8,128)(2,1)S(1)}, bf16[128,512]{1,0:T(8,128)(2,1)}, u32[]{:S(2)}, u32[]{:S(2)}) collective-permute-start(bf16[128,512]{1,0:T(8,128)(2,1)S(1)} %get-tuple-element.162), channel_id=1, source_target_pairs={{0,8},{4,12},{8,16},{12,20},{16,24},{20,28},{24,0},{28,4},{1,9},{5... | collective-permute-start | bytes 393224 | tf_op jit(solution)/shard_map/ppermute | solution.py:261
  (151 other events, 1412.0 us)

commit v2 on v1

v2 whole, which is shorter than its diff:
```python
import functools

import jax
import jax.numpy as jnp
from jax import lax
from jax.experimental import pallas as pl
from jax.experimental.pallas import tpu as pltpu
from jax.sharding import Mesh, PartitionSpec as P

H = 16
KVH = 2
DH = 128
TOPK = 8
GROUP = H // KVH
STEPS = 2

NEG = -1e30
OPT = {
    "att": lambda cot, blocks: cot[0][1:] + [blocks[-1][1], blocks[-2][1]],
    "hop": lambda step, flipped, kv, cot: {1: [flipped], 3: cot[0][1:3] + [kv[2]] if cot else []}.get(step, []),
    "flip": lambda step, kv: {1: [kv[1]], 3: kv[3:4]}.get(step, []),
    "ga": lambda kv: [],
    "nh": lambda cot, normed, step: {2: cot[1:3], 3: cot[3:] + normed[0][:1] if normed else []}.get(step, []),
    "nf": lambda normed, step: normed[0][1:3] if step == 2 else [],
    "nb": lambda normed: normed[:4],
    "hb": lambda arrivals: [arrivals[0]],
    "ea": lambda normed: [],
    "eb": lambda rows: [],
    "row1": lambda backs: [],
    "ca": lambda backs: [],
    "attb": lambda back: [],
    "hop2": lambda back: [],
}
EPSILON = 1e-06
SCALE = DH ** (-0.5)
F32 = jnp.float32
BF16 = jnp.bfloat16
I32 = jnp.int32
SMEM = pl.BlockSpec(memory_space=pltpu.SMEM)
VMEM = pl.BlockSpec(memory_space=pltpu.VMEM)
MIB = 1 << 20


def dot_f32(a, b, dims=((1,), (0,))):
    return lax.dot_general(a, b, (dims, ((), ())), preferred_element_type=F32)


def flip_axis(value, name):
    return lax.ppermute(value, name, [(0, 1), (1, 0)])


def flip_xy(value):
    return lax.ppermute(value, ("x", "y"), [(i, 3 - i) for i in range(4)])


def ring_up(value):
    size = lax.axis_size("z")
    return lax.ppermute(value, "z", [(i, (i + 1) % size) for i in range(size)])


def line_up(value):
    size = lax.axis_size("z")
    return lax.ppermute(value, "z", [(i, i + 1) for i in range(size - 1)])


def line_down(value):
    size = lax.axis_size("z")
    return lax.ppermute(value, "z", [(i + 1, i) for i in range(size - 1)])


def ring_down(value):
    size = lax.axis_size("z")
    return lax.ppermute(value, "z", [(i, (i - 1) % size) for i in range(size)])


def to_chips(blocks):
    with jax.named_scope("to_y"):
        to_y = flip_axis(blocks[1], "y")
    with jax.named_scope("to_x"):
        to_x = flip_axis(blocks[2], "x")
    with jax.named_scope("to_xy"):
        to_xy = flip_xy(blocks[3])
    return [blocks[0], to_y, to_x, to_xy]


def params(mib):
    return pltpu.CompilerParams(vmem_limit_bytes=mib * MIB)


def cost(microseconds):
    return pl.CostEstimate(flops=0, bytes_accessed=int(microseconds * 1e6), transcendentals=0)


def gated(values, *others):
    return lax.optimization_barrier((*values, *others))[: len(values)]


def after(value, *others):
    return lax.optimization_barrier((value,) + others)[0]


def routing_kernel(experts, chosen_ref, raw_ref, cot_ref, payload_ref):
    rows, width = cot_ref.shape
    chosen = chosen_ref[...]
    raw = raw_ref[...]
    share = raw / jnp.sum(raw, axis=0, keepdims=True)
    names = lax.broadcasted_iota(I32, (experts, rows), 0)
    hit = jnp.zeros((experts, rows), F32)
    table = jnp.zeros((experts, rows), F32)
    for k in range(TOPK):
        here = names == chosen[k : k + 1]
        hit = hit + jnp.where(here, 1.0, 0.0)
        table = table + jnp.where(here, share[k : k + 1], 0.0)
    before = lax.broadcasted_iota(I32, (rows, rows), 0) < lax.broadcasted_iota(I32, (rows, rows), 1)
    earlier = dot_f32(hit.astype(BF16), jnp.where(before, 1.0, 0.0).astype(BF16))
    slots = jnp.where(hit > 0.5, earlier, -1.0)
    high = table.astype(BF16).astype(F32)
    middle = (table - high).astype(BF16).astype(F32)
    low = table - high - middle
    meta = jnp.concatenate([slots, high, middle, low], axis=0).astype(BF16)
    payload_ref[:, :width] = cot_ref[...]
    for block in range(4 * experts // rows):
        payload_ref[:, width + block * rows : width + (block + 1) * rows] = meta[
            block * rows : (block + 1) * rows
        ]


def routing(chosen, raw, cotangent, experts):
    rows, width = cotangent.shape
    return pl.pallas_call(
        functools.partial(routing_kernel, experts),
        in_specs=[VMEM] * 3,
        out_specs=VMEM,
        out_shape=jax.ShapeDtypeStruct((rows, width + 4 * experts), BF16),
        compiler_params=params(16),
        cost_estimate=cost(3),
        name="routing",
    )(chosen.T, raw.T, cotangent)


def table_row(meta, kind, experts, expert):
    rows = meta.shape[0]
    block, offset = divmod(kind * experts, rows)
    part = meta[:, block * rows : (block + 1) * rows].astype(F32)[offset : offset + experts]
    here = lax.broadcasted_iota(I32, part.shape, 0) == expert
    return jnp.sum(jnp.where(here, part, 0.0), axis=0, keepdims=True)


def table_column(meta_turned, kind, experts, expert):
    rows = meta_turned[0].shape[0]
    block, offset = divmod(kind * experts, rows)
    part = meta_turned[block]
    here = lax.broadcasted_iota(I32, part.shape, 1) == expert + offset
    return jnp.sum(jnp.where(here, part, 0.0), axis=1, keepdims=True)


def gather_kernel(experts, capacity, weighted, blocks, names_ref, *refs):
    token_refs = refs[:blocks]
    meta_refs = refs[blocks : 2 * blocks]
    out_refs = refs[2 * blocks : 2 * blocks + 4]
    pick_all, share_all = refs[2 * blocks + 4 :]
    sent_rows = out_refs[0].shape[0]
    rows = token_refs[0].shape[0]

    @pl.when(pl.program_id(0) == 0)
    def _():
        metas = [ref[...] for ref in meta_refs]
        places = lax.broadcasted_iota(I32, (sent_rows, rows), 0)
        for chip in range(4):
            expert = names_ref[chip]
            share = jnp.zeros((sent_rows, rows), F32)
            for which, meta in enumerate(metas):
                slot = table_row(meta, 0, experts, expert)
                target = jnp.where(slot >= 0, slot + which * capacity, -1.0).astype(I32)
                pick = places == target
                if weighted:
                    row = (
                        table_row(meta, 1, experts, expert)
                        + table_row(meta, 2, experts, expert)
                        + table_row(meta, 3, experts, expert)
                    )
                    share = share + jnp.where(pick, row, 0.0)
                pick_all[chip, :, which * rows : (which + 1) * rows] = jnp.where(
                    pick, 1.0, 0.0
                ).astype(BF16)
            if weighted:
                share_all[chip] = jnp.sum(share, axis=1, keepdims=True)

    tokens = jnp.concatenate([ref[...] for ref in token_refs], axis=0)
    for chip in range(4):
        found = dot_f32(pick_all[chip], tokens)
        if weighted:
            found = found * share_all[chip]
        out_refs[chip][...] = found.astype(BF16)


def gather_rows(names, token_blocks, meta_blocks, width, experts, capacity, weighted):
    rows = token_blocks[0].shape[0]
    blocks = len(token_blocks)
    sent_rows = blocks * capacity
    meta_width = 4 * experts
    cut = 512
    return pl.pallas_call(
        functools.partial(gather_kernel, experts, capacity, weighted, blocks),
        grid=(width // cut,),
        in_specs=[SMEM]
        + [pl.BlockSpec((rows, cut), lambda c: (0, c))] * blocks
        + [pl.BlockSpec((rows, meta_width), lambda c: (0, width // meta_width))] * blocks,
        out_specs=[pl.BlockSpec((sent_rows, cut), lambda c: (0, c))] * 4,
        out_shape=[jax.ShapeDtypeStruct((sent_rows, width), BF16)] * 4,
        scratch_shapes=[
            pltpu.VMEM((4, sent_rows, blocks * rows), BF16),
            pltpu.VMEM((4, sent_rows, 1), F32),
        ],
        compiler_params=params(32),
        cost_estimate=cost(4),
        name="gather_weighted" if weighted else "gather_plain",
    )(names, *token_blocks, *meta_blocks)


def expert_kernel(*refs):
    normed_refs = refs[0:4]
    cot_refs = refs[4:8]
    weight_refs = refs[8:11]
    row_refs = refs[11:15]
    made_refs = refs[15:19]
    gate, up, down, normed_all, cot_all, row_all, made_all, in_sem, weight_sem, out_sem = refs[19:]
    piece = normed_refs[0].shape[0]
    half = 2 * piece

    def place(chip):
        return pl.ds(chip * piece, piece)

    normed_in = [
        pltpu.make_async_copy(normed_refs[c], normed_all.at[place(c)], in_sem.at[0, c])
        for c in range(4)
    ]
    cot_in = [
        pltpu.make_async_copy(cot_refs[c], cot_all.at[place(c)], in_sem.at[1, c]) for c in range(4)
    ]
    weight_in = [
        pltpu.make_async_copy(weight_refs[w], held, weight_sem.at[w])
        for w, held in enumerate((gate, up, down))
    ]
    for copy in normed_in[:2] + weight_in[:2] + cot_in[:2] + weight_in[2:]:
        copy.start()
    for copy in normed_in[2:] + cot_in[2:]:
        copy.start()
    copies_out = []
    for part in range(2):
        chips = (2 * part, 2 * part + 1)
        rows = pl.ds(part * half, half)
        for c in chips:
            normed_in[c].wait()
        if part == 0:
            weight_in[0].wait()
        gate_act = dot_f32(normed_all[rows], gate[...])
        if part == 0:
            weight_in[1].wait()
        up_act = dot_f32(normed_all[rows], up[...])
        for c in chips:
            cot_in[c].wait()
        if part == 0:
            weight_in[2].wait()
        act_cot = dot_f32(cot_all[rows], down[...], ((1,), (1,)))
        sigma = jax.nn.sigmoid(gate_act)
        silu = gate_act * sigma
        gate_cot = (act_cot * up_act * sigma * (1.0 + gate_act * (1.0 - sigma))).astype(BF16)
        up_cot = (act_cot * silu).astype(BF16)
        activation = (silu * up_act).astype(BF16)
        row_all[rows] = (
            dot_f32(gate_cot, gate[...], ((1,), (1,))) + dot_f32(up_cot, up[...], ((1,), (1,)))
        ).astype(BF16)
        for c in chips:
            copy = pltpu.make_async_copy(row_all.at[place(c)], row_refs[c], out_sem.at[0, c])
            copy.start()
            copies_out.append(copy)
        made_all[rows] = dot_f32(activation, down[...]).astype(BF16)
        for c in chips:
            copy = pltpu.make_async_copy(made_all.at[place(c)], made_refs[c], out_sem.at[1, c])
            copy.start()
            copies_out.append(copy)
    for copy in copies_out:
        copy.wait()


def run_expert(normed_pieces, cot_pieces, gate_mat, up_mat, down_mat):
    piece, width = normed_pieces[0].shape
    anywhere = pl.BlockSpec(memory_space=pl.ANY)
    everything = pltpu.VMEM((4 * piece, width), BF16)
    result = pl.pallas_call(
        expert_kernel,
        in_specs=[anywhere] * 11,
        out_specs=[anywhere] * 8,
        out_shape=[jax.ShapeDtypeStruct((piece, width), BF16)] * 8,
        scratch_shapes=[
            pltpu.VMEM(gate_mat.shape, BF16),
            pltpu.VMEM(up_mat.shape, BF16),
            pltpu.VMEM(down_mat.shape, BF16),
        ]
        + [everything] * 4
        + [
            pltpu.SemaphoreType.DMA((2, 4)),
            pltpu.SemaphoreType.DMA((3,)),
            pltpu.SemaphoreType.DMA((2, 4)),
        ],
        compiler_params=params(60),
        cost_estimate=cost(18),
        name="expert",
    )(*normed_pieces, *cot_pieces, gate_mat, up_mat, down_mat)
    return result[0:4], result[4:8]


def combine_kernel(experts, capacity, blocks, names_ref, *refs):
    back_refs = refs[:4]
    meta_refs = refs[4 : 4 + blocks]
    own_refs = refs[4 + blocks : 4 + blocks + blocks // 2]
    other_ref = refs[4 + blocks + blocks // 2]
    pick_all = refs[5 + blocks + blocks // 2]

    @pl.when(pl.program_id(0) == 0)
    def _():
        fill_picks(
            experts, capacity, False, names_ref, back_refs[0].shape[0], meta_refs, pick_all
        )

    rows = meta_refs[0].shape[0]
    total = dot_f32(pick_all[...], jnp.concatenate([ref[...] for ref in back_refs], axis=0))
    for which in range(blocks):
        part = total[which * rows : (which + 1) * rows]
        if which % 2 == 0:
            own_refs[which // 2][...] = part
        else:
            other_ref[which // 2 * rows : (which // 2 + 1) * rows] = part.astype(BF16)


def fill_picks(experts, capacity, weighted, names_ref, piece, meta_refs, pick_all):
    rows = meta_refs[0].shape[0]
    places = lax.broadcasted_iota(I32, (rows, 4 * piece), 1)
    for which, meta_ref in enumerate(meta_refs):
        meta = meta_ref[...].astype(F32)
        turned = [meta[:, b * rows : (b + 1) * rows].T for b in range(meta.shape[1] // rows)]
        pick = jnp.zeros((rows, 4 * piece), F32)
        for chip in range(4):
            expert = names_ref[chip]
            slot = table_column(turned, 0, experts, expert)
            target = jnp.where(slot >= 0, slot + (which * capacity + chip * piece), -1.0)
            here = places == target.astype(I32)
            value = table_column(turned, 1, experts, expert) if weighted else 1.0
            pick = jnp.where(here, value, pick)
        pick_all[which * rows : (which + 1) * rows] = pick.astype(BF16)


def weighted_kernel(experts, capacity, blocks, names_ref, *refs):
    back_refs = refs[:4]
    meta_refs = refs[4 : 4 + blocks]
    cot_refs = refs[4 + blocks : 4 + 2 * blocks]
    own_refs = refs[4 + 2 * blocks : 4 + 2 * blocks + blocks // 2]
    other_ref, pick_all, dots_all = refs[4 + 2 * blocks + blocks // 2 :]
    piece, cut = back_refs[0].shape
    rows = meta_refs[0].shape[0]
    step = pl.program_id(0)

    @pl.when(step == 0)
    def _():
        fill_picks(experts, capacity, True, names_ref, piece, meta_refs, pick_all)
        dots_all[...] = jnp.zeros_like(dots_all)

    back = jnp.concatenate([ref[...] for ref in back_refs], axis=0)
    cots = jnp.concatenate([ref[...] for ref in cot_refs], axis=0)
    dots_all[...] += dot_f32(cots, back, ((1,), (1,)))
    total = dot_f32(pick_all[...], back)
    at = pl.ds(pl.multiple_of(step * cut, cut), cut)
    for which in range(blocks):
        part = total[which * rows : (which + 1) * rows]
        if which % 2 == 0:
            own_refs[which // 2][:, at] = part
        else:
            other_ref[which // 2 * rows : (which // 2 + 1) * rows, at] = part.astype(BF16)

    @pl.when(step == pl.num_programs(0) - 1)
    def _():
        width = other_ref.shape[1] - 4 * experts
        places = lax.broadcasted_iota(I32, (rows, 4 * piece), 1)
        lane = lax.broadcasted_iota(I32, (rows, 4 * experts), 1)
        for which in range(blocks):
            found = dots_all[which * rows : (which + 1) * rows]
            picked = pick_all[which * rows : (which + 1) * rows].astype(F32) > 0
            found = jnp.where(picked, found, 0.0)
            tail = jnp.zeros((rows, 4 * experts), F32)
            for chip in range(4):
                here = (places >= chip * piece) & (places < (chip + 1) * piece)
                value = jnp.sum(jnp.where(here, found, 0.0), axis=1, keepdims=True)
                for part in range(3):
                    low = value.astype(BF16).astype(F32)
                    tail = jnp.where(lane == names_ref[chip] + part * experts, low, tail)
                    value = value - low
            if which % 2 == 0:
                own_refs[which // 2][:, width:] = tail
            else:
                other_ref[which // 2 * rows : (which // 2 + 1) * rows, width:] = tail.astype(BF16)


def combine_rows(names, back, metas, width, experts, capacity, weighted):
    piece = back[0].shape[0]
    rows = metas[0].shape[0]
    blocks = len(metas)
    meta_width = 4 * experts
    cut = 512
    chunks = [pl.BlockSpec((piece, cut), lambda c: (0, c))] * 4
    metas_in = [pl.BlockSpec((rows, meta_width), lambda c: (0, width // meta_width))] * blocks
    if weighted:
        kernel = weighted_kernel
        metas_in = metas_in + [pl.BlockSpec((rows, cut), lambda c: (0, c))] * blocks
        metas = metas + metas
        width_out = width + meta_width
        own_spec = pl.BlockSpec((rows, width_out), lambda c: (0, 0))
        other_spec = pl.BlockSpec((blocks // 2 * rows, width_out), lambda c: (0, 0))
        scratch = [
            pltpu.VMEM((blocks * rows, 4 * piece), BF16),
            pltpu.VMEM((blocks * rows, 4 * piece), F32),
        ]
    else:
        kernel = combine_kernel
        width_out = width
        own_spec = pl.BlockSpec((rows, cut), lambda c: (0, c))
        other_spec = pl.BlockSpec((blocks // 2 * rows, cut), lambda c: (0, c))
        scratch = [pltpu.VMEM((blocks * rows, 4 * piece), BF16)]
    result = pl.pallas_call(
        functools.partial(kernel, experts, capacity, blocks),
        grid=(width // cut,),
        in_specs=[SMEM] + chunks + metas_in,
        out_specs=[own_spec] * (blocks // 2) + [other_spec],
        out_shape=[jax.ShapeDtypeStruct((rows, width_out), F32)] * (blocks // 2)
        + [jax.ShapeDtypeStruct((blocks // 2 * rows, width_out), BF16)],
        scratch_shapes=scratch,
        compiler_params=params(32),
        cost_estimate=cost(8),
        name="combine_weighted" if weighted else "combine_plain",
    )(names, *back, *metas)
    return result[:-1], result[-1]


def threshold(step, z_index, x_index):
    lower = jnp.where(step == 1, x_index == 1, step // 2 <= z_index)
    return jnp.where(step == 0, 0, jnp.where(lower, DH * 1024, -DH * 1024))


def stacked_heads(ref, kv_head):
    first = kv_head * GROUP
    return jnp.concatenate(
        [ref[:, (first + h) * DH : (first + h + 1) * DH] for h in range(GROUP)], axis=0
    )


def forward_kernel(count, ctx_ref, query_ref, residual_ref, gain_ref, *refs):
    kv_refs = refs[:count]
    attended_ref, hidden_ref, normed_ref, inverse_ref, log_ref = refs[count : count + 5]
    kv_all, score_all = refs[count + 5 :]
    rows = query_ref.shape[0]
    kv_width = KVH * DH
    for step in range(count):
        kv_all[2 * step * rows : (2 * step + 2) * rows] = kv_refs[step][...]
    z_index = ctx_ref[0]
    x_index = ctx_ref[1]
    shape = (rows, GROUP * rows)
    ahead = lax.broadcasted_iota(I32, shape, 0) - lax.rem(lax.broadcasted_iota(I32, shape, 1), rows)
    for kv_head in range(KVH):
        query = stacked_heads(query_ref, kv_head)

        def score(step, top):
            at = pl.ds(pl.multiple_of(step * rows, rows), rows)
            key = kv_all[at, kv_head * DH : (kv_head + 1) * DH]
            found = dot_f32(key, query, ((1,), (1,))) * SCALE
            found = jnp.where(ahead <= threshold(step, z_index, x_index), found, NEG)
            score_all[at] = found
            return jnp.maximum(top, jnp.max(found, axis=0, keepdims=True))

        top = lax.fori_loop(0, 2 * count, score, jnp.full((1, GROUP * rows), NEG, F32))

        def gather_values(step, state):
            total, mixed = state
            at = pl.ds(pl.multiple_of(step * rows, rows), rows)
            weight = jnp.exp(score_all[at] - top)
            value = kv_all[at, kv_width + kv_head * DH : kv_width + (kv_head + 1) * DH]
            total = total + jnp.sum(weight, axis=0, keepdims=True)
            mixed = mixed + dot_f32(value.T, weight.astype(BF16))
            return total, mixed

        total, mixed = lax.fori_loop(
            0,
            2 * count,
            gather_values,
            (jnp.zeros((1, GROUP * rows), F32), jnp.zeros((DH, GROUP * rows), F32)),
        )
        mixed = mixed / total
        log_sum = top + jnp.log(total)
        for h in range(GROUP):
            head = kv_head * GROUP + h
            at = slice(h * rows, (h + 1) * rows)
            attended_ref[:, head * DH : (head + 1) * DH] = mixed[:, at].T.astype(BF16)
            log_ref[head : head + 1, :] = log_sum[:, at]
    hidden = (residual_ref[...].astype(F32) + attended_ref[...].astype(F32)).astype(BF16)
    hidden_ref[...] = hidden
    wide = hidden.astype(F32)
    inverse = lax.rsqrt(jnp.mean(wide * wide, axis=1, keepdims=True) + EPSILON)
    inverse_ref[...] = inverse
    normed_ref[...] = (wide * inverse * gain_ref[...]).astype(BF16)


def attend_forward(ctx, query, residual, gain, kv_blocks):
    rows, width = query.shape
    count = len(kv_blocks)
    flat = jax.ShapeDtypeStruct((rows, width), BF16)
    return pl.pallas_call(
        functools.partial(forward_kernel, count),
        in_specs=[SMEM] + [VMEM] * (3 + count),
        out_specs=[VMEM] * 5,
        out_shape=[
            flat,
            flat,
            flat,
            jax.ShapeDtypeStruct((rows, 1), F32),
            jax.ShapeDtypeStruct((H, rows), F32),
        ],
        scratch_shapes=[
            pltpu.VMEM((2 * count * rows, 2 * KVH * DH), BF16),
            pltpu.VMEM((2 * count * rows, GROUP * rows), F32),
        ],
        compiler_params=params(60),
        cost_estimate=cost(12),
        name="attend_forward",
    )(ctx, query, residual, gain, *kv_blocks)


def backward_kernel(count, ctx_ref, *refs):
    (query_ref, attended_ref, hidden_ref, cot_ref, gain_ref, inverse_ref, log_ref) = refs[:7]
    ring_ref, own_ref, other_ref = refs[7:10]
    kv_refs = refs[10 : 10 + count]
    residual_ref, query_out = refs[10 + count : 12 + count]
    kv_outs = refs[12 + count : 12 + 2 * count]
    kv_all, part_all = refs[12 + 2 * count :]
    rows = query_ref.shape[0]
    kv_width = KVH * DH
    for step in range(count):
        kv_all[2 * step * rows : (2 * step + 2) * rows] = kv_refs[step][...]
    z_index = ctx_ref[0]
    x_index = ctx_ref[1]

    normed_cot = ring_ref[...].astype(F32) + own_ref[...] + other_ref[:rows].astype(F32)
    gained = gain_ref[...] * normed_cot
    hidden = hidden_ref[...].astype(F32)
    inverse = inverse_ref[...]
    mean = jnp.mean(hidden * gained, axis=1, keepdims=True)
    hidden_cot = inverse * gained - hidden * (inverse * inverse * inverse) * mean
    residual_ref[...] = (cot_ref[...].astype(F32) + hidden_cot).astype(BF16)

    lane = lax.broadcasted_iota(I32, (rows, DH), 1)
    dots = jnp.zeros((rows, DH), F32)
    for head in range(H):
        at = slice(head * DH, (head + 1) * DH)
        product = residual_ref[:, at].astype(F32) * attended_ref[:, at].astype(F32)
        dots = jnp.where(lane == head, jnp.sum(product, axis=1, keepdims=True), dots)
    dots = dots.T

    shape = (rows, GROUP * rows)
    ahead = lax.broadcasted_iota(I32, shape, 0) - lax.rem(lax.broadcasted_iota(I32, shape, 1), rows)
    for kv_head in range(KVH):
        query = stacked_heads(query_ref, kv_head)
        grad = stacked_heads(residual_ref, kv_head)
        heads = range(kv_head * GROUP, (kv_head + 1) * GROUP)
        log_row = jnp.concatenate([log_ref[h : h + 1, :] for h in heads], axis=1)
        dot_row = jnp.concatenate([dots[h : h + 1, :] for h in heads], axis=1)
        key_at = slice(kv_head * DH, (kv_head + 1) * DH)
        value_at = slice(kv_width + kv_head * DH, kv_width + (kv_head + 1) * DH)

        def visit(step, query_grad):
            at = pl.ds(pl.multiple_of(step * rows, rows), rows)
            key = kv_all[at, key_at]
            value = kv_all[at, value_at]
            found = dot_f32(key, query, ((1,), (1,))) * SCALE
            weight = jnp.where(ahead <= threshold(step, z_index, x_index), jnp.exp(found - log_row), 0.0)
            grad_weight = dot_f32(value, grad, ((1,), (1,)))
            score_cot = (weight * (grad_weight - dot_row)).astype(BF16)
            part_all[at, value_at] = dot_f32(weight.astype(BF16), grad)
            part_all[at, key_at] = dot_f32(score_cot, query) * SCALE
            return query_grad + dot_f32(key.T, score_cot)

        query_grad = lax.fori_loop(0, 2 * count, visit, jnp.zeros((DH, GROUP * rows), F32))
        query_grad = query_grad * SCALE
        for h in range(GROUP):
            head = kv_head * GROUP + h
            query_out[:, head * DH : (head + 1) * DH] = query_grad[
                :, h * rows : (h + 1) * rows
            ].T.astype(BF16)
    for step in range(count):
        found = part_all[2 * step * rows : 2 * (step + 1) * rows]
        kv_outs[step][...] = found.astype(kv_outs[step].dtype)


def attend_backward(ctx, query, attended, hidden, cot, gain, inverse, log_sum, parts, kv_blocks):
    rows, width = query.shape
    count = len(kv_blocks)
    flat = jax.ShapeDtypeStruct((rows, width), BF16)
    kv_shape = (2 * rows, 2 * KVH * DH)
    result = pl.pallas_call(
        functools.partial(backward_kernel, count),
        in_specs=[SMEM] + [VMEM] * (10 + count),
        out_specs=[VMEM] * (2 + count),
        out_shape=[flat, flat]
        + [jax.ShapeDtypeStruct(kv_shape, F32)] * (count - 1)
        + [jax.ShapeDtypeStruct(kv_shape, BF16)],
        scratch_shapes=[
            pltpu.VMEM((2 * count * rows, 2 * KVH * DH), BF16),
            pltpu.VMEM((2 * count * rows, 2 * KVH * DH), F32),
        ],
        compiler_params=params(60),
        cost_estimate=cost(15),
        name="attend_backward",
    )(ctx, query, attended, hidden, cot, gain, inverse, log_sum, *parts, *kv_blocks)
    return result[0], result[1], result[2:]


def per_device(
    residual,
    query_heads,
    key_heads,
    value_heads,
    norm_gain,
    chosen_experts,
    route_weights,
    gate_weight,
    up_weight,
    down_weight,
    cotangent,
):
    rows = residual.shape[1]
    width = residual.shape[2]
    kv_width = key_heads.shape[2]
    planes = lax.axis_size("z")
    experts = planes * 8
    capacity = (9 * rows * TOPK + 8 * experts - 1) // (8 * experts)
    capacity = (capacity + 3) // 4 * 4
    z_index = lax.axis_index("z")
    x_index = lax.axis_index("x")
    y_index = lax.axis_index("y")
    core_index = lax.axis_index("core")
    groups = [list(range(first, first + STEPS)) for first in range(0, planes, STEPS)]
    names = jnp.stack(
        [
            ((z_index * 2 + (x_index ^ (chip >> 1))) * 2 + (y_index ^ (chip & 1))) * 2 + core_index
            for chip in range(4)
        ]
    ).astype(I32)
    ctx = jnp.stack([z_index, x_index]).astype(I32)
    gain = norm_gain[None, :]

    kv_own = jnp.concatenate([key_heads[0], value_heads[0]], axis=1)
    with jax.named_scope("kv_flip"):
        kv_flipped = flip_axis(kv_own, "x")
    kv_blocks = [jnp.concatenate([kv_own, kv_flipped], axis=0)]
    with jax.named_scope("kv_hop"):
        for step in range(1, planes):
            kv_blocks.append(line_up(kv_blocks[-1]))

    chosen = chosen_experts[0]
    payload = routing(chosen, route_weights[0], cotangent[0], experts)

    def gather(blocks, index, weighted, *earlier):
        sent = gather_rows(
            after(names, *earlier), blocks, metas[index], width, experts, capacity, weighted
        )
        return to_chips(sent)

    def hop(block, *earlier):
        with jax.named_scope("hop"):
            return ring_up(after(block, *earlier))

    def both_cores(block, *earlier):
        with jax.named_scope("flip"):
            return [block, flip_axis(after(block, *earlier), "core")]

    cot_pieces = []
    metas = []
    payload_blocks = []
    block = payload
    for index, group in enumerate(groups):
        for step in group:
            with jax.named_scope("cot"):
                earlier = []
                if step:
                    waits = OPT["hop"](step, kv_flipped, kv_blocks, cot_pieces)
                    block = hop(block, *waits)
                    earlier = OPT["flip"](step, kv_blocks)
                payload_blocks.append(both_cores(block, *earlier))
        metas.append(sum([payload_blocks[step] for step in group], []))
        if index == 0:
            with jax.named_scope("cot0"):
                cot_pieces.append(gather(metas[0], 0, True, *OPT["ga"](kv_blocks)))
    attended, hidden, normed, inverse, log_sum = attend_forward(
        after(ctx, *OPT["att"](cot_pieces, payload_blocks)),
        query_heads[0],
        residual[0],
        gain,
        kv_blocks,
    )
    order = inverse
    for index in range(1, len(groups)):
        with jax.named_scope("cot1"):
            cot_pieces.append(gather(metas[index], index, True, order, *cot_pieces[-1][1:]))
        order = cot_pieces[-1][0]

    normed_blocks = []
    normed_pieces = []
    earlier = cot_pieces[-1][:3]
    block = normed
    for index, group in enumerate(groups):
        for step in group:
            with jax.named_scope("normed"):
                if step:
                    block = hop(block, *OPT["nh"](cot_pieces[-1], normed_pieces, step))
                normed_blocks.append(both_cores(block, *OPT["nf"](normed_pieces, step)))
        tokens = sum([normed_blocks[step] for step in group], [])
        with jax.named_scope("normed1" if index else "normed0"):
            normed_pieces.append(gather(tokens, index, False, *earlier))
        earlier = OPT["nb"](normed_pieces[-1]) + cot_pieces[-1][3:]
    order = normed_pieces[-1][0]
    row_pieces = []
    made_pieces = []
    for index in range(len(groups)):
        pieces = normed_pieces[index]
        waits = OPT['ea'](normed_pieces) if index == 0 else OPT['eb'](row_first)
        pieces = [after(pieces[0], order, *waits)] + pieces[1:]
        row_cot, produced = run_expert(
            pieces, cot_pieces[index], gate_weight[0], up_weight[0], down_weight[0]
        )
        order = row_cot[0]
        row_first = row_cot
        row_pieces.append(row_cot)
        made_pieces.append(produced)

    def sums(back, index, weighted, *earlier):
        own, other = combine_rows(
            after(names, *earlier), back, metas[index], width, experts, capacity, weighted
        )
        with jax.named_scope("sum_flip"):
            return own, flip_axis(other, "core")

    def term(parts, at):
        own, other = parts
        return own[at] + other[at * rows : (at + 1) * rows].astype(F32)

    row_backs = []
    row_sums = []
    for index in range(len(groups)):
        with jax.named_scope("row1" if index else "row0"):
            row_backs.append(to_chips(gated(row_pieces[index], *OPT['row1'](row_backs))))
    for index in range(len(groups)):
        with jax.named_scope("row1" if index else "row0"):
            later = [first_moved] if index else OPT['ca'](row_backs)
            row_sums.append(sums(row_backs[index], index, False, order, *later))
        if index == 0:
            total = term(row_sums[0], 1).astype(BF16)
            with jax.named_scope("row_hop"):
                first_moved = ring_up(total)
        order = row_sums[-1][0][0]

    made_backs = [None] * len(groups)
    made_sums = [None] * len(groups)
    earlier = row_backs[-1]
    for index in reversed(range(len(groups))):
        with jax.named_scope("made1" if index else "made0"):
            made_backs[index] = to_chips(gated(made_pieces[index], *earlier[1:]))
        earlier = made_backs[index]

    with jax.named_scope("row_hop"):
        for step in range(2, planes):
            if step == 2:
                moved = first_moved
            else:
                moved = ring_up(after(total, *OPT['hop2'](made_backs[-1])))
            total = moved.astype(F32) + term(row_sums[step // STEPS], step % STEPS)
            total = total.astype(BF16)
        cot_terms = (ring_up(total), row_sums[0][0][0], row_sums[0][1])
    for index in reversed(range(1, len(groups))):
        with jax.named_scope("made1"):
            made_sums[index] = sums(made_backs[index], index, True, cot_terms[0])

    residual_gradient, query_gradient, kv_parts = attend_backward(
        after(ctx, made_sums[1][0][0], *OPT['attb'](made_backs[0])),
        query_heads[0],
        attended,
        hidden,
        cotangent[0],
        gain,
        inverse,
        log_sum,
        cot_terms,
        kv_blocks,
    )
    kv_total = kv_parts[-1]
    arrivals = []
    kv_low = []
    for step in reversed(range(planes - 1)):
        with jax.named_scope("kv_back_hop"):
            arrivals.append(line_down(kv_total.astype(BF16)))
        kv_total = arrivals[-1].astype(F32) + kv_parts[step]
        if step:
            kv_total = kv_total.astype(BF16)
            kv_low.append(kv_total)
    with jax.named_scope("kv_back_flip"):
        kv_flipped_total = flip_axis(kv_total[rows:].astype(BF16), "x")
    kv_total = kv_total[:rows] + kv_flipped_total.astype(F32)
    kv_total = kv_total.astype(BF16)
    key_gradient = kv_total[:, :kv_width]
    value_gradient = kv_total[:, kv_width:]

    made_total = None
    for step in reversed(range(STEPS, planes)):
        part = term(made_sums[step // STEPS], step % STEPS)
        with jax.named_scope("made_hop"):
            if made_total is not None:
                part = after(made_total, *OPT['hb'](arrivals)).astype(F32) + part
            made_total = ring_down(part.astype(BF16))
    with jax.named_scope("made0"):
        made_sums[0] = sums(made_backs[0], 0, True, kv_low[0])
    for step in reversed(range(STEPS)):
        moe_sum = made_total.astype(F32) + term(made_sums[0], step)
        if step:
            with jax.named_scope("made_hop"):
                made_total = ring_down(moe_sum.astype(BF16))
    layer_out = (hidden.astype(F32) + moe_sum[:, :width]).astype(BF16)

    found = moe_sum[:, width:].reshape(rows, 4, experts)
    found = found[:, 0] + found[:, 1] + found[:, 2]
    hits = chosen[:, :, None] == jnp.arange(experts, dtype=I32)
    route_dot = jnp.sum(jnp.where(hits, found[:, None, :], 0.0), axis=2)
    share_raw = route_weights[0]
    route_total = jnp.sum(share_raw, axis=1, keepdims=True)
    route_share = share_raw / route_total
    route_gradient = (
        route_dot - jnp.sum(route_share * route_dot, axis=1, keepdims=True)
    ) / route_total
    return (
        layer_out[None],
        residual_gradient[None],
        query_gradient[None],
        key_gradient[None],
        value_gradient[None],
        route_gradient[None],
    )


def solution(mesh):
    fine = Mesh(
        mesh.devices.reshape(mesh.shape["ctx"] // 2, 2, mesh.shape["exp"] // 2, 2),
        ("z", "x", "y", "core"),
    )
    tokens = P(("y", "core"), ("z", "x"), None)
    expert = P(("z", "x", "y", "core"), None, None)
    return jax.shard_map(
        per_device,
        mesh=fine,
        in_specs=(tokens,) * 4 + (P(),) + (tokens,) * 2 + (expert,) * 3 + (tokens,),
        out_specs=(tokens,) * 6,
        check_vma=False,
    )
```

time: 469 us -> 386 us (0.82)
  Pallas kernels: 0 us -> 102 us
  matrix products: 89.3 us -> 0 us
  local copies, waits for them, and re-layouts: 86.9 us -> 13.5 us
  waiting for transfers between devices: 136 us -> 182 us
  other arithmetic: 50.4 us -> 10.7 us
  starting transfers between devices: 94.4 us -> 69.9 us
    pallas_call x0 -> x13, Pallas kernels: none -> 102 us  [the longest x2 35.6 us: run_expert(): pl.pallas_call(expert_kernel, in_specs=[anywhere] * 11, out_specs=[anywhe...]
    dot_general x51 -> x0, matrix products: 89.3 us -> none  [the longest x45 73.5 us: dot_f32(): return lax.dot_general(a, b, (dims, ((), ())), preferred_element_type=F32)]
    ppermute x14 -> x9, waiting for transfers between devices: 12.1 us -> 74.6 us  [the longest x3 39.1 us: line_up(): return lax.ppermute(value, 'z', [(i, i + 1) for i in range(size - 1)])]
    slice x33 -> x3, local copies, waits for them, and re-layouts: 33.3 us -> 0.11 us  [the longest x2 0.09 us: per_device(): found = moe_sum[:, width:].reshape(rows, 4, experts)]
    ppermute x48 -> x30, starting transfers between devices: 40.1 us -> 16.9 us  [flip_axis(): return lax.ppermute(value, name, [(0, 1), (1, 0)])]
    ppermute x16 -> x8, waiting for transfers between devices: 52.7 us -> 31.8 us  [flip_xy(): return lax.ppermute(value, ('x', 'y'), [(i, 3 - i) for i in range(4)])]
    convert_element_type x18 -> x6, other arithmetic: 24.2 us -> 3.92 us  [the longest x2 2.29 us: per_device(): made_total = ring_down(part.astype(BF16))]
    ppermute x12 -> x9, waiting for transfers between devices: 51.8 us -> 66.8 us  [ring_up(): return lax.ppermute(value, 'z', [(i, (i + 1) % size) for i in range(size)])]
  transfers between devices with their start and end apart: 91 -> 56, of which waited for: 36 -> 23; matrix products, arithmetic and copies ran while one was open for 40% -> 2% of each run, Pallas kernels for 0% -> 16%
where the time goes in v2:
time: 386 us; the launch traced here: 380 us
  waiting for transfers between devices  182 us (47%)
  Pallas kernels  102 us (26%)
  starting transfers between devices  69.9 us (18%)
  local copies, waits for them, and re-layouts  13.5 us (3%)
  other arithmetic  10.7 us (3%)
    ppermute x9, waiting for transfers between devices, ring_up(): return lax.ppermute(value, 'z', [(i, (i + 1) % size) for i in range(size)])  66.8 us
    ppermute x3, waiting for transfers between devices, line_up(): return lax.ppermute(value, 'z', [(i, i + 1) for i in range(size - 1)])  39.1 us
    pallas_call x2, Pallas kernels, run_expert(): pl.pallas_call(expert_kernel, in_specs=[anywhere] * 11, out_specs=[anywhe...  35.6 us
    ppermute x8, waiting for transfers between devices, flip_xy(): return lax.ppermute(value, ('x', 'y'), [(i, 3 - i) for i in range(4)])  31.8 us
    ppermute x3, waiting for transfers between devices, line_down(): return lax.ppermute(value, 'z', [(i + 1, i) for i in range(size - 1)])  26.4 us
    pallas_call x4, Pallas kernels, combine_rows(): pl.pallas_call(functools.partial(kernel, experts, capacity, blocks), grid...  24.2 us
    ppermute x8, starting transfers between devices, flip_xy(): return lax.ppermute(value, ('x', 'y'), [(i, 3 - i) for i in range(4)])  17.7 us
    ppermute x30, starting transfers between devices, flip_axis(): return lax.ppermute(value, name, [(0, 1), (1, 0)])  16.9 us
  transfers between devices with their start and end apart: 56, of which 23 were waited for; matrix products, arithmetic and copies ran while one was open for 2% of the time, Pallas kernels for 16%

profile of v2, /device:TPU:0, one launch (start us, length us, event | category | flops | bytes accessed | tf_op | source)
XLA Modules:
  0.0 379.5 jit_solution(13852002649937013825)
XLA Ops:
  1.6 3.0 collective-permute-start.1
  9.9 3.5 collective-permute-start.3
  13.5 13.0 %collective-permute-done.3.refs_1_.refs_11_ = bf16[256,512]{1,0:T(8,128)(2,1)S(1)} collective-permute-done((bf16[256,512]{1,0:T(8,128)(2,1)S(1)}, bf16[256,512]{1,0:T(8,128)(2,1)S(1)}, u32[]{:S(2)}, u32[]{:S(2)}) %collective-permute-start.3) | collective-permute-done | bytes 262176 | tf_op jit(solution)/shard_map/kv_hop/ppermute | solution.py:63
  28.5 3.7 gather_weighted.2
  36.0 2.5 collective-permute-start.8
  38.6 3.5 collective-permute-start.9
  42.1 13.8 %collective-permute-done.9.refs_2_.refs_12_ = bf16[256,512]{1,0:T(8,128)(2,1)S(1)} collective-permute-done((bf16[256,512]{1,0:T(8,128)(2,1)S(1)}, bf16[256,512]{1,0:T(8,128)(2,1)S(1)}, u32[]{:S(2)}, u32[]{:S(2)}) %collective-permute-start.9) | collective-permute-done | bytes 262176 | tf_op jit(solution)/shard_map/kv_hop/ppermute | solution.py:63
  55.9 2.5 collective-permute-start.10
  58.4 3.5 collective-permute-start.11
  62.4 12.3 %collective-permute-done.11.refs_3_.refs_13_ = bf16[256,512]{1,0:T(8,128)(2,1)S(1)} collective-permute-done((bf16[256,512]{1,0:T(8,128)(2,1)S(1)}, bf16[256,512]{1,0:T(8,128)(2,1)S(1)}, u32[]{:S(2)}, u32[]{:S(2)}) %collective-permute-start.11) | collective-permute-done | bytes 262176 | tf_op jit(solution)/shard_map/kv_hop/ppermute | solution.py:63
  77.5 12.1 %attend_forward.1 = (bf16[128,2048]{1,0:T(8,128)(2,1)}, bf16[128,2048]{1,0:T(8,128)(2,1)}, bf16[128,2048]{1,0:T(8,128)(2,1)}, f32[128,1]{1,0:T(8,128)}, f32[16,128]{1,0:T(8,128)}) custom-call(s32[2]{0:T(128)} %pad_add_fusion.ctx_ref, bf16[128,2048]{1,0:T(8,128)(2,1)} %bitcast.52, bf16[128,2048]{1,0:T(8,128)(2,1)} %bitcast.54, f32[1,2048]{1,0:T(1,128)} %bitcast.60, ...), custom_call_target="tpu_custom_call" | custom-call | bytes 12000000 | tf_op jit(solution)/shard_map/attend_forward/pallas_call | solution.py:515
  90.7 3.7 gather_weighted.3
  96.3 2.5 collective-permute-start.17
  98.8 2.5 collective-permute-start.22
  101.2 11.2 %collective-permute-done.17.refs_2_ = bf16[128,2048]{1,0:T(8,128)(2,1)S(1)} collective-permute-done((bf16[128,2048]{1,0:T(8,128)(2,1)S(1)}, bf16[128,2048]{1,0:T(8,128)(2,1)S(1)}, u32[]{:S(2)}, u32[]{:S(2)}) %collective-permute-start.17) | collective-permute-done | bytes 524320 | tf_op jit(solution)/shard_map/normed/hop/ppermute | solution.py:58
  114.5 3.1 gather_plain.2
  120.5 5.1 %collective-permute-done.22.refs_7_ = bf16[144,2048]{1,0:T(8,128)(2,1)S(1)} collective-permute-done((bf16[144,2048]{1,0:T(8,128)(2,1)S(1)}, bf16[144,2048]{1,0:T(8,128)(2,1)S(1)}, u32[]{:S(2)}, u32[]{:S(2)}) %collective-permute-start.22) | collective-permute-done | bytes 589856 | tf_op jit(solution)/shard_map/cot1/to_xy/ppermute | solution.py:53
  125.6 3.1 collective-permute-done.23.refs_0_
  128.7 2.5 collective-permute-start.21
  131.1 12.8 %collective-permute-done.25.refs_2_ = bf16[128,2048]{1,0:T(8,128)(2,1)S(1)} collective-permute-done((bf16[128,2048]{1,0:T(8,128)(2,1)S(1)}, bf16[128,2048]{1,0:T(8,128)(2,1)S(1)}, u32[]{:S(2)}, u32[]{:S(2)}) %collective-permute-start.25) | collective-permute-done | bytes 524320 | tf_op jit(solution)/shard_map/normed/hop/ppermute | solution.py:58
  144.5 5.3 %collective-permute-done.21.refs_3_ = bf16[144,2048]{1,0:T(8,128)(2,1)S(1)} collective-permute-done((bf16[144,2048]{1,0:T(8,128)(2,1)S(1)}, bf16[144,2048]{1,0:T(8,128)(2,1)S(1)}, u32[]{:S(2)}, u32[]{:S(2)}) %collective-permute-start.21) | collective-permute-done | bytes 589856 | tf_op jit(solution)/shard_map/normed0/to_xy/ppermute | solution.py:53
  149.8 4.1 %gather_plain.3 = (bf16[144,2048]{1,0:T(8,128)(2,1)S(1)}, bf16[144,2048]{1,0:T(8,128)(2,1)}, bf16[144,2048]{1,0:T(8,128)(2,1)}, bf16[144,2048]{1,0:T(8,128)(2,1)}) custom-call(s32[4]{0:T(128)S(1)} %pad_add_fusion.1.names_ref, bf16[128,2048]{1,0:T(8,128)(2,1)S(1)} %collective-permute-done.23.refs_0_, bf16[128,2048]{1,0:T(8,128)(2,1)S(1)} %collective-permute-done.24.refs_1_, ...), custom_call_target="tpu_custom_call" | custom-call | bytes 4000000 | tf_op jit(solution)/shard_map/normed1/gather_plain/pallas_call | solution.py:203
  155.8 2.5 collective-permute-start.29
  158.3 17.6 %expert.2 = (bf16[144,2048]{1,0:T(8,128)(2,1)}, bf16[144,2048]{1,0:T(8,128)(2,1)}, bf16[144,2048]{1,0:T(8,128)(2,1)}, bf16[144,2048]{1,0:T(8,128)(2,1)}, bf16[14...) custom-call(bf16[144,2048]{1,0:T(8,128)(2,1)} %copy-done.10, ...), custom_call_target="tpu_custom_call" | custom-call | bytes 18000000 | tf_op jit(solution)/shard_map/expert/pallas_call | solution.py:291
  176.9 2.5 collective-permute-start.32
  179.4 6.1 %collective-permute-done.29.refs_3_ = bf16[144,2048]{1,0:T(8,128)(2,1)} collective-permute-done((bf16[144,2048]{1,0:T(8,128)(2,1)}, bf16[144,2048]{1,0:T(8,128)(2,1)}, u32[]{:S(2)}, u32[]{:S(2)}) %collective-permute-start.29) | collective-permute-done | bytes 589856 | tf_op jit(solution)/shard_map/normed1/to_xy/ppermute | solution.py:53
  185.5 18.0 %expert.3 = (bf16[144,2048]{1,0:T(8,128)(2,1)}, bf16[144,2048]{1,0:T(8,128)(2,1)}, bf16[144,2048]{1,0:T(8,128)(2,1)}, bf16[144,2048]{1,0:T(8,128)(2,1)}, bf16[14...) custom-call(bf16[144,2048]{1,0:T(8,128)(2,1)} %copy-done.12, ...), custom_call_target="tpu_custom_call" | custom-call | bytes 18000000 | tf_op jit(solution)/shard_map/expert/pallas_call | solution.py:291
  203.5 4.9 %collective-permute-done.32.refs_3_ = bf16[144,2048]{1,0:T(8,128)(2,1)} collective-permute-done((bf16[144,2048]{1,0:T(8,128)(2,1)}, bf16[144,2048]{1,0:T(8,128)(2,1)}, u32[]{:S(2)}, u32[]{:S(2)}) %collective-permute-start.32) | collective-permute-done | bytes 589856 | tf_op jit(solution)/shard_map/row0/to_xy/ppermute | solution.py:53
  209.6 5.2 %combine_plain.2 = (f32[128,2048]{1,0:T(8,128)S(1)}, f32[128,2048]{1,0:T(8,128)S(1)}, bf16[256,2048]{1,0:T(8,128)(2,1)S(1)}) custom-call(s32[4]{0:T(128)S(1)} %pad_add_fusion.1.names_ref, bf16[144,2048]{1,0:T(8,128)(2,1)S(1)} %copy-done.13, bf16[144,2048]{1,0:T(8,128)(2,1)} %collective-permute-done.30.refs_1_, ...), custom_call_target="tpu_custom_call" | custom-call | bytes 8000000 | tf_op jit(solution)/shard_map/row0/combine_plain/pallas_call | solution.py:429
  216.1 2.4 collective-permute-start.37
  218.6 2.5 collective-permute-start.34
  221.1 13.7 %collective-permute-done.34 = bf16[128,2048]{1,0:T(8,128)(2,1)S(1)} collective-permute-done((bf16[128,2048]{1,0:T(8,128)(2,1)S(1)}, bf16[128,2048]{1,0:T(8,128)(2,1)S(1)}, u32[]{:S(2)}, u32[]{:S(2)}) %collective-permute-start.34) | collective-permute-done | bytes 524320 | tf_op jit(solution)/shard_map/row_hop/ppermute | solution.py:58
  234.9 9.6 %collective-permute-done.37.refs_3_ = bf16[144,2048]{1,0:T(8,128)(2,1)S(1)} collective-permute-done((bf16[144,2048]{1,0:T(8,128)(2,1)S(1)}, bf16[144,2048]{1,0:T(8,128)(2,1)S(1)}, u32[]{:S(2)}, u32[]{:S(2)}) %collective-permute-start.37) | collective-permute-done | bytes 589856 | tf_op jit(solution)/shard_map/row1/to_xy/ppermute | solution.py:53
  244.5 4.4 %combine_plain.3 = (f32[128,2048]{1,0:T(8,128)S(1)}, f32[128,2048]{1,0:T(8,128)S(1)}, bf16[256,2048]{1,0:T(8,128)(2,1)S(1)}) custom-call(s32[4]{0:T(128)S(1)} %pad_add_fusion.1.names_ref, bf16[144,2048]{1,0:T(8,128)(2,1)S(1)} %copy-done.11, bf16[144,2048]{1,0:T(8,128)(2,1)S(1)} %collective-permute-done.35.refs_1_, ...), custom_call_target="tpu_custom_call" | custom-call | bytes 8000000 | tf_op jit(solution)/shard_map/row1/combine_plain/pallas_call | solution.py:429
  248.9 2.6 collective-permute-done.38
  251.8 2.5 collective-permute-start.39
  255.4 2.4 collective-permute-start.43
  257.8 10.8 %collective-permute-done.39 = bf16[128,2048]{1,0:T(8,128)(2,1)S(1)} collective-permute-done((bf16[128,2048]{1,0:T(8,128)(2,1)S(1)}, bf16[128,2048]{1,0:T(8,128)(2,1)S(1)}, u32[]{:S(2)}, u32[]{:S(2)}) %collective-permute-start.39) | collective-permute-done | bytes 524320 | tf_op jit(solution)/shard_map/row_hop/ppermute | solution.py:58
  268.8 15.2 %collective-permute-done.40.refs_7_ = bf16[128,2048]{1,0:T(8,128)(2,1)S(1)} collective-permute-done((bf16[128,2048]{1,0:T(8,128)(2,1)S(1)}, bf16[128,2048]{1,0:T(8,128)(2,1)S(1)}, u32[]{:S(2)}, u32[]{:S(2)}) %collective-permute-start.40) | collective-permute-done | bytes 524320 | tf_op jit(solution)/shard_map/row_hop/ppermute | solution.py:58
  284.9 7.2 %combine_weighted.2 = (f32[128,2176]{1,0:T(8,128)S(1)}, f32[128,2176]{1,0:T(8,128)S(1)}, bf16[256,2176]{1,0:T(8,128)(2,1)S(1)}) custom-call(s32[4]{0:T(128)S(1)} %pad_add_fusion.1.names_ref, bf16[144,2048]{1,0:T(8,128)(2,1)S(1)} %copy-done.15, bf16[144,2048]{1,0:T(8,128)(2,1)S(1)} %collective-permute-done.41.refs_1_, ...), custom_call_target="tpu_custom_call" | custom-call | bytes 8000000 | tf_op jit(solution)/shard_map/made1/combine_weighted/pallas_call | solution.py:429
  293.3 2.5 collective-permute-start.50
  298.3 15.2 %attend_backward.1 = (bf16[128,2048]{1,0:T(8,128)(2,1)}, bf16[128,2048]{1,0:T(8,128)(2,1)}, f32[256,512]{1,0:T(8,128)}, f32[256,512]{1,0:T(8,128)}, f32[256,512]{1,0:T(8,128)}, /*index=5*/bf16[256,512]{1,0:T(8,128)(2,1)}) custom-call(s32[2]{0:T(128)} %pad_add_fusion.ctx_ref, bf16[128,2048]{1,0:T(8,128)(2,1)} %bitcast.53, ...), custom_call_target="tpu_custom_call" | custom-call | bytes 15000000 | tf_op jit(solution)/shard_map/attend_backward/pallas_call | solution.py:606
  314.9 8.3 %collective-permute-done.46 = bf16[256,512]{1,0:T(8,128)(2,1)S(1)} collective-permute-done((bf16[256,512]{1,0:T(8,128)(2,1)}, bf16[256,512]{1,0:T(8,128)(2,1)S(1)}, u32[]{:S(2)}, u32[]{:S(2)}) %collective-permute-start.46) | collective-permute-done | bytes 262176 | tf_op jit(solution)/shard_map/kv_back_hop/ppermute | solution.py:68
  329.7 7.4 %combine_weighted.3 = (f32[128,2176]{1,0:T(8,128)S(1)}, f32[128,2176]{1,0:T(8,128)S(1)}, bf16[256,2176]{1,0:T(8,128)(2,1)S(1)}) custom-call(s32[4]{0:T(128)S(1)} %pad_add_fusion.1.names_ref, bf16[144,2048]{1,0:T(8,128)(2,1)S(1)} %copy-done.14, bf16[144,2048]{1,0:T(8,128)(2,1)S(1)} %copy-done.17, bf16[144,2048]{1,0:T(8,128)(2,1)S(1)} %copy-done.19, ...), custom_call_target="tpu_custom_call" | custom-call | bytes 8000000 | tf_op jit(solution)/shard_map/made0/combine_weighted/pallas_call | solution.py:429
  338.5 2.1 collective-permute-start.47
  342.0 18.1 %collective-permute-done.54 = bf16[256,512]{1,0:T(8,128)(2,1)S(1)} collective-permute-done((bf16[256,512]{1,0:T(8,128)(2,1)S(1)}, bf16[256,512]{1,0:T(8,128)(2,1)S(1)}, u32[]{:S(2)}, u32[]{:S(2)}) %collective-permute-start.54) | collective-permute-done | bytes 262176 | tf_op jit(solution)/shard_map/kv_back_hop/ppermute | solution.py:68
  362.8 2.9 collective-permute-done.55
  367.2 9.1 %collective-permute-done.52 = bf16[128,2176]{1,0:T(8,128)(2,1)S(1)} collective-permute-done((bf16[128,2176]{1,0:T(8,128)(2,1)}, bf16[128,2176]{1,0:T(8,128)(2,1)S(1)}, u32[]{:S(2)}, u32[]{:S(2)}) %collective-permute-start.52) | collective-permute-done | bytes 557088 | tf_op jit(solution)/shard_map/made_hop/ppermute | solution.py:73
  (210 shorter events, 53.1 us)
Async XLA Ops:
  1.6 6.5 %collective-permute-start.1 = (bf16[128,512]{1,0:T(8,128)(2,1)S(1)}, bf16[128,512]{1,0:T(8,128)(2,1)S(1)}, u32[]{:S(2)}, u32[]{:S(2)}) collective-permute-start(bf16[128,512]{1,0:T(8,128)(2,1)S(1)} %pad_maximum_fusion.1), channel_id=1, source_target_pairs={{0,4},{4,0},{1,5},{5,1},{2,6},{6,2},{3,7},{7,3},{8,12},{12,8},{9,1... | collective-permute-start | bytes 393224 | tf_op jit(solution)/shard_map/kv_flip/ppermute | solution.py:49
  8.1 18.5 %collective-permute-start.2 = (bf16[128,2176]{1,0:T(8,128)(2,1)S(1)}, bf16[128,2176]{1,0:T(8,128)(2,1)S(1)}, u32[]{:S(2)}, u32[]{:S(2)}) collective-permute-start(bf16[128,2176]{1,0:T(8,128)(2,1)S(1)} %routing.1.refs_0_.refs_4_.refs_8_), channel_id=1, source_target_pairs={{0,8},{8,16},{16,24},{24,0},{1,9},{9,17},{17,25},{25,1},{2,10},{10... | collective-permute-start | bytes 1671176 | tf_op jit(solution)/shard_map/cot/hop/ppermute | solution.py:58
  9.9 16.6 %collective-permute-start.3 = (bf16[256,512]{1,0:T(8,128)(2,1)S(1)}, bf16[256,512]{1,0:T(8,128)(2,1)S(1)}, u32[]{:S(2)}, u32[]{:S(2)}) collective-permute-start(bf16[256,512]{1,0:T(8,128)(2,1)S(1)} %pad_maximum_fusion.refs_0_.refs_10_), channel_id=1, source_target_pairs={{0,8},{8,16},{16,24},{1,9},{9,17},{17,25},{2,10},{10,18},{18,26},{... | collective-permute-start | bytes 786440 | tf_op jit(solution)/shard_map/kv_hop/ppermute | solution.py:63
  13.4 13.2 %collective-permute-start = (bf16[128,2176]{1,0:T(8,128)(2,1)S(1)}, bf16[128,2176]{1,0:T(8,128)(2,1)S(1)}, u32[]{:S(2)}, u32[]{:S(2)}) collective-permute-start(bf16[128,2176]{1,0:T(8,128)(2,1)S(1)} %routing.1.refs_0_.refs_4_.refs_8_), channel_id=1, source_target_pairs={{0,1},{1,0},{2,3},{3,2},{4,5},{5,4},{6,7},{7,6},{8,9},{9,8},{10,11... | collective-permute-start | bytes 1671176 | tf_op jit(solution)/shard_map/cot/flip/ppermute | solution.py:49
  33.0 22.8 %collective-permute-start.5 = (bf16[144,2048]{1,0:T(8,128)(2,1)S(1)}, bf16[144,2048]{1,0:T(8,128)(2,1)S(1)}, u32[]{:S(2)}, u32[]{:S(2)}) collective-permute-start(bf16[144,2048]{1,0:T(8,128)(2,1)S(1)} %get-tuple-element.98), channel_id=1, source_target_pairs={{0,2},{2,0},{1,3},{3,1},{4,6},{6,4},{5,7},{7,5},{8,10},{10,8},{9,1... | collective-permute-start | bytes 1769480 | tf_op jit(solution)/shard_map/cot0/to_y/ppermute | solution.py:49
  34.5 21.3 %collective-permute-start.6 = (bf16[144,2048]{1,0:T(8,128)(2,1)S(1)}, bf16[144,2048]{1,0:T(8,128)(2,1)S(1)}, u32[]{:S(2)}, u32[]{:S(2)}) collective-permute-start(bf16[144,2048]{1,0:T(8,128)(2,1)S(1)} %get-tuple-element.99), channel_id=1, source_target_pairs={{0,4},{4,0},{1,5},{5,1},{2,6},{6,2},{3,7},{7,3},{8,12},{12,8},{9,1... | collective-permute-start | bytes 1769480 | tf_op jit(solution)/shard_map/cot0/to_x/ppermute | solution.py:49
  36.0 19.8 %collective-permute-start.8 = (bf16[128,2176]{1,0:T(8,128)(2,1)S(1)}, bf16[128,2176]{1,0:T(8,128)(2,1)S(1)}, u32[]{:S(2)}, u32[]{:S(2)}) collective-permute-start(bf16[128,2176]{1,0:T(8,128)(2,1)S(1)} %collective-permute-done.2.refs_2_.refs_6_.refs_10_), channel_id=1, source_target_pairs={{0,8},{8,16},{16,24},{24,0},{1,9},{9,17},{17,25},{25,1},{2,10},{10... | collective-permute-start | bytes 1671176 | tf_op jit(solution)/shard_map/cot/hop/ppermute | solution.py:58
  38.6 17.2 %collective-permute-start.9 = (bf16[256,512]{1,0:T(8,128)(2,1)S(1)}, bf16[256,512]{1,0:T(8,128)(2,1)S(1)}, u32[]{:S(2)}, u32[]{:S(2)}) collective-permute-start(bf16[256,512]{1,0:T(8,128)(2,1)S(1)} %collective-permute-done.3.refs_1_.refs_11_), channel_id=1, source_target_pairs={{0,8},{8,16},{16,24},{1,9},{9,17},{17,25},{2,10},{10,18},{18,26},{... | collective-permute-start | bytes 786440 | tf_op jit(solution)/shard_map/kv_hop/ppermute | solution.py:63
  55.9 18.9 %collective-permute-start.10 = (bf16[128,2176]{1,0:T(8,128)(2,1)S(1)}, bf16[128,2176]{1,0:T(8,128)(2,1)S(1)}, u32[]{:S(2)}, u32[]{:S(2)}) collective-permute-start(bf16[128,2176]{1,0:T(8,128)(2,1)S(1)} %collective-permute-done.8.refs_0_.refs_4_.refs_8_), channel_id=1, source_target_pairs={{0,8},{8,16},{16,24},{24,0},{1,9},{9,17},{17,25},{25,1},{2,10},{10... | collective-permute-start | bytes 1671176 | tf_op jit(solution)/shard_map/cot/hop/ppermute | solution.py:58
  58.4 16.3 %collective-permute-start.11 = (bf16[256,512]{1,0:T(8,128)(2,1)S(1)}, bf16[256,512]{1,0:T(8,128)(2,1)S(1)}, u32[]{:S(2)}, u32[]{:S(2)}) collective-permute-start(bf16[256,512]{1,0:T(8,128)(2,1)S(1)} %collective-permute-done.9.refs_2_.refs_12_), channel_id=1, source_target_pairs={{0,8},{8,16},{16,24},{1,9},{9,17},{17,25},{2,10},{10,18},{18,26},{... | collective-permute-start | bytes 786440 | tf_op jit(solution)/shard_map/kv_hop/ppermute | solution.py:63
  61.9 14.3 %collective-permute-start.7 = (bf16[144,2048]{1,0:T(8,128)(2,1)S(1)}, bf16[144,2048]{1,0:T(8,128)(2,1)S(1)}, u32[]{:S(2)}, u32[]{:S(2)}) collective-permute-start(bf16[144,2048]{1,0:T(8,128)(2,1)S(1)} %get-tuple-element.100), channel_id=1, source_target_pairs={{0,6},{2,4},{4,2},{6,0},{1,7},{3,5},{5,3},{7,1},{8,14},{10,12},{12... | collective-permute-start | bytes 1769480 | tf_op jit(solution)/shard_map/cot0/to_xy/ppermute | solution.py:53
  62.4 13.0 %collective-permute-start.13 = (bf16[128,2176]{1,0:T(8,128)(2,1)S(1)}, bf16[128,2176]{1,0:T(8,128)(2,1)S(1)}, u32[]{:S(2)}, u32[]{:S(2)}) collective-permute-start(bf16[128,2176]{1,0:T(8,128)(2,1)S(1)} %collective-permute-done.8.refs_0_.refs_4_.refs_8_), channel_id=1, source_target_pairs={{0,1},{1,0},{2,3},{3,2},{4,5},{5,4},{6,7},{7,6},{8,9},{9,8},{10,11... | collective-permute-start | bytes 1671176 | tf_op jit(solution)/shard_map/cot/flip/ppermute | solution.py:49
  95.2 17.2 %collective-permute-start.14 = (bf16[144,2048]{1,0:T(8,128)(2,1)S(1)}, bf16[144,2048]{1,0:T(8,128)(2,1)S(1)}, u32[]{:S(2)}, u32[]{:S(2)}) collective-permute-start(bf16[144,2048]{1,0:T(8,128)(2,1)S(1)} %get-tuple-element.108), channel_id=1, source_target_pairs={{0,2},{2,0},{1,3},{3,1},{4,6},{6,4},{5,7},{7,5},{8,10},{10,8},{9,1... | collective-permute-start | bytes 1769480 | tf_op jit(solution)/shard_map/cot1/to_y/ppermute | solution.py:49
  95.8 16.7 %collective-permute-start.15 = (bf16[144,2048]{1,0:T(8,128)(2,1)S(1)}, bf16[144,2048]{1,0:T(8,128)(2,1)S(1)}, u32[]{:S(2)}, u32[]{:S(2)}) collective-permute-start(bf16[144,2048]{1,0:T(8,128)(2,1)S(1)} %get-tuple-element.109), channel_id=1, source_target_pairs={{0,4},{4,0},{1,5},{5,1},{2,6},{6,2},{3,7},{7,3},{8,12},{12,8},{9,1... | collective-permute-start | bytes 1769480 | tf_op jit(solution)/shard_map/cot1/to_x/ppermute | solution.py:49
  96.3 16.2 %collective-permute-start.17 = (bf16[128,2048]{1,0:T(8,128)(2,1)S(1)}, bf16[128,2048]{1,0:T(8,128)(2,1)S(1)}, u32[]{:S(2)}, u32[]{:S(2)}) collective-permute-start(bf16[128,2048]{1,0:T(8,128)(2,1)S(1)} %copy-done.20), channel_id=1, source_target_pairs={{0,8},{8,16},{16,24},{24,0},{1,9},{9,17},{17,25},{25,1},{2,10},{10... | collective-permute-start | bytes 1572872 | tf_op jit(solution)/shard_map/normed/hop/ppermute | solution.py:58
  98.8 26.8 %collective-permute-start.22 = (bf16[144,2048]{1,0:T(8,128)(2,1)S(1)}, bf16[144,2048]{1,0:T(8,128)(2,1)S(1)}, u32[]{:S(2)}, u32[]{:S(2)}) collective-permute-start(bf16[144,2048]{1,0:T(8,128)(2,1)S(1)} %get-tuple-element.116), channel_id=1, source_target_pairs={{0,6},{2,4},{4,2},{6,0},{1,7},{3,5},{5,3},{7,1},{8,14},{10,12},{12... | collective-permute-start | bytes 1769480 | tf_op jit(solution)/shard_map/cot1/to_xy/ppermute | solution.py:53
  101.2 13.2 %collective-permute-start.16 = (bf16[128,2048]{1,0:T(8,128)(2,1)S(1)}, bf16[128,2048]{1,0:T(8,128)(2,1)S(1)}, u32[]{:S(2)}, u32[]{:S(2)}) collective-permute-start(bf16[128,2048]{1,0:T(8,128)(2,1)S(1)} %copy-done.20), channel_id=1, source_target_pairs={{0,1},{1,0},{2,3},{3,2},{4,5},{5,4},{6,7},{7,6},{8,9},{9,8},{10,11... | collective-permute-start | bytes 1572872 | tf_op jit(solution)/shard_map/normed/flip/ppermute | solution.py:49
  112.5 16.2 %collective-permute-start.23 = (bf16[128,2048]{1,0:T(8,128)(2,1)S(1)}, bf16[128,2048]{1,0:T(8,128)(2,1)S(1)}, u32[]{:S(2)}, u32[]{:S(2)}) collective-permute-start(bf16[128,2048]{1,0:T(8,128)(2,1)S(1)} %collective-permute-done.17.refs_2_), channel_id=1, source_target_pairs={{0,8},{8,16},{16,24},{24,0},{1,9},{9,17},{17,25},{25,1},{2,10},{10... | collective-permute-start | bytes 1572872 | tf_op jit(solution)/shard_map/normed/hop/ppermute | solution.py:58
  117.6 26.3 %collective-permute-start.19 = (bf16[144,2048]{1,0:T(8,128)(2,1)S(1)}, bf16[144,2048]{1,0:T(8,128)(2,1)S(1)}, u32[]{:S(2)}, u32[]{:S(2)}) collective-permute-start(bf16[144,2048]{1,0:T(8,128)(2,1)S(1)} %get-tuple-element.113), channel_id=1, source_target_pairs={{0,2},{2,0},{1,3},{3,1},{4,6},{6,4},{5,7},{7,5},{8,10},{10,8},{9,1... | collective-permute-start | bytes 1769480 | tf_op jit(solution)/shard_map/normed0/to_y/ppermute | solution.py:49
  119.1 24.8 %collective-permute-start.20 = (bf16[144,2048]{1,0:T(8,128)(2,1)S(1)}, bf16[144,2048]{1,0:T(8,128)(2,1)S(1)}, u32[]{:S(2)}, u32[]{:S(2)}) collective-permute-start(bf16[144,2048]{1,0:T(8,128)(2,1)S(1)} %get-tuple-element.114), channel_id=1, source_target_pairs={{0,4},{4,0},{1,5},{5,1},{2,6},{6,2},{3,7},{7,3},{8,12},{12,8},{9,1... | collective-permute-start | bytes 1769480 | tf_op jit(solution)/shard_map/normed0/to_x/ppermute | solution.py:49
  128.7 15.2 %collective-permute-start.25 = (bf16[128,2048]{1,0:T(8,128)(2,1)S(1)}, bf16[128,2048]{1,0:T(8,128)(2,1)S(1)}, u32[]{:S(2)}, u32[]{:S(2)}) collective-permute-start(bf16[128,2048]{1,0:T(8,128)(2,1)S(1)} %collective-permute-done.23.refs_0_), channel_id=1, source_target_pairs={{0,8},{8,16},{16,24},{24,0},{1,9},{9,17},{17,25},{25,1},{2,10},{10... | collective-permute-start | bytes 1572872 | tf_op jit(solution)/shard_map/normed/hop/ppermute | solution.py:58
  128.7 21.1 %collective-permute-start.21 = (bf16[144,2048]{1,0:T(8,128)(2,1)S(1)}, bf16[144,2048]{1,0:T(8,128)(2,1)S(1)}, u32[]{:S(2)}, u32[]{:S(2)}) collective-permute-start(bf16[144,2048]{1,0:T(8,128)(2,1)S(1)} %get-tuple-element.115), channel_id=1, source_target_pairs={{0,6},{2,4},{4,2},{6,0},{1,7},{3,5},{5,3},{7,1},{8,14},{10,12},{12... | collective-permute-start | bytes 1769480 | tf_op jit(solution)/shard_map/normed0/to_xy/ppermute | solution.py:53
  143.9 5.9 %collective-permute-start.26 = (bf16[128,2048]{1,0:T(8,128)(2,1)S(1)}, bf16[128,2048]{1,0:T(8,128)(2,1)S(1)}, u32[]{:S(2)}, u32[]{:S(2)}) collective-permute-start(bf16[128,2048]{1,0:T(8,128)(2,1)S(1)} %collective-permute-done.25.refs_2_), channel_id=1, source_target_pairs={{0,1},{1,0},{2,3},{3,2},{4,5},{5,4},{6,7},{7,6},{8,9},{9,8},{10,11... | collective-permute-start | bytes 1572872 | tf_op jit(solution)/shard_map/normed/flip/ppermute | solution.py:49
  154.8 22.1 %collective-permute-start.27 = (bf16[144,2048]{1,0:T(8,128)(2,1)}, bf16[144,2048]{1,0:T(8,128)(2,1)}, u32[]{:S(2)}, u32[]{:S(2)}) collective-permute-start(bf16[144,2048]{1,0:T(8,128)(2,1)} %get-tuple-element.126), channel_id=1, source_target_pairs={{0,2},{2,0},{1,3},{3,1},{4,6},{6,4},{5,7},{7,5},{8,10},{10,8},{9,1... | collective-permute-start | bytes 1769480 | tf_op jit(solution)/shard_map/normed1/to_y/ppermute | solution.py:49
  155.3 24.1 %collective-permute-start.28 = (bf16[144,2048]{1,0:T(8,128)(2,1)}, bf16[144,2048]{1,0:T(8,128)(2,1)}, u32[]{:S(2)}, u32[]{:S(2)}) collective-permute-start(bf16[144,2048]{1,0:T(8,128)(2,1)} %get-tuple-element.127), channel_id=1, source_target_pairs={{0,4},{4,0},{1,5},{5,1},{2,6},{6,2},{3,7},{7,3},{8,12},{12,8},{9,1... | collective-permute-start | bytes 1769480 | tf_op jit(solution)/shard_map/normed1/to_x/ppermute | solution.py:49
  155.8 29.7 %collective-permute-start.29 = (bf16[144,2048]{1,0:T(8,128)(2,1)}, bf16[144,2048]{1,0:T(8,128)(2,1)}, u32[]{:S(2)}, u32[]{:S(2)}) collective-permute-start(bf16[144,2048]{1,0:T(8,128)(2,1)} %get-tuple-element.128), channel_id=1, source_target_pairs={{0,6},{2,4},{4,2},{6,0},{1,7},{3,5},{5,3},{7,1},{8,14},{10,12},{12... | collective-permute-start | bytes 1769480 | tf_op jit(solution)/shard_map/normed1/to_xy/ppermute | solution.py:53
  175.9 27.6 %collective-permute-start.30 = (bf16[144,2048]{1,0:T(8,128)(2,1)}, bf16[144,2048]{1,0:T(8,128)(2,1)}, u32[]{:S(2)}, u32[]{:S(2)}) collective-permute-start(bf16[144,2048]{1,0:T(8,128)(2,1)} %get-tuple-element.135), channel_id=1, source_target_pairs={{0,2},{2,0},{1,3},{3,1},{4,6},{6,4},{5,7},{7,5},{8,10},{10,8},{9,1... | collective-permute-start | bytes 1769480 | tf_op jit(solution)/shard_map/row0/to_y/ppermute | solution.py:49
  176.5 27.1 %collective-permute-start.31 = (bf16[144,2048]{1,0:T(8,128)(2,1)}, bf16[144,2048]{1,0:T(8,128)(2,1)}, u32[]{:S(2)}, u32[]{:S(2)}) collective-permute-start(bf16[144,2048]{1,0:T(8,128)(2,1)} %get-tuple-element.136), channel_id=1, source_target_pairs={{0,4},{4,0},{1,5},{5,1},{2,6},{6,2},{3,7},{7,3},{8,12},{12,8},{9,1... | collective-permute-start | bytes 1769480 | tf_op jit(solution)/shard_map/row0/to_x/ppermute | solution.py:49
  176.9 31.5 %collective-permute-start.32 = (bf16[144,2048]{1,0:T(8,128)(2,1)}, bf16[144,2048]{1,0:T(8,128)(2,1)}, u32[]{:S(2)}, u32[]{:S(2)}) collective-permute-start(bf16[144,2048]{1,0:T(8,128)(2,1)} %get-tuple-element.137), channel_id=1, source_target_pairs={{0,6},{2,4},{4,2},{6,0},{1,7},{3,5},{5,3},{7,1},{8,14},{10,12},{12... | collective-permute-start | bytes 1769480 | tf_op jit(solution)/shard_map/row0/to_xy/ppermute | solution.py:53
  214.9 19.9 %collective-permute-start.35 = (bf16[144,2048]{1,0:T(8,128)(2,1)S(1)}, bf16[144,2048]{1,0:T(8,128)(2,1)S(1)}, u32[]{:S(2)}, u32[]{:S(2)}) collective-permute-start(bf16[144,2048]{1,0:T(8,128)(2,1)S(1)} %copy-done.53), channel_id=1, source_target_pairs={{0,2},{2,0},{1,3},{3,1},{4,6},{6,4},{5,7},{7,5},{8,10},{10,8},{9,1... | collective-permute-start | bytes 1769480 | tf_op jit(solution)/shard_map/row1/to_y/ppermute | solution.py:49
  215.5 19.4 %collective-permute-start.36 = (bf16[144,2048]{1,0:T(8,128)(2,1)S(1)}, bf16[144,2048]{1,0:T(8,128)(2,1)S(1)}, u32[]{:S(2)}, u32[]{:S(2)}) collective-permute-start(bf16[144,2048]{1,0:T(8,128)(2,1)S(1)} %copy-done.52), channel_id=1, source_target_pairs={{0,4},{4,0},{1,5},{5,1},{2,6},{6,2},{3,7},{7,3},{8,12},{12,8},{9,1... | collective-permute-start | bytes 1769480 | tf_op jit(solution)/shard_map/row1/to_x/ppermute | solution.py:49
  216.1 28.4 %collective-permute-start.37 = (bf16[144,2048]{1,0:T(8,128)(2,1)S(1)}, bf16[144,2048]{1,0:T(8,128)(2,1)S(1)}, u32[]{:S(2)}, u32[]{:S(2)}) collective-permute-start(bf16[144,2048]{1,0:T(8,128)(2,1)S(1)} %copy-done.51), channel_id=1, source_target_pairs={{0,6},{2,4},{4,2},{6,0},{1,7},{3,5},{5,3},{7,1},{8,14},{10,12},{12... | collective-permute-start | bytes 1769480 | tf_op jit(solution)/shard_map/row1/to_xy/ppermute | solution.py:53
  218.6 16.2 %collective-permute-start.34 = (bf16[128,2048]{1,0:T(8,128)(2,1)S(1)}, bf16[128,2048]{1,0:T(8,128)(2,1)S(1)}, u32[]{:S(2)}, u32[]{:S(2)}) collective-permute-start(bf16[128,2048]{1,0:T(8,128)(2,1)S(1)} %add_convert_fusion.5), channel_id=1, source_target_pairs={{0,8},{8,16},{16,24},{24,0},{1,9},{9,17},{17,25},{25,1},{2,10},{10... | collective-permute-start | bytes 1572872 | tf_op jit(solution)/shard_map/row_hop/ppermute | solution.py:58
  251.8 16.8 %collective-permute-start.39 = (bf16[128,2048]{1,0:T(8,128)(2,1)S(1)}, bf16[128,2048]{1,0:T(8,128)(2,1)S(1)}, u32[]{:S(2)}, u32[]{:S(2)}) collective-permute-start(bf16[128,2048]{1,0:T(8,128)(2,1)S(1)} %add_convert_fusion.4), channel_id=1, source_target_pairs={{0,8},{8,16},{16,24},{24,0},{1,9},{9,17},{17,25},{25,1},{2,10},{10... | collective-permute-start | bytes 1572872 | tf_op jit(solution)/shard_map/row_hop/ppermute | solution.py:58
  254.3 29.8 %collective-permute-start.41 = (bf16[144,2048]{1,0:T(8,128)(2,1)S(1)}, bf16[144,2048]{1,0:T(8,128)(2,1)S(1)}, u32[]{:S(2)}, u32[]{:S(2)}) collective-permute-start(bf16[144,2048]{1,0:T(8,128)(2,1)S(1)} %copy-done.50), channel_id=1, source_target_pairs={{0,2},{2,0},{1,3},{3,1},{4,6},{6,4},{5,7},{7,5},{8,10},{10,8},{9,1... | collective-permute-start | bytes 1769480 | tf_op jit(solution)/shard_map/made1/to_y/ppermute | solution.py:49
  254.9 29.2 %collective-permute-start.42 = (bf16[144,2048]{1,0:T(8,128)(2,1)S(1)}, bf16[144,2048]{1,0:T(8,128)(2,1)S(1)}, u32[]{:S(2)}, u32[]{:S(2)}) collective-permute-start(bf16[144,2048]{1,0:T(8,128)(2,1)S(1)} %copy-done.49), channel_id=1, source_target_pairs={{0,4},{4,0},{1,5},{5,1},{2,6},{6,2},{3,7},{7,3},{8,12},{12,8},{9,1... | collective-permute-start | bytes 1769480 | tf_op jit(solution)/shard_map/made1/to_x/ppermute | solution.py:49
  255.4 29.6 %collective-permute-start.43 = (bf16[144,2048]{1,0:T(8,128)(2,1)S(1)}, bf16[144,2048]{1,0:T(8,128)(2,1)S(1)}, u32[]{:S(2)}, u32[]{:S(2)}) collective-permute-start(bf16[144,2048]{1,0:T(8,128)(2,1)S(1)} %copy-done.48), channel_id=1, source_target_pairs={{0,6},{2,4},{4,2},{6,0},{1,7},{3,5},{5,3},{7,1},{8,14},{10,12},{12... | collective-permute-start | bytes 1769480 | tf_op jit(solution)/shard_map/made1/to_xy/ppermute | solution.py:53
  268.8 15.3 %collective-permute-start.40 = (bf16[128,2048]{1,0:T(8,128)(2,1)S(1)}, bf16[128,2048]{1,0:T(8,128)(2,1)S(1)}, u32[]{:S(2)}, u32[]{:S(2)}) collective-permute-start(bf16[128,2048]{1,0:T(8,128)(2,1)S(1)} %add_convert_fusion.3), channel_id=1, source_target_pairs={{0,8},{8,16},{16,24},{24,0},{1,9},{9,17},{17,25},{25,1},{2,10},{10... | collective-permute-start | bytes 1572872 | tf_op jit(solution)/shard_map/row_hop/ppermute | solution.py:58
  292.2 33.6 %collective-permute-start.48 = (bf16[144,2048]{1,0:T(8,128)(2,1)}, bf16[144,2048]{1,0:T(8,128)(2,1)S(1)}, u32[]{:S(2)}, u32[]{:S(2)}) collective-permute-start(bf16[144,2048]{1,0:T(8,128)(2,1)} %get-tuple-element.176), channel_id=1, source_target_pairs={{0,2},{2,0},{1,3},{3,1},{4,6},{6,4},{5,7},{7,5},{8,10},{10,8},{9,1... | collective-permute-start | bytes 1769480 | tf_op jit(solution)/shard_map/made0/to_y/ppermute | solution.py:49
  292.8 33.9 %collective-permute-start.49 = (bf16[144,2048]{1,0:T(8,128)(2,1)}, bf16[144,2048]{1,0:T(8,128)(2,1)S(1)}, u32[]{:S(2)}, u32[]{:S(2)}) collective-permute-start(bf16[144,2048]{1,0:T(8,128)(2,1)} %get-tuple-element.177), channel_id=1, source_target_pairs={{0,4},{4,0},{1,5},{5,1},{2,6},{6,2},{3,7},{7,3},{8,12},{12,8},{9,1... | collective-permute-start | bytes 1769480 | tf_op jit(solution)/shard_map/made0/to_x/ppermute | solution.py:49
  293.3 34.2 %collective-permute-start.50 = (bf16[144,2048]{1,0:T(8,128)(2,1)}, bf16[144,2048]{1,0:T(8,128)(2,1)}, u32[]{:S(2)}, u32[]{:S(2)}) collective-permute-start(bf16[144,2048]{1,0:T(8,128)(2,1)} %get-tuple-element.178), channel_id=1, source_target_pairs={{0,6},{2,4},{4,2},{6,0},{1,7},{3,5},{5,3},{7,1},{8,14},{10,12},{12... | collective-permute-start | bytes 1769480 | tf_op jit(solution)/shard_map/made0/to_xy/ppermute | solution.py:53
  296.9 40.3 %collective-permute-start.45 = (bf16[128,2176]{1,0:T(8,128)(2,1)}, bf16[128,2176]{1,0:T(8,128)(2,1)}, u32[]{:S(2)}, u32[]{:S(2)}) collective-permute-start(bf16[128,2176]{1,0:T(8,128)(2,1)} %add_convert_fusion.2), channel_id=1, source_target_pairs={{0,24},{8,0},{16,8},{24,16},{1,25},{9,1},{17,9},{25,17},{2,26},{10... | collective-permute-start | bytes 1671176 | tf_op jit(solution)/shard_map/made_hop/ppermute | solution.py:73
  313.5 9.8 %collective-permute-start.46 = (bf16[256,512]{1,0:T(8,128)(2,1)}, bf16[256,512]{1,0:T(8,128)(2,1)S(1)}, u32[]{:S(2)}, u32[]{:S(2)}) collective-permute-start(bf16[256,512]{1,0:T(8,128)(2,1)} %get-tuple-element.167), channel_id=1, source_target_pairs={{8,0},{16,8},{24,16},{9,1},{17,9},{25,17},{10,2},{18,10},{26,18},{... | collective-permute-start | bytes 786440 | tf_op jit(solution)/shard_map/kv_back_hop/ppermute | solution.py:68
  324.4 16.2 %collective-permute-start.53 = (bf16[256,512]{1,0:T(8,128)(2,1)S(1)}, bf16[256,512]{1,0:T(8,128)(2,1)S(1)}, u32[]{:S(2)}, u32[]{:S(2)}) collective-permute-start(bf16[256,512]{1,0:T(8,128)(2,1)S(1)} %add_convert_fusion.7), channel_id=1, source_target_pairs={{8,0},{16,8},{24,16},{9,1},{17,9},{25,17},{10,2},{18,10},{26,18},{... | collective-permute-start | bytes 786440 | tf_op jit(solution)/shard_map/kv_back_hop/ppermute | solution.py:68
  337.1 23.7 %collective-permute-start.51 = (bf16[256,2176]{1,0:T(8,128)(2,1)S(1)}, bf16[256,2176]{1,0:T(8,128)(2,1)S(1)}, u32[]{:S(2)}, u32[]{:S(2)}) collective-permute-start(bf16[256,2176]{1,0:T(8,128)(2,1)S(1)} %get-tuple-element.180), channel_id=1, source_target_pairs={{0,1},{1,0},{2,3},{3,2},{4,5},{5,4},{6,7},{7,6},{8,9},{9,8},{10,11... | collective-permute-start | bytes 3342344 | tf_op jit(solution)/shard_map/made0/sum_flip/ppermute | solution.py:49
  338.5 22.3 %collective-permute-start.47 = (bf16[128,2176]{1,0:T(8,128)(2,1)S(1)}, bf16[128,2176]{1,0:T(8,128)(2,1)S(1)}, u32[]{:S(2)}, u32[]{:S(2)}) collective-permute-start(bf16[128,2176]{1,0:T(8,128)(2,1)S(1)} %add_convert_fusion.1), channel_id=1, source_target_pairs={{0,24},{8,0},{16,8},{24,16},{1,25},{9,1},{17,9},{25,17},{2,26},{10... | collective-permute-start | bytes 1671176 | tf_op jit(solution)/shard_map/made_hop/ppermute | solution.py:73
  340.7 19.4 %collective-permute-start.54 = (bf16[256,512]{1,0:T(8,128)(2,1)S(1)}, bf16[256,512]{1,0:T(8,128)(2,1)S(1)}, u32[]{:S(2)}, u32[]{:S(2)}) collective-permute-start(bf16[256,512]{1,0:T(8,128)(2,1)S(1)} %add_convert_fusion.6), channel_id=1, source_target_pairs={{8,0},{16,8},{24,16},{9,1},{17,9},{25,17},{10,2},{18,10},{26,18},{... | collective-permute-start | bytes 786440 | tf_op jit(solution)/shard_map/kv_back_hop/ppermute | solution.py:68
  362.0 14.3 %collective-permute-start.52 = (bf16[128,2176]{1,0:T(8,128)(2,1)}, bf16[128,2176]{1,0:T(8,128)(2,1)S(1)}, u32[]{:S(2)}, u32[]{:S(2)}) collective-permute-start(bf16[128,2176]{1,0:T(8,128)(2,1)} %add_convert_fusion), channel_id=1, source_target_pairs={{0,24},{8,0},{16,8},{24,16},{1,25},{9,1},{17,9},{25,17},{2,26},{10... | collective-permute-start | bytes 1671176 | tf_op jit(solution)/shard_map/made_hop/ppermute | solution.py:73
  (62 other events, 495.4 us)

commit v3 on v2

--- a/solution.py
+++ b/solution.py
@@ -16,14 +16,13 @@
 
 NEG = -1e30
 OPT = {
-    "att": lambda cot, blocks: cot[0][1:] + [blocks[-1][1], blocks[-2][1]],
+    "att": lambda cot, blocks: [cot[-1][0]],
     "hop": lambda step, flipped, kv, cot: {1: [flipped], 3: cot[0][1:3] + [kv[2]] if cot else []}.get(step, []),
     "flip": lambda step, kv: {1: [kv[1]], 3: kv[3:4]}.get(step, []),
     "ga": lambda kv: [],
     "nh": lambda cot, normed, step: {2: cot[1:3], 3: cot[3:] + normed[0][:1] if normed else []}.get(step, []),
     "nf": lambda normed, step: normed[0][1:3] if step == 2 else [],
     "nb": lambda normed: normed[:4],
-    "hb": lambda arrivals: [arrivals[0]],
     "ea": lambda normed: [],
     "eb": lambda rows: [],
     "row1": lambda backs: [],
@@ -697,6 +696,9 @@
         if index == 0:
             with jax.named_scope("cot0"):
                 cot_pieces.append(gather(metas[0], 0, True, *OPT["ga"](kv_blocks)))
+    for index in range(1, len(groups)):
+        with jax.named_scope("cot1"):
+            cot_pieces.append(gather(metas[index], index, True, cot_pieces[-1][0], cot_pieces[-1][3]))
     attended, hidden, normed, inverse, log_sum = attend_forward(
         after(ctx, *OPT["att"](cot_pieces, payload_blocks)),
         query_heads[0],
@@ -704,12 +706,6 @@
         gain,
         kv_blocks,
     )
-    order = inverse
-    for index in range(1, len(groups)):
-        with jax.named_scope("cot1"):
-            cot_pieces.append(gather(metas[index], index, True, order, *cot_pieces[-1][1:]))
-        order = cot_pieces[-1][0]
-
     normed_blocks = []
     normed_pieces = []
     earlier = cot_pieces[-1][:3]
@@ -799,36 +795,38 @@
         kv_blocks,
     )
     kv_total = kv_parts[-1]
-    arrivals = []
     kv_low = []
-    for step in reversed(range(planes - 1)):
+    for step in reversed(range(1, planes - 1)):
         with jax.named_scope("kv_back_hop"):
-            arrivals.append(line_down(kv_total.astype(BF16)))
-        kv_total = arrivals[-1].astype(F32) + kv_parts[step]
-        if step:
-            kv_total = kv_total.astype(BF16)
-            kv_low.append(kv_total)
-    with jax.named_scope("kv_back_flip"):
-        kv_flipped_total = flip_axis(kv_total[rows:].astype(BF16), "x")
-    kv_total = kv_total[:rows] + kv_flipped_total.astype(F32)
-    kv_total = kv_total.astype(BF16)
-    key_gradient = kv_total[:, :kv_width]
-    value_gradient = kv_total[:, kv_width:]
+            kv_total = line_down(kv_total)
+        kv_total = (kv_total.astype(F32) + kv_parts[step]).astype(BF16)
+        kv_low.append(kv_total)
 
     made_total = None
     for step in reversed(range(STEPS, planes)):
         part = term(made_sums[step // STEPS], step % STEPS)
         with jax.named_scope("made_hop"):
             if made_total is not None:
-                part = after(made_total, *OPT['hb'](arrivals)).astype(F32) + part
+                part = after(made_total, kv_low[0]).astype(F32) + part
             made_total = ring_down(part.astype(BF16))
     with jax.named_scope("made0"):
-        made_sums[0] = sums(made_backs[0], 0, True, kv_low[0])
+        made_sums[0] = sums(made_backs[0], 0, True, *kv_low, made_total)
     for step in reversed(range(STEPS)):
         moe_sum = made_total.astype(F32) + term(made_sums[0], step)
         if step:
+            moved = moe_sum.astype(BF16)
             with jax.named_scope("made_hop"):
-                made_total = ring_down(moe_sum.astype(BF16))
+                made_total = ring_down(moved)
+            with jax.named_scope("kv_back_hop"):
+                kv_total = line_down(kv_total)
+            kv_total = kv_total.astype(F32) + kv_parts[0]
+            with jax.named_scope("kv_back_flip"):
+                kv_flipped_total = flip_axis(
+                    after(kv_total[rows:].astype(BF16), made_total), "x"
+                )
+            kv_total = (kv_total[:rows] + kv_flipped_total.astype(F32)).astype(BF16)
+    key_gradient = kv_total[:, :kv_width]
+    value_gradient = kv_total[:, kv_width:]
     layer_out = (hidden.astype(F32) + moe_sum[:, :width]).astype(BF16)
 
     found = moe_sum[:, width:].reshape(rows, 4, experts)

time: 386 us -> 391 us (1.013)
  waiting for transfers between devices: 182 us -> 195 us
  starting transfers between devices: 69.9 us -> 61.6 us
    ppermute x3, waiting for transfers between devices: 26.4 us -> 42.2 us  [line_down(): return lax.ppermute(value, 'z', [(i + 1, i) for i in range(size - 1)])]
    ppermute x30, starting transfers between devices: 16.9 us -> 27.9 us  [flip_axis(): return lax.ppermute(value, name, [(0, 1), (1, 0)])]
    ppermute x8, starting transfers between devices: 17.7 us -> 7.81 us  [flip_xy(): return lax.ppermute(value, ('x', 'y'), [(i, 3 - i) for i in range(4)])]
    ppermute x3, waiting for transfers between devices: 9.07 us -> 0.01 us  [ring_down(): return lax.ppermute(value, 'z', [(i, (i - 1) % size) for i in range(size)])]
    ppermute x30, waiting for transfers between devices: 8.87 us -> 16 us  [flip_axis(): return lax.ppermute(value, name, [(0, 1), (1, 0)])]
    ppermute x9, starting transfers between devices: 16.4 us -> 9.64 us  [ring_up(): return lax.ppermute(value, 'z', [(i, (i + 1) % size) for i in range(size)])]
    ppermute x8, waiting for transfers between devices: 31.8 us -> 25.2 us  [flip_xy(): return lax.ppermute(value, ('x', 'y'), [(i, 3 - i) for i in range(4)])]
    ppermute x9, waiting for transfers between devices: 66.8 us -> 72.9 us  [ring_up(): return lax.ppermute(value, 'z', [(i, (i + 1) % size) for i in range(size)])]
  transfers between devices with their start and end apart: 56 -> 56, of which waited for: 23 -> 25; matrix products, arithmetic and copies ran while one was open for 2% -> 2% of each run, Pallas kernels for 16% -> 17%
where the time goes in v3:
time: 391 us; the launch traced here: 385 us
  waiting for transfers between devices  195 us (50%)
  Pallas kernels  103 us (26%)
  starting transfers between devices  61.6 us (16%)
  local copies, waits for them, and re-layouts  11.9 us (3%)
  other arithmetic  11.5 us (3%)
    ppermute x9, waiting for transfers between devices, ring_up(): return lax.ppermute(value, 'z', [(i, (i + 1) % size) for i in range(size)])  72.9 us
    ppermute x3, waiting for transfers between devices, line_down(): return lax.ppermute(value, 'z', [(i + 1, i) for i in range(size - 1)])  42.2 us
    ppermute x3, waiting for transfers between devices, line_up(): return lax.ppermute(value, 'z', [(i, i + 1) for i in range(size - 1)])  39.1 us
    pallas_call x2, Pallas kernels, run_expert(): pl.pallas_call(expert_kernel, in_specs=[anywhere] * 11, out_specs=[anywhe...  35.4 us
    ppermute x30, starting transfers between devices, flip_axis(): return lax.ppermute(value, name, [(0, 1), (1, 0)])  27.9 us
    ppermute x8, waiting for transfers between devices, flip_xy(): return lax.ppermute(value, ('x', 'y'), [(i, 3 - i) for i in range(4)])  25.2 us
    pallas_call x4, Pallas kernels, combine_rows(): pl.pallas_call(functools.partial(kernel, experts, capacity, blocks), grid...  24.4 us
    ppermute x30, waiting for transfers between devices, flip_axis(): return lax.ppermute(value, name, [(0, 1), (1, 0)])  16 us
  transfers between devices with their start and end apart: 56, of which 25 were waited for; matrix products, arithmetic and copies ran while one was open for 2% of the time, Pallas kernels for 17%

profile of v3, /device:TPU:0, one launch (start us, length us, event | category | flops | bytes accessed | tf_op | source)
XLA Modules:
  0.0 384.5 jit_solution(12439540058136069930)
XLA Ops:
  1.6 3.0 collective-permute-start.1
  8.1 1.8 collective-permute-start.2
  9.9 3.5 collective-permute-start.3
  13.5 13.0 %collective-permute-done.3.refs_1_.refs_11_ = bf16[256,512]{1,0:T(8,128)(2,1)S(1)} collective-permute-done((bf16[256,512]{1,0:T(8,128)(2,1)S(1)}, bf16[256,512]{1,0:T(8,128)(2,1)S(1)}, u32[]{:S(2)}, u32[]{:S(2)}) %collective-permute-start.3) | collective-permute-done | bytes 262176 | tf_op jit(solution)/shard_map/kv_hop/ppermute | solution.py:62
  26.6 1.8 collective-permute-done.4.refs_3_.refs_7_.refs_11_
  28.5 3.7 gather_weighted.2
  32.2 1.6 collective-permute-start.8
  35.3 2.5 collective-permute-start.6
  37.8 3.5 collective-permute-start.10
  41.3 13.8 %collective-permute-done.10.refs_2_.refs_12_ = bf16[256,512]{1,0:T(8,128)(2,1)S(1)} collective-permute-done((bf16[256,512]{1,0:T(8,128)(2,1)S(1)}, bf16[256,512]{1,0:T(8,128)(2,1)S(1)}, u32[]{:S(2)}, u32[]{:S(2)}) %collective-permute-start.10) | collective-permute-done | bytes 262176 | tf_op jit(solution)/shard_map/kv_hop/ppermute | solution.py:62
  55.1 2.5 collective-permute-start.11
  57.7 3.5 collective-permute-start.12
  61.7 12.3 %collective-permute-done.12.refs_3_.refs_13_ = bf16[256,512]{1,0:T(8,128)(2,1)S(1)} collective-permute-done((bf16[256,512]{1,0:T(8,128)(2,1)S(1)}, bf16[256,512]{1,0:T(8,128)(2,1)S(1)}, u32[]{:S(2)}, u32[]{:S(2)}) %collective-permute-start.12) | collective-permute-done | bytes 262176 | tf_op jit(solution)/shard_map/kv_hop/ppermute | solution.py:62
  76.7 4.4 %gather_weighted.3 = (bf16[144,2048]{1,0:T(8,128)(2,1)S(1)}, bf16[144,2048]{1,0:T(8,128)(2,1)}, bf16[144,2048]{1,0:T(8,128)(2,1)}, bf16[144,2048]{1,0:T(8,128)(2,1)S(1)}) custom-call(s32[4]{0:T(128)S(1)} %pad_add_fusion.1.names_ref, bf16[128,2176]{1,0:T(8,128)(2,1)S(1)} %collective-permute-done.6.refs_0_.refs_4_.refs_8_, ...), custom_call_target="tpu_custom_call" | custom-call | bytes 4000000 | tf_op jit(solution)/shard_map/cot1/gather_weighted/pallas_call | solution.py:202
  83.7 12.1 %attend_forward.1 = (bf16[128,2048]{1,0:T(8,128)(2,1)}, bf16[128,2048]{1,0:T(8,128)(2,1)}, bf16[128,2048]{1,0:T(8,128)(2,1)}, f32[128,1]{1,0:T(8,128)}, f32[16,128]{1,0:T(8,128)}) custom-call(s32[2]{0:T(128)} %pad_add_fusion.ctx_ref, bf16[128,2048]{1,0:T(8,128)(2,1)} %bitcast.52, bf16[128,2048]{1,0:T(8,128)(2,1)} %bitcast.54, f32[1,2048]{1,0:T(1,128)} %bitcast.60, ...), custom_call_target="tpu_custom_call" | custom-call | bytes 12000000 | tf_op jit(solution)/shard_map/attend_forward/pallas_call | solution.py:514
  95.9 2.5 collective-permute-start.17
  98.3 2.4 collective-permute-start.22
  100.8 11.4 %collective-permute-done.17.refs_2_ = bf16[128,2048]{1,0:T(8,128)(2,1)S(1)} collective-permute-done((bf16[128,2048]{1,0:T(8,128)(2,1)}, bf16[128,2048]{1,0:T(8,128)(2,1)S(1)}, u32[]{:S(2)}, u32[]{:S(2)}) %collective-permute-start.17) | collective-permute-done | bytes 524320 | tf_op jit(solution)/shard_map/normed/hop/ppermute | solution.py:57
  112.3 1.8 collective-permute-done.18.refs_3_
  115.2 3.0 gather_plain.2
  118.2 1.6 collective-permute-start.19
  121.3 7.1 %collective-permute-done.23.refs_0_ = bf16[128,2048]{1,0:T(8,128)(2,1)S(1)} collective-permute-done((bf16[128,2048]{1,0:T(8,128)(2,1)S(1)}, bf16[128,2048]{1,0:T(8,128)(2,1)S(1)}, u32[]{:S(2)}, u32[]{:S(2)}) %collective-permute-start.23) | collective-permute-done | bytes 524320 | tf_op jit(solution)/shard_map/normed/hop/ppermute | solution.py:57
  128.4 2.5 collective-permute-start.21
  130.8 12.8 %collective-permute-done.25.refs_2_ = bf16[128,2048]{1,0:T(8,128)(2,1)S(1)} collective-permute-done((bf16[128,2048]{1,0:T(8,128)(2,1)S(1)}, bf16[128,2048]{1,0:T(8,128)(2,1)S(1)}, u32[]{:S(2)}, u32[]{:S(2)}) %collective-permute-start.25) | collective-permute-done | bytes 524320 | tf_op jit(solution)/shard_map/normed/hop/ppermute | solution.py:57
  144.3 3.2 collective-permute-done.21.refs_3_
  147.5 4.1 %gather_plain.3 = (bf16[144,2048]{1,0:T(8,128)(2,1)S(1)}, bf16[144,2048]{1,0:T(8,128)(2,1)}, bf16[144,2048]{1,0:T(8,128)(2,1)}, bf16[144,2048]{1,0:T(8,128)(2,1)}) custom-call(s32[4]{0:T(128)S(1)} %pad_add_fusion.1.names_ref, bf16[128,2048]{1,0:T(8,128)(2,1)S(1)} %collective-permute-done.23.refs_0_, bf16[128,2048]{1,0:T(8,128)(2,1)S(1)} %collective-permute-done.24.refs_1_, ...), custom_call_target="tpu_custom_call" | custom-call | bytes 4000000 | tf_op jit(solution)/shard_map/normed1/gather_plain/pallas_call | solution.py:202
  156.0 17.6 %expert.2 = (bf16[144,2048]{1,0:T(8,128)(2,1)}, bf16[144,2048]{1,0:T(8,128)(2,1)}, bf16[144,2048]{1,0:T(8,128)(2,1)}, bf16[144,2048]{1,0:T(8,128)(2,1)}, bf16[14...) custom-call(bf16[144,2048]{1,0:T(8,128)(2,1)} %copy-done.9, ...), custom_call_target="tpu_custom_call" | custom-call | bytes 18000000 | tf_op jit(solution)/shard_map/expert/pallas_call | solution.py:290
  177.2 6.1 %collective-permute-done.29.refs_3_ = bf16[144,2048]{1,0:T(8,128)(2,1)} collective-permute-done((bf16[144,2048]{1,0:T(8,128)(2,1)}, bf16[144,2048]{1,0:T(8,128)(2,1)}, u32[]{:S(2)}, u32[]{:S(2)}) %collective-permute-start.29) | collective-permute-done | bytes 589856 | tf_op jit(solution)/shard_map/normed1/to_xy/ppermute | solution.py:52
  183.3 17.8 %expert.3 = (bf16[144,2048]{1,0:T(8,128)(2,1)}, bf16[144,2048]{1,0:T(8,128)(2,1)}, bf16[144,2048]{1,0:T(8,128)(2,1)}, bf16[144,2048]{1,0:T(8,128)(2,1)}, bf16[14...) custom-call(bf16[144,2048]{1,0:T(8,128)(2,1)} %copy-done.11, ...), custom_call_target="tpu_custom_call" | custom-call | bytes 18000000 | tf_op jit(solution)/shard_map/expert/pallas_call | solution.py:290
  201.1 5.1 %collective-permute-done.32.refs_3_ = bf16[144,2048]{1,0:T(8,128)(2,1)} collective-permute-done((bf16[144,2048]{1,0:T(8,128)(2,1)}, bf16[144,2048]{1,0:T(8,128)(2,1)}, u32[]{:S(2)}, u32[]{:S(2)}) %collective-permute-start.32) | collective-permute-done | bytes 589856 | tf_op jit(solution)/shard_map/row0/to_xy/ppermute | solution.py:52
  207.3 5.2 %combine_plain.2 = (f32[128,2048]{1,0:T(8,128)S(1)}, f32[128,2048]{1,0:T(8,128)S(1)}, bf16[256,2048]{1,0:T(8,128)(2,1)S(1)}) custom-call(s32[4]{0:T(128)S(1)} %pad_add_fusion.1.names_ref, bf16[144,2048]{1,0:T(8,128)(2,1)S(1)} %copy-done.12, bf16[144,2048]{1,0:T(8,128)(2,1)} %collective-permute-done.30.refs_1_, ...), custom_call_target="tpu_custom_call" | custom-call | bytes 8000000 | tf_op jit(solution)/shard_map/row0/combine_plain/pallas_call | solution.py:428
  216.4 15.2 %collective-permute-done.34 = bf16[128,2048]{1,0:T(8,128)(2,1)S(1)} collective-permute-done((bf16[128,2048]{1,0:T(8,128)(2,1)S(1)}, bf16[128,2048]{1,0:T(8,128)(2,1)S(1)}, u32[]{:S(2)}, u32[]{:S(2)}) %collective-permute-start.34) | collective-permute-done | bytes 524320 | tf_op jit(solution)/shard_map/row_hop/ppermute | solution.py:57
  231.6 10.6 %collective-permute-done.37.refs_3_ = bf16[144,2048]{1,0:T(8,128)(2,1)S(1)} collective-permute-done((bf16[144,2048]{1,0:T(8,128)(2,1)S(1)}, bf16[144,2048]{1,0:T(8,128)(2,1)S(1)}, u32[]{:S(2)}, u32[]{:S(2)}) %collective-permute-start.37) | collective-permute-done | bytes 589856 | tf_op jit(solution)/shard_map/row1/to_xy/ppermute | solution.py:52
  242.2 4.6 %combine_plain.3 = (f32[128,2048]{1,0:T(8,128)S(1)}, f32[128,2048]{1,0:T(8,128)S(1)}, bf16[256,2048]{1,0:T(8,128)(2,1)S(1)}) custom-call(s32[4]{0:T(128)S(1)} %pad_add_fusion.1.names_ref, bf16[144,2048]{1,0:T(8,128)(2,1)S(1)} %copy-done.10, bf16[144,2048]{1,0:T(8,128)(2,1)S(1)} %collective-permute-done.35.refs_1_, ...), custom_call_target="tpu_custom_call" | custom-call | bytes 8000000 | tf_op jit(solution)/shard_map/row1/combine_plain/pallas_call | solution.py:428
  246.9 2.6 collective-permute-done.38
  254.1 11.5 %collective-permute-done.39 = bf16[128,2048]{1,0:T(8,128)(2,1)S(1)} collective-permute-done((bf16[128,2048]{1,0:T(8,128)(2,1)S(1)}, bf16[128,2048]{1,0:T(8,128)(2,1)S(1)}, u32[]{:S(2)}, u32[]{:S(2)}) %collective-permute-start.39) | collective-permute-done | bytes 524320 | tf_op jit(solution)/shard_map/row_hop/ppermute | solution.py:57
  265.9 14.9 %collective-permute-done.40.refs_7_ = bf16[128,2048]{1,0:T(8,128)(2,1)S(1)} collective-permute-done((bf16[128,2048]{1,0:T(8,128)(2,1)S(1)}, bf16[128,2048]{1,0:T(8,128)(2,1)S(1)}, u32[]{:S(2)}, u32[]{:S(2)}) %collective-permute-start.40) | collective-permute-done | bytes 524320 | tf_op jit(solution)/shard_map/row_hop/ppermute | solution.py:57
  280.8 7.2 %combine_weighted.2 = (f32[128,2176]{1,0:T(8,128)S(1)}, f32[128,2176]{1,0:T(8,128)S(1)}, bf16[256,2176]{1,0:T(8,128)(2,1)S(1)}) custom-call(s32[4]{0:T(128)S(1)} %pad_add_fusion.1.names_ref, bf16[144,2048]{1,0:T(8,128)(2,1)S(1)} %copy-done.14, bf16[144,2048]{1,0:T(8,128)(2,1)S(1)} %collective-permute-done.41.refs_1_, ...), custom_call_target="tpu_custom_call" | custom-call | bytes 8000000 | tf_op jit(solution)/shard_map/made1/combine_weighted/pallas_call | solution.py:428
  288.1 2.7 collective-permute-done.44
  292.0 1.7 collective-permute-start.45
  293.8 15.2 %attend_backward.1 = (bf16[128,2048]{1,0:T(8,128)(2,1)}, bf16[128,2048]{1,0:T(8,128)(2,1)}, f32[256,512]{1,0:T(8,128)}, f32[256,512]{1,0:T(8,128)}, f32[256,512]{1,0:T(8,128)}, /*index=5*/bf16[256,512]{1,0:T(8,128)(2,1)}) custom-call(s32[2]{0:T(128)} %pad_add_fusion.ctx_ref, bf16[128,2048]{1,0:T(8,128)(2,1)} %bitcast.53, ...), custom_call_target="tpu_custom_call" | custom-call | bytes 15000000 | tf_op jit(solution)/shard_map/attend_backward/pallas_call | solution.py:605
  310.3 1.6 collective-permute-start.49
  313.9 5.3 %collective-permute-done.46 = bf16[256,512]{1,0:T(8,128)(2,1)S(1)} collective-permute-done((bf16[256,512]{1,0:T(8,128)(2,1)}, bf16[256,512]{1,0:T(8,128)(2,1)S(1)}, u32[]{:S(2)}, u32[]{:S(2)}) %collective-permute-start.46) | collective-permute-done | bytes 262176 | tf_op jit(solution)/shard_map/kv_back_hop/ppermute | solution.py:67
  323.2 17.7 %collective-permute-done.48 = bf16[256,512]{1,0:T(8,128)(2,1)S(1)} collective-permute-done((bf16[256,512]{1,0:T(8,128)(2,1)S(1)}, bf16[256,512]{1,0:T(8,128)(2,1)S(1)}, u32[]{:S(2)}, u32[]{:S(2)}) %collective-permute-start.48) | collective-permute-done | bytes 262176 | tf_op jit(solution)/shard_map/kv_back_hop/ppermute | solution.py:67
  341.6 7.4 %combine_weighted.3 = (f32[128,2176]{1,0:T(8,128)S(1)}, f32[128,2176]{1,0:T(8,128)S(1)}, bf16[256,2176]{1,0:T(8,128)(2,1)S(1)}) custom-call(s32[4]{0:T(128)S(1)} %pad_add_fusion.1.names_ref, bf16[144,2048]{1,0:T(8,128)(2,1)S(1)} %copy-done.13, bf16[144,2048]{1,0:T(8,128)(2,1)S(1)} %collective-permute-done.49.refs_1_, ...), custom_call_target="tpu_custom_call" | custom-call | bytes 8000000 | tf_op jit(solution)/shard_map/made0/combine_weighted/pallas_call | solution.py:428
  349.1 2.7 collective-permute-done.52
  354.3 19.2 %collective-permute-done.54 = bf16[256,512]{1,0:T(8,128)(2,1)S(1)} collective-permute-done((bf16[256,512]{1,0:T(8,128)(2,1)}, bf16[256,512]{1,0:T(8,128)(2,1)S(1)}, u32[]{:S(2)}, u32[]{:S(2)}) %collective-permute-start.54) | collective-permute-done | bytes 262176 | tf_op jit(solution)/shard_map/kv_back_hop/ppermute | solution.py:67
  380.8 2.8 collective-permute-done.55
  (200 shorter events, 52.5 us)
Async XLA Ops:
  1.6 6.5 %collective-permute-start.1 = (bf16[128,512]{1,0:T(8,128)(2,1)S(1)}, bf16[128,512]{1,0:T(8,128)(2,1)S(1)}, u32[]{:S(2)}, u32[]{:S(2)}) collective-permute-start(bf16[128,512]{1,0:T(8,128)(2,1)S(1)} %pad_maximum_fusion.1), channel_id=1, source_target_pairs={{0,4},{4,0},{1,5},{5,1},{2,6},{6,2},{3,7},{7,3},{8,12},{12,8},{9,1... | collective-permute-start | bytes 393224 | tf_op jit(solution)/shard_map/kv_flip/ppermute | solution.py:48
  8.1 18.5 %collective-permute-start.2 = (bf16[128,2176]{1,0:T(8,128)(2,1)S(1)}, bf16[128,2176]{1,0:T(8,128)(2,1)S(1)}, u32[]{:S(2)}, u32[]{:S(2)}) collective-permute-start(bf16[128,2176]{1,0:T(8,128)(2,1)S(1)} %routing.1.refs_0_.refs_4_.refs_8_), channel_id=1, source_target_pairs={{0,8},{8,16},{16,24},{24,0},{1,9},{9,17},{17,25},{25,1},{2,10},{10... | collective-permute-start | bytes 1671176 | tf_op jit(solution)/shard_map/cot/hop/ppermute | solution.py:57
  9.9 16.6 %collective-permute-start.3 = (bf16[256,512]{1,0:T(8,128)(2,1)S(1)}, bf16[256,512]{1,0:T(8,128)(2,1)S(1)}, u32[]{:S(2)}, u32[]{:S(2)}) collective-permute-start(bf16[256,512]{1,0:T(8,128)(2,1)S(1)} %pad_maximum_fusion.refs_0_.refs_10_), channel_id=1, source_target_pairs={{0,8},{8,16},{16,24},{1,9},{9,17},{17,25},{2,10},{10,18},{18,26},{... | collective-permute-start | bytes 786440 | tf_op jit(solution)/shard_map/kv_hop/ppermute | solution.py:62
  13.4 13.2 %collective-permute-start = (bf16[128,2176]{1,0:T(8,128)(2,1)S(1)}, bf16[128,2176]{1,0:T(8,128)(2,1)S(1)}, u32[]{:S(2)}, u32[]{:S(2)}) collective-permute-start(bf16[128,2176]{1,0:T(8,128)(2,1)S(1)} %routing.1.refs_0_.refs_4_.refs_8_), channel_id=1, source_target_pairs={{0,1},{1,0},{2,3},{3,2},{4,5},{5,4},{6,7},{7,6},{8,9},{9,8},{10,11... | collective-permute-start | bytes 1671176 | tf_op jit(solution)/shard_map/cot/flip/ppermute | solution.py:48
  32.2 22.9 %collective-permute-start.8 = (bf16[144,2048]{1,0:T(8,128)(2,1)S(1)}, bf16[144,2048]{1,0:T(8,128)(2,1)S(1)}, u32[]{:S(2)}, u32[]{:S(2)}) collective-permute-start(bf16[144,2048]{1,0:T(8,128)(2,1)S(1)} %get-tuple-element.102), channel_id=1, source_target_pairs={{0,2},{2,0},{1,3},{3,1},{4,6},{6,4},{5,7},{7,5},{8,10},{10,8},{9,1... | collective-permute-start | bytes 1769480 | tf_op jit(solution)/shard_map/cot0/to_y/ppermute | solution.py:48
  33.8 21.3 %collective-permute-start.9 = (bf16[144,2048]{1,0:T(8,128)(2,1)S(1)}, bf16[144,2048]{1,0:T(8,128)(2,1)S(1)}, u32[]{:S(2)}, u32[]{:S(2)}) collective-permute-start(bf16[144,2048]{1,0:T(8,128)(2,1)S(1)} %get-tuple-element.103), channel_id=1, source_target_pairs={{0,4},{4,0},{1,5},{5,1},{2,6},{6,2},{3,7},{7,3},{8,12},{12,8},{9,1... | collective-permute-start | bytes 1769480 | tf_op jit(solution)/shard_map/cot0/to_x/ppermute | solution.py:48
  35.3 19.8 %collective-permute-start.6 = (bf16[128,2176]{1,0:T(8,128)(2,1)S(1)}, bf16[128,2176]{1,0:T(8,128)(2,1)S(1)}, u32[]{:S(2)}, u32[]{:S(2)}) collective-permute-start(bf16[128,2176]{1,0:T(8,128)(2,1)S(1)} %collective-permute-done.2.refs_2_.refs_6_.refs_10_), channel_id=1, source_target_pairs={{0,8},{8,16},{16,24},{24,0},{1,9},{9,17},{17,25},{25,1},{2,10},{10... | collective-permute-start | bytes 1671176 | tf_op jit(solution)/shard_map/cot/hop/ppermute | solution.py:57
  37.8 17.2 %collective-permute-start.10 = (bf16[256,512]{1,0:T(8,128)(2,1)S(1)}, bf16[256,512]{1,0:T(8,128)(2,1)S(1)}, u32[]{:S(2)}, u32[]{:S(2)}) collective-permute-start(bf16[256,512]{1,0:T(8,128)(2,1)S(1)} %collective-permute-done.3.refs_1_.refs_11_), channel_id=1, source_target_pairs={{0,8},{8,16},{16,24},{1,9},{9,17},{17,25},{2,10},{10,18},{18,26},{... | collective-permute-start | bytes 786440 | tf_op jit(solution)/shard_map/kv_hop/ppermute | solution.py:62
  55.1 19.6 %collective-permute-start.11 = (bf16[128,2176]{1,0:T(8,128)(2,1)S(1)}, bf16[128,2176]{1,0:T(8,128)(2,1)S(1)}, u32[]{:S(2)}, u32[]{:S(2)}) collective-permute-start(bf16[128,2176]{1,0:T(8,128)(2,1)S(1)} %collective-permute-done.6.refs_0_.refs_4_.refs_8_), channel_id=1, source_target_pairs={{0,8},{8,16},{16,24},{24,0},{1,9},{9,17},{17,25},{25,1},{2,10},{10... | collective-permute-start | bytes 1671176 | tf_op jit(solution)/shard_map/cot/hop/ppermute | solution.py:57
  57.7 16.3 %collective-permute-start.12 = (bf16[256,512]{1,0:T(8,128)(2,1)S(1)}, bf16[256,512]{1,0:T(8,128)(2,1)S(1)}, u32[]{:S(2)}, u32[]{:S(2)}) collective-permute-start(bf16[256,512]{1,0:T(8,128)(2,1)S(1)} %collective-permute-done.10.refs_2_.refs_12_), channel_id=1, source_target_pairs={{0,8},{8,16},{16,24},{1,9},{9,17},{17,25},{2,10},{10,18},{18,26},{... | collective-permute-start | bytes 786440 | tf_op jit(solution)/shard_map/kv_hop/ppermute | solution.py:62
  61.2 14.3 %collective-permute-start.5 = (bf16[144,2048]{1,0:T(8,128)(2,1)S(1)}, bf16[144,2048]{1,0:T(8,128)(2,1)S(1)}, u32[]{:S(2)}, u32[]{:S(2)}) collective-permute-start(bf16[144,2048]{1,0:T(8,128)(2,1)S(1)} %get-tuple-element.100), channel_id=1, source_target_pairs={{0,6},{2,4},{4,2},{6,0},{1,7},{3,5},{5,3},{7,1},{8,14},{10,12},{12... | collective-permute-start | bytes 1769480 | tf_op jit(solution)/shard_map/cot0/to_xy/ppermute | solution.py:52
  61.7 13.8 %collective-permute-start.7 = (bf16[128,2176]{1,0:T(8,128)(2,1)S(1)}, bf16[128,2176]{1,0:T(8,128)(2,1)S(1)}, u32[]{:S(2)}, u32[]{:S(2)}) collective-permute-start(bf16[128,2176]{1,0:T(8,128)(2,1)S(1)} %collective-permute-done.6.refs_0_.refs_4_.refs_8_), channel_id=1, source_target_pairs={{0,1},{1,0},{2,3},{3,2},{4,5},{5,4},{6,7},{7,6},{8,9},{9,8},{10,11... | collective-permute-start | bytes 1671176 | tf_op jit(solution)/shard_map/cot/flip/ppermute | solution.py:48
  82.7 29.6 %collective-permute-start.14 = (bf16[144,2048]{1,0:T(8,128)(2,1)}, bf16[144,2048]{1,0:T(8,128)(2,1)}, u32[]{:S(2)}, u32[]{:S(2)}) collective-permute-start(bf16[144,2048]{1,0:T(8,128)(2,1)} %get-tuple-element.109), channel_id=1, source_target_pairs={{0,2},{2,0},{1,3},{3,1},{4,6},{6,4},{5,7},{7,5},{8,10},{10,8},{9,1... | collective-permute-start | bytes 1769480 | tf_op jit(solution)/shard_map/cot1/to_y/ppermute | solution.py:48
  83.2 29.0 %collective-permute-start.15 = (bf16[144,2048]{1,0:T(8,128)(2,1)}, bf16[144,2048]{1,0:T(8,128)(2,1)}, u32[]{:S(2)}, u32[]{:S(2)}) collective-permute-start(bf16[144,2048]{1,0:T(8,128)(2,1)} %get-tuple-element.110), channel_id=1, source_target_pairs={{0,4},{4,0},{1,5},{5,1},{2,6},{6,2},{3,7},{7,3},{8,12},{12,8},{9,1... | collective-permute-start | bytes 1769480 | tf_op jit(solution)/shard_map/cot1/to_x/ppermute | solution.py:48
  95.9 16.4 %collective-permute-start.17 = (bf16[128,2048]{1,0:T(8,128)(2,1)}, bf16[128,2048]{1,0:T(8,128)(2,1)S(1)}, u32[]{:S(2)}, u32[]{:S(2)}) collective-permute-start(bf16[128,2048]{1,0:T(8,128)(2,1)} %get-tuple-element.112.refs_0_), channel_id=1, source_target_pairs={{0,8},{8,16},{16,24},{24,0},{1,9},{9,17},{17,25},{25,1},{2,10},{10... | collective-permute-start | bytes 1572872 | tf_op jit(solution)/shard_map/normed/hop/ppermute | solution.py:57
  98.3 23.0 %collective-permute-start.22 = (bf16[144,2048]{1,0:T(8,128)(2,1)}, bf16[144,2048]{1,0:T(8,128)(2,1)S(1)}, u32[]{:S(2)}, u32[]{:S(2)}) collective-permute-start(bf16[144,2048]{1,0:T(8,128)(2,1)} %copy-done.20), channel_id=1, source_target_pairs={{0,6},{2,4},{4,2},{6,0},{1,7},{3,5},{5,3},{7,1},{8,14},{10,12},{12... | collective-permute-start | bytes 1769480 | tf_op jit(solution)/shard_map/cot1/to_xy/ppermute | solution.py:52
  100.8 11.5 %collective-permute-start.16 = (bf16[128,2048]{1,0:T(8,128)(2,1)}, bf16[128,2048]{1,0:T(8,128)(2,1)S(1)}, u32[]{:S(2)}, u32[]{:S(2)}) collective-permute-start(bf16[128,2048]{1,0:T(8,128)(2,1)} %get-tuple-element.112.refs_0_), channel_id=1, source_target_pairs={{0,1},{1,0},{2,3},{3,2},{4,5},{5,4},{6,7},{7,6},{8,9},{9,8},{10,11... | collective-permute-start | bytes 1572872 | tf_op jit(solution)/shard_map/normed/flip/ppermute | solution.py:48
  112.3 16.1 %collective-permute-start.23 = (bf16[128,2048]{1,0:T(8,128)(2,1)S(1)}, bf16[128,2048]{1,0:T(8,128)(2,1)S(1)}, u32[]{:S(2)}, u32[]{:S(2)}) collective-permute-start(bf16[128,2048]{1,0:T(8,128)(2,1)S(1)} %collective-permute-done.17.refs_2_), channel_id=1, source_target_pairs={{0,8},{8,16},{16,24},{24,0},{1,9},{9,17},{17,25},{25,1},{2,10},{10... | collective-permute-start | bytes 1572872 | tf_op jit(solution)/shard_map/normed/hop/ppermute | solution.py:57
  118.2 25.4 %collective-permute-start.19 = (bf16[144,2048]{1,0:T(8,128)(2,1)S(1)}, bf16[144,2048]{1,0:T(8,128)(2,1)S(1)}, u32[]{:S(2)}, u32[]{:S(2)}) collective-permute-start(bf16[144,2048]{1,0:T(8,128)(2,1)S(1)} %get-tuple-element.114), channel_id=1, source_target_pairs={{0,2},{2,0},{1,3},{3,1},{4,6},{6,4},{5,7},{7,5},{8,10},{10,8},{9,1... | collective-permute-start | bytes 1769480 | tf_op jit(solution)/shard_map/normed0/to_y/ppermute | solution.py:48
  119.8 23.9 %collective-permute-start.20 = (bf16[144,2048]{1,0:T(8,128)(2,1)S(1)}, bf16[144,2048]{1,0:T(8,128)(2,1)S(1)}, u32[]{:S(2)}, u32[]{:S(2)}) collective-permute-start(bf16[144,2048]{1,0:T(8,128)(2,1)S(1)} %get-tuple-element.115), channel_id=1, source_target_pairs={{0,4},{4,0},{1,5},{5,1},{2,6},{6,2},{3,7},{7,3},{8,12},{12,8},{9,1... | collective-permute-start | bytes 1769480 | tf_op jit(solution)/shard_map/normed0/to_x/ppermute | solution.py:48
  128.4 15.3 %collective-permute-start.25 = (bf16[128,2048]{1,0:T(8,128)(2,1)S(1)}, bf16[128,2048]{1,0:T(8,128)(2,1)S(1)}, u32[]{:S(2)}, u32[]{:S(2)}) collective-permute-start(bf16[128,2048]{1,0:T(8,128)(2,1)S(1)} %collective-permute-done.23.refs_0_), channel_id=1, source_target_pairs={{0,8},{8,16},{16,24},{24,0},{1,9},{9,17},{17,25},{25,1},{2,10},{10... | collective-permute-start | bytes 1572872 | tf_op jit(solution)/shard_map/normed/hop/ppermute | solution.py:57
  128.4 19.1 %collective-permute-start.21 = (bf16[144,2048]{1,0:T(8,128)(2,1)S(1)}, bf16[144,2048]{1,0:T(8,128)(2,1)S(1)}, u32[]{:S(2)}, u32[]{:S(2)}) collective-permute-start(bf16[144,2048]{1,0:T(8,128)(2,1)S(1)} %get-tuple-element.116), channel_id=1, source_target_pairs={{0,6},{2,4},{4,2},{6,0},{1,7},{3,5},{5,3},{7,1},{8,14},{10,12},{12... | collective-permute-start | bytes 1769480 | tf_op jit(solution)/shard_map/normed0/to_xy/ppermute | solution.py:52
  143.7 3.8 collective-permute-start.26
  152.5 24.2 %collective-permute-start.27 = (bf16[144,2048]{1,0:T(8,128)(2,1)}, bf16[144,2048]{1,0:T(8,128)(2,1)}, u32[]{:S(2)}, u32[]{:S(2)}) collective-permute-start(bf16[144,2048]{1,0:T(8,128)(2,1)} %get-tuple-element.126), channel_id=1, source_target_pairs={{0,2},{2,0},{1,3},{3,1},{4,6},{6,4},{5,7},{7,5},{8,10},{10,8},{9,1... | collective-permute-start | bytes 1769480 | tf_op jit(solution)/shard_map/normed1/to_y/ppermute | solution.py:48
  154.1 23.1 %collective-permute-start.28 = (bf16[144,2048]{1,0:T(8,128)(2,1)}, bf16[144,2048]{1,0:T(8,128)(2,1)}, u32[]{:S(2)}, u32[]{:S(2)}) collective-permute-start(bf16[144,2048]{1,0:T(8,128)(2,1)} %get-tuple-element.127), channel_id=1, source_target_pairs={{0,4},{4,0},{1,5},{5,1},{2,6},{6,2},{3,7},{7,3},{8,12},{12,8},{9,1... | collective-permute-start | bytes 1769480 | tf_op jit(solution)/shard_map/normed1/to_x/ppermute | solution.py:48
  155.6 27.7 %collective-permute-start.29 = (bf16[144,2048]{1,0:T(8,128)(2,1)}, bf16[144,2048]{1,0:T(8,128)(2,1)}, u32[]{:S(2)}, u32[]{:S(2)}) collective-permute-start(bf16[144,2048]{1,0:T(8,128)(2,1)} %get-tuple-element.128), channel_id=1, source_target_pairs={{0,6},{2,4},{4,2},{6,0},{1,7},{3,5},{5,3},{7,1},{8,14},{10,12},{12... | collective-permute-start | bytes 1769480 | tf_op jit(solution)/shard_map/normed1/to_xy/ppermute | solution.py:52
  173.6 27.5 %collective-permute-start.30 = (bf16[144,2048]{1,0:T(8,128)(2,1)}, bf16[144,2048]{1,0:T(8,128)(2,1)}, u32[]{:S(2)}, u32[]{:S(2)}) collective-permute-start(bf16[144,2048]{1,0:T(8,128)(2,1)} %get-tuple-element.135), channel_id=1, source_target_pairs={{0,2},{2,0},{1,3},{3,1},{4,6},{6,4},{5,7},{7,5},{8,10},{10,8},{9,1... | collective-permute-start | bytes 1769480 | tf_op jit(solution)/shard_map/row0/to_y/ppermute | solution.py:48
  175.2 25.9 %collective-permute-start.31 = (bf16[144,2048]{1,0:T(8,128)(2,1)}, bf16[144,2048]{1,0:T(8,128)(2,1)}, u32[]{:S(2)}, u32[]{:S(2)}) collective-permute-start(bf16[144,2048]{1,0:T(8,128)(2,1)} %get-tuple-element.136), channel_id=1, source_target_pairs={{0,4},{4,0},{1,5},{5,1},{2,6},{6,2},{3,7},{7,3},{8,12},{12,8},{9,1... | collective-permute-start | bytes 1769480 | tf_op jit(solution)/shard_map/row0/to_x/ppermute | solution.py:48
  176.7 29.5 %collective-permute-start.32 = (bf16[144,2048]{1,0:T(8,128)(2,1)}, bf16[144,2048]{1,0:T(8,128)(2,1)}, u32[]{:S(2)}, u32[]{:S(2)}) collective-permute-start(bf16[144,2048]{1,0:T(8,128)(2,1)} %get-tuple-element.137), channel_id=1, source_target_pairs={{0,6},{2,4},{4,2},{6,0},{1,7},{3,5},{5,3},{7,1},{8,14},{10,12},{12... | collective-permute-start | bytes 1769480 | tf_op jit(solution)/shard_map/row0/to_xy/ppermute | solution.py:52
  212.7 19.0 %collective-permute-start.35 = (bf16[144,2048]{1,0:T(8,128)(2,1)S(1)}, bf16[144,2048]{1,0:T(8,128)(2,1)S(1)}, u32[]{:S(2)}, u32[]{:S(2)}) collective-permute-start(bf16[144,2048]{1,0:T(8,128)(2,1)S(1)} %copy-done.48), channel_id=1, source_target_pairs={{0,2},{2,0},{1,3},{3,1},{4,6},{6,4},{5,7},{7,5},{8,10},{10,8},{9,1... | collective-permute-start | bytes 1769480 | tf_op jit(solution)/shard_map/row1/to_y/ppermute | solution.py:48
  214.2 17.4 %collective-permute-start.36 = (bf16[144,2048]{1,0:T(8,128)(2,1)S(1)}, bf16[144,2048]{1,0:T(8,128)(2,1)S(1)}, u32[]{:S(2)}, u32[]{:S(2)}) collective-permute-start(bf16[144,2048]{1,0:T(8,128)(2,1)S(1)} %copy-done.47), channel_id=1, source_target_pairs={{0,4},{4,0},{1,5},{5,1},{2,6},{6,2},{3,7},{7,3},{8,12},{12,8},{9,1... | collective-permute-start | bytes 1769480 | tf_op jit(solution)/shard_map/row1/to_x/ppermute | solution.py:48
  215.7 26.5 %collective-permute-start.37 = (bf16[144,2048]{1,0:T(8,128)(2,1)S(1)}, bf16[144,2048]{1,0:T(8,128)(2,1)S(1)}, u32[]{:S(2)}, u32[]{:S(2)}) collective-permute-start(bf16[144,2048]{1,0:T(8,128)(2,1)S(1)} %copy-done.46), channel_id=1, source_target_pairs={{0,6},{2,4},{4,2},{6,0},{1,7},{3,5},{5,3},{7,1},{8,14},{10,12},{12... | collective-permute-start | bytes 1769480 | tf_op jit(solution)/shard_map/row1/to_xy/ppermute | solution.py:52
  216.3 15.3 %collective-permute-start.34 = (bf16[128,2048]{1,0:T(8,128)(2,1)S(1)}, bf16[128,2048]{1,0:T(8,128)(2,1)S(1)}, u32[]{:S(2)}, u32[]{:S(2)}) collective-permute-start(bf16[128,2048]{1,0:T(8,128)(2,1)S(1)} %add_convert_fusion.5), channel_id=1, source_target_pairs={{0,8},{8,16},{16,24},{24,0},{1,9},{9,17},{17,25},{25,1},{2,10},{10... | collective-permute-start | bytes 1572872 | tf_op jit(solution)/shard_map/row_hop/ppermute | solution.py:57
  249.8 15.8 %collective-permute-start.39 = (bf16[128,2048]{1,0:T(8,128)(2,1)S(1)}, bf16[128,2048]{1,0:T(8,128)(2,1)S(1)}, u32[]{:S(2)}, u32[]{:S(2)}) collective-permute-start(bf16[128,2048]{1,0:T(8,128)(2,1)S(1)} %add_convert_fusion.4), channel_id=1, source_target_pairs={{0,8},{8,16},{16,24},{24,0},{1,9},{9,17},{17,25},{25,1},{2,10},{10... | collective-permute-start | bytes 1572872 | tf_op jit(solution)/shard_map/row_hop/ppermute | solution.py:57
  250.6 30.1 %collective-permute-start.41 = (bf16[144,2048]{1,0:T(8,128)(2,1)S(1)}, bf16[144,2048]{1,0:T(8,128)(2,1)S(1)}, u32[]{:S(2)}, u32[]{:S(2)}) collective-permute-start(bf16[144,2048]{1,0:T(8,128)(2,1)S(1)} %copy-done.45), channel_id=1, source_target_pairs={{0,2},{2,0},{1,3},{3,1},{4,6},{6,4},{5,7},{7,5},{8,10},{10,8},{9,1... | collective-permute-start | bytes 1769480 | tf_op jit(solution)/shard_map/made1/to_y/ppermute | solution.py:48
  252.2 28.6 %collective-permute-start.42 = (bf16[144,2048]{1,0:T(8,128)(2,1)S(1)}, bf16[144,2048]{1,0:T(8,128)(2,1)S(1)}, u32[]{:S(2)}, u32[]{:S(2)}) collective-permute-start(bf16[144,2048]{1,0:T(8,128)(2,1)S(1)} %copy-done.44), channel_id=1, source_target_pairs={{0,4},{4,0},{1,5},{5,1},{2,6},{6,2},{3,7},{7,3},{8,12},{12,8},{9,1... | collective-permute-start | bytes 1769480 | tf_op jit(solution)/shard_map/made1/to_x/ppermute | solution.py:48
  253.7 27.1 %collective-permute-start.43 = (bf16[144,2048]{1,0:T(8,128)(2,1)S(1)}, bf16[144,2048]{1,0:T(8,128)(2,1)S(1)}, u32[]{:S(2)}, u32[]{:S(2)}) collective-permute-start(bf16[144,2048]{1,0:T(8,128)(2,1)S(1)} %copy-done.43), channel_id=1, source_target_pairs={{0,6},{2,4},{4,2},{6,0},{1,7},{3,5},{5,3},{7,1},{8,14},{10,12},{12... | collective-permute-start | bytes 1769480 | tf_op jit(solution)/shard_map/made1/to_xy/ppermute | solution.py:52
  265.8 15.0 %collective-permute-start.40 = (bf16[128,2048]{1,0:T(8,128)(2,1)S(1)}, bf16[128,2048]{1,0:T(8,128)(2,1)S(1)}, u32[]{:S(2)}, u32[]{:S(2)}) collective-permute-start(bf16[128,2048]{1,0:T(8,128)(2,1)S(1)} %add_convert_fusion.3), channel_id=1, source_target_pairs={{0,8},{8,16},{16,24},{24,0},{1,9},{9,17},{17,25},{25,1},{2,10},{10... | collective-permute-start | bytes 1572872 | tf_op jit(solution)/shard_map/row_hop/ppermute | solution.py:57
  292.0 28.3 %collective-permute-start.45 = (bf16[128,2176]{1,0:T(8,128)(2,1)}, bf16[128,2176]{1,0:T(8,128)(2,1)S(1)}, u32[]{:S(2)}, u32[]{:S(2)}) collective-permute-start(bf16[128,2176]{1,0:T(8,128)(2,1)} %add_convert_fusion.2), channel_id=1, source_target_pairs={{0,24},{8,0},{16,8},{24,16},{1,25},{9,1},{17,9},{25,17},{2,26},{10... | collective-permute-start | bytes 1671176 | tf_op jit(solution)/shard_map/made_hop/ppermute | solution.py:72
  309.0 10.2 %collective-permute-start.46 = (bf16[256,512]{1,0:T(8,128)(2,1)}, bf16[256,512]{1,0:T(8,128)(2,1)S(1)}, u32[]{:S(2)}, u32[]{:S(2)}) collective-permute-start(bf16[256,512]{1,0:T(8,128)(2,1)} %get-tuple-element.168), channel_id=1, source_target_pairs={{8,0},{16,8},{24,16},{9,1},{17,9},{25,17},{10,2},{18,10},{26,18},{... | collective-permute-start | bytes 786440 | tf_op jit(solution)/shard_map/kv_back_hop/ppermute | solution.py:67
  310.3 31.3 %collective-permute-start.49 = (bf16[144,2048]{1,0:T(8,128)(2,1)}, bf16[144,2048]{1,0:T(8,128)(2,1)S(1)}, u32[]{:S(2)}, u32[]{:S(2)}) collective-permute-start(bf16[144,2048]{1,0:T(8,128)(2,1)} %get-tuple-element.178), channel_id=1, source_target_pairs={{0,2},{2,0},{1,3},{3,1},{4,6},{6,4},{5,7},{7,5},{8,10},{10,8},{9,1... | collective-permute-start | bytes 1769480 | tf_op jit(solution)/shard_map/made0/to_y/ppermute | solution.py:48
  311.9 29.7 %collective-permute-start.50 = (bf16[144,2048]{1,0:T(8,128)(2,1)}, bf16[144,2048]{1,0:T(8,128)(2,1)S(1)}, u32[]{:S(2)}, u32[]{:S(2)}) collective-permute-start(bf16[144,2048]{1,0:T(8,128)(2,1)} %get-tuple-element.179), channel_id=1, source_target_pairs={{0,4},{4,0},{1,5},{5,1},{2,6},{6,2},{3,7},{7,3},{8,12},{12,8},{9,1... | collective-permute-start | bytes 1769480 | tf_op jit(solution)/shard_map/made0/to_x/ppermute | solution.py:48
  313.4 28.3 %collective-permute-start.51 = (bf16[144,2048]{1,0:T(8,128)(2,1)}, bf16[144,2048]{1,0:T(8,128)(2,1)S(1)}, u32[]{:S(2)}, u32[]{:S(2)}) collective-permute-start(bf16[144,2048]{1,0:T(8,128)(2,1)} %get-tuple-element.180), channel_id=1, source_target_pairs={{0,6},{2,4},{4,2},{6,0},{1,7},{3,5},{5,3},{7,1},{8,14},{10,12},{12... | collective-permute-start | bytes 1769480 | tf_op jit(solution)/shard_map/made0/to_xy/ppermute | solution.py:52
  321.7 20.0 %collective-permute-start.47 = (bf16[128,2176]{1,0:T(8,128)(2,1)S(1)}, bf16[128,2176]{1,0:T(8,128)(2,1)S(1)}, u32[]{:S(2)}, u32[]{:S(2)}) collective-permute-start(bf16[128,2176]{1,0:T(8,128)(2,1)S(1)} %add_convert_fusion.1), channel_id=1, source_target_pairs={{0,24},{8,0},{16,8},{24,16},{1,25},{9,1},{17,9},{25,17},{2,26},{10... | collective-permute-start | bytes 1671176 | tf_op jit(solution)/shard_map/made_hop/ppermute | solution.py:72
  321.7 19.1 %collective-permute-start.48 = (bf16[256,512]{1,0:T(8,128)(2,1)S(1)}, bf16[256,512]{1,0:T(8,128)(2,1)S(1)}, u32[]{:S(2)}, u32[]{:S(2)}) collective-permute-start(bf16[256,512]{1,0:T(8,128)(2,1)S(1)} %add_convert_fusion.7), channel_id=1, source_target_pairs={{8,0},{16,8},{24,16},{9,1},{17,9},{25,17},{10,2},{18,10},{26,18},{... | collective-permute-start | bytes 786440 | tf_op jit(solution)/shard_map/kv_back_hop/ppermute | solution.py:67
  353.0 22.4 %collective-permute-start.53 = (bf16[128,2176]{1,0:T(8,128)(2,1)}, bf16[128,2176]{1,0:T(8,128)(2,1)S(1)}, u32[]{:S(2)}, u32[]{:S(2)}) collective-permute-start(bf16[128,2176]{1,0:T(8,128)(2,1)} %add_convert_fusion), channel_id=1, source_target_pairs={{0,24},{8,0},{16,8},{24,16},{1,25},{9,1},{17,9},{25,17},{2,26},{10... | collective-permute-start | bytes 1671176 | tf_op jit(solution)/shard_map/made_hop/ppermute | solution.py:72
  353.0 20.5 %collective-permute-start.54 = (bf16[256,512]{1,0:T(8,128)(2,1)}, bf16[256,512]{1,0:T(8,128)(2,1)S(1)}, u32[]{:S(2)}, u32[]{:S(2)}) collective-permute-start(bf16[256,512]{1,0:T(8,128)(2,1)} %add_convert_fusion.6), channel_id=1, source_target_pairs={{8,0},{16,8},{24,16},{9,1},{17,9},{25,17},{10,2},{18,10},{26,18},{... | collective-permute-start | bytes 786440 | tf_op jit(solution)/shard_map/kv_back_hop/ppermute | solution.py:67
  378.6 5.0 %collective-permute-start.55 = (bf16[128,512]{1,0:T(8,128)(2,1)S(1)}, bf16[128,512]{1,0:T(8,128)(2,1)S(1)}, u32[]{:S(2)}, u32[]{:S(2)}) collective-permute-start(bf16[128,512]{1,0:T(8,128)(2,1)S(1)} %slice.106), channel_id=1, source_target_pairs={{0,4},{4,0},{1,5},{5,1},{2,6},{6,2},{3,7},{7,3},{8,12},{12,8},{9,1... | collective-permute-start | bytes 393224 | tf_op jit(solution)/shard_map/kv_back_flip/ppermute | solution.py:48
  (57 other events, 563.7 us)

commit v4 on v2

--- a/solution.py
+++ b/solution.py
@@ -16,7 +16,7 @@
 
 NEG = -1e30
 OPT = {
-    "att": lambda cot, blocks: cot[0][1:] + [blocks[-1][1], blocks[-2][1]],
+    "att": lambda cot, blocks: [cot[-1][0]],
     "hop": lambda step, flipped, kv, cot: {1: [flipped], 3: cot[0][1:3] + [kv[2]] if cot else []}.get(step, []),
     "flip": lambda step, kv: {1: [kv[1]], 3: kv[3:4]}.get(step, []),
     "ga": lambda kv: [],
@@ -697,6 +697,9 @@
         if index == 0:
             with jax.named_scope("cot0"):
                 cot_pieces.append(gather(metas[0], 0, True, *OPT["ga"](kv_blocks)))
+    for index in range(1, len(groups)):
+        with jax.named_scope("cot1"):
+            cot_pieces.append(gather(metas[index], index, True, cot_pieces[-1][0], cot_pieces[-1][3]))
     attended, hidden, normed, inverse, log_sum = attend_forward(
         after(ctx, *OPT["att"](cot_pieces, payload_blocks)),
         query_heads[0],
@@ -704,12 +707,6 @@
         gain,
         kv_blocks,
     )
-    order = inverse
-    for index in range(1, len(groups)):
-        with jax.named_scope("cot1"):
-            cot_pieces.append(gather(metas[index], index, True, order, *cot_pieces[-1][1:]))
-        order = cot_pieces[-1][0]
-
     normed_blocks = []
     normed_pieces = []
     earlier = cot_pieces[-1][:3]

time: 386 us -> 383 us (level)
  starting transfers between devices: 69.9 us -> 64.5 us
    ppermute x30, starting transfers between devices: 16.9 us -> 27.9 us  [flip_axis(): return lax.ppermute(value, name, [(0, 1), (1, 0)])]
    ppermute x8, starting transfers between devices: 17.7 us -> 7.82 us  [flip_xy(): return lax.ppermute(value, ('x', 'y'), [(i, 3 - i) for i in range(4)])]
    ppermute x8, waiting for transfers between devices: 31.8 us -> 24.9 us  [flip_xy(): return lax.ppermute(value, ('x', 'y'), [(i, 3 - i) for i in range(4)])]
    ppermute x9, starting transfers between devices: 16.4 us -> 9.64 us  [ring_up(): return lax.ppermute(value, 'z', [(i, (i + 1) % size) for i in range(size)])]
    ppermute x9, waiting for transfers between devices: 66.8 us -> 72.9 us  [ring_up(): return lax.ppermute(value, 'z', [(i, (i + 1) % size) for i in range(size)])]
    unnamed x108 -> x104, local copies, waits for them, and re-layouts: 12.8 us -> 14.3 us
  transfers between devices with their start and end apart: 56 -> 56, of which waited for: 23 -> 23; matrix products, arithmetic and copies ran while one was open for 2% -> 2% of each run, Pallas kernels for 16% -> 20%
where the time goes in v4:
time: 383 us; the launch traced here: 376 us
  waiting for transfers between devices  182 us (48%)
  Pallas kernels  102 us (27%)
  starting transfers between devices  64.5 us (17%)
  local copies, waits for them, and re-layouts  15 us (4%)
  other arithmetic  10.7 us (3%)
    ppermute x9, waiting for transfers between devices, ring_up(): return lax.ppermute(value, 'z', [(i, (i + 1) % size) for i in range(size)])  72.9 us
    ppermute x3, waiting for transfers between devices, line_up(): return lax.ppermute(value, 'z', [(i, i + 1) for i in range(size - 1)])  39.1 us
    pallas_call x2, Pallas kernels, run_expert(): pl.pallas_call(expert_kernel, in_specs=[anywhere] * 11, out_specs=[anywhe...  35.6 us
    ppermute x30, starting transfers between devices, flip_axis(): return lax.ppermute(value, name, [(0, 1), (1, 0)])  27.9 us
    ppermute x3, waiting for transfers between devices, line_down(): return lax.ppermute(value, 'z', [(i + 1, i) for i in range(size - 1)])  26.2 us
    ppermute x8, waiting for transfers between devices, flip_xy(): return lax.ppermute(value, ('x', 'y'), [(i, 3 - i) for i in range(4)])  24.9 us
    pallas_call x4, Pallas kernels, combine_rows(): pl.pallas_call(functools.partial(kernel, experts, capacity, blocks), grid...  24.2 us
    pallas_call x4, Pallas kernels, gather_rows(): pl.pallas_call(functools.partial(gather_kernel, experts, capacity, weight...  15.2 us
  transfers between devices with their start and end apart: 56, of which 23 were waited for; matrix products, arithmetic and copies ran while one was open for 2% of the time, Pallas kernels for 20%

profile of v4, /device:TPU:0, one launch (start us, length us, event | category | flops | bytes accessed | tf_op | source)
XLA Modules:
  0.0 376.4 jit_solution(7842585048411451702)
XLA Ops:
  1.6 3.0 collective-permute-start.1
  8.1 1.8 collective-permute-start.2
  9.9 3.5 collective-permute-start.3
  13.5 13.0 %collective-permute-done.3.refs_1_.refs_11_ = bf16[256,512]{1,0:T(8,128)(2,1)S(1)} collective-permute-done((bf16[256,512]{1,0:T(8,128)(2,1)S(1)}, bf16[256,512]{1,0:T(8,128)(2,1)S(1)}, u32[]{:S(2)}, u32[]{:S(2)}) %collective-permute-start.3) | collective-permute-done | bytes 262176 | tf_op jit(solution)/shard_map/kv_hop/ppermute | solution.py:63
  26.6 1.8 collective-permute-done.4.refs_3_.refs_7_.refs_11_
  28.5 3.7 gather_weighted.2
  32.2 1.6 collective-permute-start.8
  35.3 2.5 collective-permute-start.6
  37.8 3.5 collective-permute-start.10
  41.3 13.8 %collective-permute-done.10.refs_2_.refs_12_ = bf16[256,512]{1,0:T(8,128)(2,1)S(1)} collective-permute-done((bf16[256,512]{1,0:T(8,128)(2,1)S(1)}, bf16[256,512]{1,0:T(8,128)(2,1)S(1)}, u32[]{:S(2)}, u32[]{:S(2)}) %collective-permute-start.10) | collective-permute-done | bytes 262176 | tf_op jit(solution)/shard_map/kv_hop/ppermute | solution.py:63
  55.1 2.5 collective-permute-start.11
  57.7 3.5 collective-permute-start.12
  61.7 12.3 %collective-permute-done.12.refs_3_.refs_13_ = bf16[256,512]{1,0:T(8,128)(2,1)S(1)} collective-permute-done((bf16[256,512]{1,0:T(8,128)(2,1)S(1)}, bf16[256,512]{1,0:T(8,128)(2,1)S(1)}, u32[]{:S(2)}, u32[]{:S(2)}) %collective-permute-start.12) | collective-permute-done | bytes 262176 | tf_op jit(solution)/shard_map/kv_hop/ppermute | solution.py:63
  76.7 4.3 %gather_weighted.3 = (bf16[144,2048]{1,0:T(8,128)(2,1)S(1)}, bf16[144,2048]{1,0:T(8,128)(2,1)}, bf16[144,2048]{1,0:T(8,128)(2,1)}, bf16[144,2048]{1,0:T(8,128)(2,1)S(1)}) custom-call(s32[4]{0:T(128)S(1)} %pad_add_fusion.1.names_ref, bf16[128,2176]{1,0:T(8,128)(2,1)S(1)} %collective-permute-done.6.refs_0_.refs_4_.refs_8_, ...), custom_call_target="tpu_custom_call" | custom-call | bytes 4000000 | tf_op jit(solution)/shard_map/cot1/gather_weighted/pallas_call | solution.py:203
  83.7 12.1 %attend_forward.1 = (bf16[128,2048]{1,0:T(8,128)(2,1)}, bf16[128,2048]{1,0:T(8,128)(2,1)}, bf16[128,2048]{1,0:T(8,128)(2,1)}, f32[128,1]{1,0:T(8,128)}, f32[16,128]{1,0:T(8,128)}) custom-call(s32[2]{0:T(128)} %pad_add_fusion.ctx_ref, bf16[128,2048]{1,0:T(8,128)(2,1)} %bitcast.52, bf16[128,2048]{1,0:T(8,128)(2,1)} %bitcast.54, f32[1,2048]{1,0:T(1,128)} %bitcast.60, ...), custom_call_target="tpu_custom_call" | custom-call | bytes 12000000 | tf_op jit(solution)/shard_map/attend_forward/pallas_call | solution.py:515
  95.8 2.5 collective-permute-start.17
  98.3 2.5 collective-permute-start.22
  100.8 11.4 %collective-permute-done.17.refs_2_ = bf16[128,2048]{1,0:T(8,128)(2,1)S(1)} collective-permute-done((bf16[128,2048]{1,0:T(8,128)(2,1)}, bf16[128,2048]{1,0:T(8,128)(2,1)S(1)}, u32[]{:S(2)}, u32[]{:S(2)}) %collective-permute-start.17) | collective-permute-done | bytes 524320 | tf_op jit(solution)/shard_map/normed/hop/ppermute | solution.py:58
  112.3 1.8 collective-permute-done.18.refs_3_
  115.2 3.0 gather_plain.2
  118.2 1.6 collective-permute-start.19
  121.3 7.1 %collective-permute-done.23.refs_0_ = bf16[128,2048]{1,0:T(8,128)(2,1)S(1)} collective-permute-done((bf16[128,2048]{1,0:T(8,128)(2,1)S(1)}, bf16[128,2048]{1,0:T(8,128)(2,1)S(1)}, u32[]{:S(2)}, u32[]{:S(2)}) %collective-permute-start.23) | collective-permute-done | bytes 524320 | tf_op jit(solution)/shard_map/normed/hop/ppermute | solution.py:58
  128.4 2.4 collective-permute-start.21
  130.8 12.8 %collective-permute-done.25.refs_2_ = bf16[128,2048]{1,0:T(8,128)(2,1)S(1)} collective-permute-done((bf16[128,2048]{1,0:T(8,128)(2,1)S(1)}, bf16[128,2048]{1,0:T(8,128)(2,1)S(1)}, u32[]{:S(2)}, u32[]{:S(2)}) %collective-permute-start.25) | collective-permute-done | bytes 524320 | tf_op jit(solution)/shard_map/normed/hop/ppermute | solution.py:58
  144.2 3.2 collective-permute-done.21.refs_3_
  147.5 4.2 %gather_plain.3 = (bf16[144,2048]{1,0:T(8,128)(2,1)S(1)}, bf16[144,2048]{1,0:T(8,128)(2,1)}, bf16[144,2048]{1,0:T(8,128)(2,1)}, bf16[144,2048]{1,0:T(8,128)(2,1)}) custom-call(s32[4]{0:T(128)S(1)} %pad_add_fusion.1.names_ref, bf16[128,2048]{1,0:T(8,128)(2,1)S(1)} %collective-permute-done.23.refs_0_, bf16[128,2048]{1,0:T(8,128)(2,1)S(1)} %collective-permute-done.24.refs_1_, ...), custom_call_target="tpu_custom_call" | custom-call | bytes 4000000 | tf_op jit(solution)/shard_map/normed1/gather_plain/pallas_call | solution.py:203
  156.0 17.6 %expert.2 = (bf16[144,2048]{1,0:T(8,128)(2,1)}, bf16[144,2048]{1,0:T(8,128)(2,1)}, bf16[144,2048]{1,0:T(8,128)(2,1)}, bf16[144,2048]{1,0:T(8,128)(2,1)}, bf16[14...) custom-call(bf16[144,2048]{1,0:T(8,128)(2,1)} %copy-done.9, ...), custom_call_target="tpu_custom_call" | custom-call | bytes 18000000 | tf_op jit(solution)/shard_map/expert/pallas_call | solution.py:291
  173.6 1.6 collective-permute-start.30
  177.2 6.1 %collective-permute-done.29.refs_3_ = bf16[144,2048]{1,0:T(8,128)(2,1)} collective-permute-done((bf16[144,2048]{1,0:T(8,128)(2,1)}, bf16[144,2048]{1,0:T(8,128)(2,1)}, u32[]{:S(2)}, u32[]{:S(2)}) %collective-permute-start.29) | collective-permute-done | bytes 589856 | tf_op jit(solution)/shard_map/normed1/to_xy/ppermute | solution.py:53
  183.3 18.0 %expert.3 = (bf16[144,2048]{1,0:T(8,128)(2,1)}, bf16[144,2048]{1,0:T(8,128)(2,1)}, bf16[144,2048]{1,0:T(8,128)(2,1)}, bf16[144,2048]{1,0:T(8,128)(2,1)}, bf16[14...) custom-call(bf16[144,2048]{1,0:T(8,128)(2,1)} %copy-done.11, ...), custom_call_target="tpu_custom_call" | custom-call | bytes 18000000 | tf_op jit(solution)/shard_map/expert/pallas_call | solution.py:291
  201.3 4.9 %collective-permute-done.32.refs_3_ = bf16[144,2048]{1,0:T(8,128)(2,1)} collective-permute-done((bf16[144,2048]{1,0:T(8,128)(2,1)}, bf16[144,2048]{1,0:T(8,128)(2,1)}, u32[]{:S(2)}, u32[]{:S(2)}) %collective-permute-start.32) | collective-permute-done | bytes 589856 | tf_op jit(solution)/shard_map/row0/to_xy/ppermute | solution.py:53
  207.3 5.2 %combine_plain.2 = (f32[128,2048]{1,0:T(8,128)S(1)}, f32[128,2048]{1,0:T(8,128)S(1)}, bf16[256,2048]{1,0:T(8,128)(2,1)S(1)}) custom-call(s32[4]{0:T(128)S(1)} %pad_add_fusion.1.names_ref, bf16[144,2048]{1,0:T(8,128)(2,1)S(1)} %copy-done.12, bf16[144,2048]{1,0:T(8,128)(2,1)} %collective-permute-done.30.refs_1_, ...), custom_call_target="tpu_custom_call" | custom-call | bytes 8000000 | tf_op jit(solution)/shard_map/row0/combine_plain/pallas_call | solution.py:429
  212.6 1.6 collective-permute-start.35
  216.4 15.2 %collective-permute-done.34 = bf16[128,2048]{1,0:T(8,128)(2,1)S(1)} collective-permute-done((bf16[128,2048]{1,0:T(8,128)(2,1)S(1)}, bf16[128,2048]{1,0:T(8,128)(2,1)S(1)}, u32[]{:S(2)}, u32[]{:S(2)}) %collective-permute-start.34) | collective-permute-done | bytes 524320 | tf_op jit(solution)/shard_map/row_hop/ppermute | solution.py:58
  231.6 10.6 %collective-permute-done.37.refs_3_ = bf16[144,2048]{1,0:T(8,128)(2,1)S(1)} collective-permute-done((bf16[144,2048]{1,0:T(8,128)(2,1)S(1)}, bf16[144,2048]{1,0:T(8,128)(2,1)S(1)}, u32[]{:S(2)}, u32[]{:S(2)}) %collective-permute-start.37) | collective-permute-done | bytes 589856 | tf_op jit(solution)/shard_map/row1/to_xy/ppermute | solution.py:53
  242.2 4.4 %combine_plain.3 = (f32[128,2048]{1,0:T(8,128)S(1)}, f32[128,2048]{1,0:T(8,128)S(1)}, bf16[256,2048]{1,0:T(8,128)(2,1)S(1)}) custom-call(s32[4]{0:T(128)S(1)} %pad_add_fusion.1.names_ref, bf16[144,2048]{1,0:T(8,128)(2,1)S(1)} %copy-done.10, bf16[144,2048]{1,0:T(8,128)(2,1)S(1)} %collective-permute-done.35.refs_1_, ...), custom_call_target="tpu_custom_call" | custom-call | bytes 8000000 | tf_op jit(solution)/shard_map/row1/combine_plain/pallas_call | solution.py:429
  246.7 2.6 collective-permute-done.38
  253.9 11.5 %collective-permute-done.39 = bf16[128,2048]{1,0:T(8,128)(2,1)S(1)} collective-permute-done((bf16[128,2048]{1,0:T(8,128)(2,1)S(1)}, bf16[128,2048]{1,0:T(8,128)(2,1)S(1)}, u32[]{:S(2)}, u32[]{:S(2)}) %collective-permute-start.39) | collective-permute-done | bytes 524320 | tf_op jit(solution)/shard_map/row_hop/ppermute | solution.py:58
  265.6 14.9 %collective-permute-done.40.refs_7_ = bf16[128,2048]{1,0:T(8,128)(2,1)S(1)} collective-permute-done((bf16[128,2048]{1,0:T(8,128)(2,1)S(1)}, bf16[128,2048]{1,0:T(8,128)(2,1)S(1)}, u32[]{:S(2)}, u32[]{:S(2)}) %collective-permute-start.40) | collective-permute-done | bytes 524320 | tf_op jit(solution)/shard_map/row_hop/ppermute | solution.py:58
  281.4 7.2 %combine_weighted.2 = (f32[128,2176]{1,0:T(8,128)S(1)}, f32[128,2176]{1,0:T(8,128)S(1)}, bf16[256,2176]{1,0:T(8,128)(2,1)S(1)}) custom-call(s32[4]{0:T(128)S(1)} %pad_add_fusion.1.names_ref, bf16[144,2048]{1,0:T(8,128)(2,1)S(1)} %copy-done.14, bf16[144,2048]{1,0:T(8,128)(2,1)S(1)} %collective-permute-done.41.refs_1_, ...), custom_call_target="tpu_custom_call" | custom-call | bytes 8000000 | tf_op jit(solution)/shard_map/made1/combine_weighted/pallas_call | solution.py:429
  288.6 1.6 collective-permute-start.48
  294.4 15.2 %attend_backward.1 = (bf16[128,2048]{1,0:T(8,128)(2,1)}, bf16[128,2048]{1,0:T(8,128)(2,1)}, f32[256,512]{1,0:T(8,128)}, f32[256,512]{1,0:T(8,128)}, f32[256,512]{1,0:T(8,128)}, /*index=5*/bf16[256,512]{1,0:T(8,128)(2,1)}) custom-call(s32[2]{0:T(128)} %pad_add_fusion.ctx_ref, bf16[128,2048]{1,0:T(8,128)(2,1)} %bitcast.53, ...), custom_call_target="tpu_custom_call" | custom-call | bytes 15000000 | tf_op jit(solution)/shard_map/attend_backward/pallas_call | solution.py:606
  311.0 8.3 %collective-permute-done.46 = bf16[256,512]{1,0:T(8,128)(2,1)S(1)} collective-permute-done((bf16[256,512]{1,0:T(8,128)(2,1)}, bf16[256,512]{1,0:T(8,128)(2,1)S(1)}, u32[]{:S(2)}, u32[]{:S(2)}) %collective-permute-start.46) | collective-permute-done | bytes 262176 | tf_op jit(solution)/shard_map/kv_back_hop/ppermute | solution.py:68
  325.7 7.4 %combine_weighted.3 = (f32[128,2176]{1,0:T(8,128)S(1)}, f32[128,2176]{1,0:T(8,128)S(1)}, bf16[256,2176]{1,0:T(8,128)(2,1)S(1)}) custom-call(s32[4]{0:T(128)S(1)} %pad_add_fusion.1.names_ref, bf16[144,2048]{1,0:T(8,128)(2,1)S(1)} %copy-done.13, bf16[144,2048]{1,0:T(8,128)(2,1)S(1)} %copy-done.16, bf16[144,2048]{1,0:T(8,128)(2,1)S(1)} %copy-done.18, ...), custom_call_target="tpu_custom_call" | custom-call | bytes 8000000 | tf_op jit(solution)/shard_map/made0/combine_weighted/pallas_call | solution.py:429
  334.5 2.3 collective-permute-start.47
  338.3 17.8 %collective-permute-done.54 = bf16[256,512]{1,0:T(8,128)(2,1)S(1)} collective-permute-done((bf16[256,512]{1,0:T(8,128)(2,1)S(1)}, bf16[256,512]{1,0:T(8,128)(2,1)S(1)}, u32[]{:S(2)}, u32[]{:S(2)}) %collective-permute-start.54) | collective-permute-done | bytes 262176 | tf_op jit(solution)/shard_map/kv_back_hop/ppermute | solution.py:68
  356.2 1.6 collective-permute-start.55
  363.2 10.0 %collective-permute-done.52 = bf16[128,2176]{1,0:T(8,128)(2,1)S(1)} collective-permute-done((bf16[128,2176]{1,0:T(8,128)(2,1)}, bf16[128,2176]{1,0:T(8,128)(2,1)S(1)}, u32[]{:S(2)}, u32[]{:S(2)}) %collective-permute-start.52) | collective-permute-done | bytes 557088 | tf_op jit(solution)/shard_map/made_hop/ppermute | solution.py:73
  (206 shorter events, 53.8 us)
Async XLA Ops:
  1.6 6.5 %collective-permute-start.1 = (bf16[128,512]{1,0:T(8,128)(2,1)S(1)}, bf16[128,512]{1,0:T(8,128)(2,1)S(1)}, u32[]{:S(2)}, u32[]{:S(2)}) collective-permute-start(bf16[128,512]{1,0:T(8,128)(2,1)S(1)} %pad_maximum_fusion.1), channel_id=1, source_target_pairs={{0,4},{4,0},{1,5},{5,1},{2,6},{6,2},{3,7},{7,3},{8,12},{12,8},{9,1... | collective-permute-start | bytes 393224 | tf_op jit(solution)/shard_map/kv_flip/ppermute | solution.py:49
  8.1 18.5 %collective-permute-start.2 = (bf16[128,2176]{1,0:T(8,128)(2,1)S(1)}, bf16[128,2176]{1,0:T(8,128)(2,1)S(1)}, u32[]{:S(2)}, u32[]{:S(2)}) collective-permute-start(bf16[128,2176]{1,0:T(8,128)(2,1)S(1)} %routing.1.refs_0_.refs_4_.refs_8_), channel_id=1, source_target_pairs={{0,8},{8,16},{16,24},{24,0},{1,9},{9,17},{17,25},{25,1},{2,10},{10... | collective-permute-start | bytes 1671176 | tf_op jit(solution)/shard_map/cot/hop/ppermute | solution.py:58
  9.9 16.6 %collective-permute-start.3 = (bf16[256,512]{1,0:T(8,128)(2,1)S(1)}, bf16[256,512]{1,0:T(8,128)(2,1)S(1)}, u32[]{:S(2)}, u32[]{:S(2)}) collective-permute-start(bf16[256,512]{1,0:T(8,128)(2,1)S(1)} %pad_maximum_fusion.refs_0_.refs_10_), channel_id=1, source_target_pairs={{0,8},{8,16},{16,24},{1,9},{9,17},{17,25},{2,10},{10,18},{18,26},{... | collective-permute-start | bytes 786440 | tf_op jit(solution)/shard_map/kv_hop/ppermute | solution.py:63
  13.4 13.2 %collective-permute-start = (bf16[128,2176]{1,0:T(8,128)(2,1)S(1)}, bf16[128,2176]{1,0:T(8,128)(2,1)S(1)}, u32[]{:S(2)}, u32[]{:S(2)}) collective-permute-start(bf16[128,2176]{1,0:T(8,128)(2,1)S(1)} %routing.1.refs_0_.refs_4_.refs_8_), channel_id=1, source_target_pairs={{0,1},{1,0},{2,3},{3,2},{4,5},{5,4},{6,7},{7,6},{8,9},{9,8},{10,11... | collective-permute-start | bytes 1671176 | tf_op jit(solution)/shard_map/cot/flip/ppermute | solution.py:49
  32.2 22.9 %collective-permute-start.8 = (bf16[144,2048]{1,0:T(8,128)(2,1)S(1)}, bf16[144,2048]{1,0:T(8,128)(2,1)S(1)}, u32[]{:S(2)}, u32[]{:S(2)}) collective-permute-start(bf16[144,2048]{1,0:T(8,128)(2,1)S(1)} %get-tuple-element.101), channel_id=1, source_target_pairs={{0,2},{2,0},{1,3},{3,1},{4,6},{6,4},{5,7},{7,5},{8,10},{10,8},{9,1... | collective-permute-start | bytes 1769480 | tf_op jit(solution)/shard_map/cot0/to_y/ppermute | solution.py:49
  33.8 21.3 %collective-permute-start.9 = (bf16[144,2048]{1,0:T(8,128)(2,1)S(1)}, bf16[144,2048]{1,0:T(8,128)(2,1)S(1)}, u32[]{:S(2)}, u32[]{:S(2)}) collective-permute-start(bf16[144,2048]{1,0:T(8,128)(2,1)S(1)} %get-tuple-element.102), channel_id=1, source_target_pairs={{0,4},{4,0},{1,5},{5,1},{2,6},{6,2},{3,7},{7,3},{8,12},{12,8},{9,1... | collective-permute-start | bytes 1769480 | tf_op jit(solution)/shard_map/cot0/to_x/ppermute | solution.py:49
  35.3 19.8 %collective-permute-start.6 = (bf16[128,2176]{1,0:T(8,128)(2,1)S(1)}, bf16[128,2176]{1,0:T(8,128)(2,1)S(1)}, u32[]{:S(2)}, u32[]{:S(2)}) collective-permute-start(bf16[128,2176]{1,0:T(8,128)(2,1)S(1)} %collective-permute-done.2.refs_2_.refs_6_.refs_10_), channel_id=1, source_target_pairs={{0,8},{8,16},{16,24},{24,0},{1,9},{9,17},{17,25},{25,1},{2,10},{10... | collective-permute-start | bytes 1671176 | tf_op jit(solution)/shard_map/cot/hop/ppermute | solution.py:58
  37.8 17.2 %collective-permute-start.10 = (bf16[256,512]{1,0:T(8,128)(2,1)S(1)}, bf16[256,512]{1,0:T(8,128)(2,1)S(1)}, u32[]{:S(2)}, u32[]{:S(2)}) collective-permute-start(bf16[256,512]{1,0:T(8,128)(2,1)S(1)} %collective-permute-done.3.refs_1_.refs_11_), channel_id=1, source_target_pairs={{0,8},{8,16},{16,24},{1,9},{9,17},{17,25},{2,10},{10,18},{18,26},{... | collective-permute-start | bytes 786440 | tf_op jit(solution)/shard_map/kv_hop/ppermute | solution.py:63
  55.1 19.6 %collective-permute-start.11 = (bf16[128,2176]{1,0:T(8,128)(2,1)S(1)}, bf16[128,2176]{1,0:T(8,128)(2,1)S(1)}, u32[]{:S(2)}, u32[]{:S(2)}) collective-permute-start(bf16[128,2176]{1,0:T(8,128)(2,1)S(1)} %collective-permute-done.6.refs_0_.refs_4_.refs_8_), channel_id=1, source_target_pairs={{0,8},{8,16},{16,24},{24,0},{1,9},{9,17},{17,25},{25,1},{2,10},{10... | collective-permute-start | bytes 1671176 | tf_op jit(solution)/shard_map/cot/hop/ppermute | solution.py:58
  57.7 16.3 %collective-permute-start.12 = (bf16[256,512]{1,0:T(8,128)(2,1)S(1)}, bf16[256,512]{1,0:T(8,128)(2,1)S(1)}, u32[]{:S(2)}, u32[]{:S(2)}) collective-permute-start(bf16[256,512]{1,0:T(8,128)(2,1)S(1)} %collective-permute-done.10.refs_2_.refs_12_), channel_id=1, source_target_pairs={{0,8},{8,16},{16,24},{1,9},{9,17},{17,25},{2,10},{10,18},{18,26},{... | collective-permute-start | bytes 786440 | tf_op jit(solution)/shard_map/kv_hop/ppermute | solution.py:63
  61.2 14.3 %collective-permute-start.5 = (bf16[144,2048]{1,0:T(8,128)(2,1)S(1)}, bf16[144,2048]{1,0:T(8,128)(2,1)S(1)}, u32[]{:S(2)}, u32[]{:S(2)}) collective-permute-start(bf16[144,2048]{1,0:T(8,128)(2,1)S(1)} %get-tuple-element.99), channel_id=1, source_target_pairs={{0,6},{2,4},{4,2},{6,0},{1,7},{3,5},{5,3},{7,1},{8,14},{10,12},{12... | collective-permute-start | bytes 1769480 | tf_op jit(solution)/shard_map/cot0/to_xy/ppermute | solution.py:53
  61.7 13.8 %collective-permute-start.7 = (bf16[128,2176]{1,0:T(8,128)(2,1)S(1)}, bf16[128,2176]{1,0:T(8,128)(2,1)S(1)}, u32[]{:S(2)}, u32[]{:S(2)}) collective-permute-start(bf16[128,2176]{1,0:T(8,128)(2,1)S(1)} %collective-permute-done.6.refs_0_.refs_4_.refs_8_), channel_id=1, source_target_pairs={{0,1},{1,0},{2,3},{3,2},{4,5},{5,4},{6,7},{7,6},{8,9},{9,8},{10,11... | collective-permute-start | bytes 1671176 | tf_op jit(solution)/shard_map/cot/flip/ppermute | solution.py:49
  82.7 29.5 %collective-permute-start.14 = (bf16[144,2048]{1,0:T(8,128)(2,1)}, bf16[144,2048]{1,0:T(8,128)(2,1)}, u32[]{:S(2)}, u32[]{:S(2)}) collective-permute-start(bf16[144,2048]{1,0:T(8,128)(2,1)} %get-tuple-element.108), channel_id=1, source_target_pairs={{0,2},{2,0},{1,3},{3,1},{4,6},{6,4},{5,7},{7,5},{8,10},{10,8},{9,1... | collective-permute-start | bytes 1769480 | tf_op jit(solution)/shard_map/cot1/to_y/ppermute | solution.py:49
  83.2 29.0 %collective-permute-start.15 = (bf16[144,2048]{1,0:T(8,128)(2,1)}, bf16[144,2048]{1,0:T(8,128)(2,1)}, u32[]{:S(2)}, u32[]{:S(2)}) collective-permute-start(bf16[144,2048]{1,0:T(8,128)(2,1)} %get-tuple-element.109), channel_id=1, source_target_pairs={{0,4},{4,0},{1,5},{5,1},{2,6},{6,2},{3,7},{7,3},{8,12},{12,8},{9,1... | collective-permute-start | bytes 1769480 | tf_op jit(solution)/shard_map/cot1/to_x/ppermute | solution.py:49
  95.8 16.4 %collective-permute-start.17 = (bf16[128,2048]{1,0:T(8,128)(2,1)}, bf16[128,2048]{1,0:T(8,128)(2,1)S(1)}, u32[]{:S(2)}, u32[]{:S(2)}) collective-permute-start(bf16[128,2048]{1,0:T(8,128)(2,1)} %get-tuple-element.111.refs_0_), channel_id=1, source_target_pairs={{0,8},{8,16},{16,24},{24,0},{1,9},{9,17},{17,25},{25,1},{2,10},{10... | collective-permute-start | bytes 1572872 | tf_op jit(solution)/shard_map/normed/hop/ppermute | solution.py:58
  98.3 23.0 %collective-permute-start.22 = (bf16[144,2048]{1,0:T(8,128)(2,1)}, bf16[144,2048]{1,0:T(8,128)(2,1)S(1)}, u32[]{:S(2)}, u32[]{:S(2)}) collective-permute-start(bf16[144,2048]{1,0:T(8,128)(2,1)} %copy-done.24), channel_id=1, source_target_pairs={{0,6},{2,4},{4,2},{6,0},{1,7},{3,5},{5,3},{7,1},{8,14},{10,12},{12... | collective-permute-start | bytes 1769480 | tf_op jit(solution)/shard_map/cot1/to_xy/ppermute | solution.py:53
  100.8 11.5 %collective-permute-start.16 = (bf16[128,2048]{1,0:T(8,128)(2,1)}, bf16[128,2048]{1,0:T(8,128)(2,1)S(1)}, u32[]{:S(2)}, u32[]{:S(2)}) collective-permute-start(bf16[128,2048]{1,0:T(8,128)(2,1)} %get-tuple-element.111.refs_0_), channel_id=1, source_target_pairs={{0,1},{1,0},{2,3},{3,2},{4,5},{5,4},{6,7},{7,6},{8,9},{9,8},{10,11... | collective-permute-start | bytes 1572872 | tf_op jit(solution)/shard_map/normed/flip/ppermute | solution.py:49
  112.2 16.1 %collective-permute-start.23 = (bf16[128,2048]{1,0:T(8,128)(2,1)S(1)}, bf16[128,2048]{1,0:T(8,128)(2,1)S(1)}, u32[]{:S(2)}, u32[]{:S(2)}) collective-permute-start(bf16[128,2048]{1,0:T(8,128)(2,1)S(1)} %collective-permute-done.17.refs_2_), channel_id=1, source_target_pairs={{0,8},{8,16},{16,24},{24,0},{1,9},{9,17},{17,25},{25,1},{2,10},{10... | collective-permute-start | bytes 1572872 | tf_op jit(solution)/shard_map/normed/hop/ppermute | solution.py:58
  118.2 25.4 %collective-permute-start.19 = (bf16[144,2048]{1,0:T(8,128)(2,1)S(1)}, bf16[144,2048]{1,0:T(8,128)(2,1)S(1)}, u32[]{:S(2)}, u32[]{:S(2)}) collective-permute-start(bf16[144,2048]{1,0:T(8,128)(2,1)S(1)} %get-tuple-element.113), channel_id=1, source_target_pairs={{0,2},{2,0},{1,3},{3,1},{4,6},{6,4},{5,7},{7,5},{8,10},{10,8},{9,1... | collective-permute-start | bytes 1769480 | tf_op jit(solution)/shard_map/normed0/to_y/ppermute | solution.py:49
  119.8 23.9 %collective-permute-start.20 = (bf16[144,2048]{1,0:T(8,128)(2,1)S(1)}, bf16[144,2048]{1,0:T(8,128)(2,1)S(1)}, u32[]{:S(2)}, u32[]{:S(2)}) collective-permute-start(bf16[144,2048]{1,0:T(8,128)(2,1)S(1)} %get-tuple-element.114), channel_id=1, source_target_pairs={{0,4},{4,0},{1,5},{5,1},{2,6},{6,2},{3,7},{7,3},{8,12},{12,8},{9,1... | collective-permute-start | bytes 1769480 | tf_op jit(solution)/shard_map/normed0/to_x/ppermute | solution.py:49
  128.4 15.3 %collective-permute-start.25 = (bf16[128,2048]{1,0:T(8,128)(2,1)S(1)}, bf16[128,2048]{1,0:T(8,128)(2,1)S(1)}, u32[]{:S(2)}, u32[]{:S(2)}) collective-permute-start(bf16[128,2048]{1,0:T(8,128)(2,1)S(1)} %collective-permute-done.23.refs_0_), channel_id=1, source_target_pairs={{0,8},{8,16},{16,24},{24,0},{1,9},{9,17},{17,25},{25,1},{2,10},{10... | collective-permute-start | bytes 1572872 | tf_op jit(solution)/shard_map/normed/hop/ppermute | solution.py:58
  128.4 19.1 %collective-permute-start.21 = (bf16[144,2048]{1,0:T(8,128)(2,1)S(1)}, bf16[144,2048]{1,0:T(8,128)(2,1)S(1)}, u32[]{:S(2)}, u32[]{:S(2)}) collective-permute-start(bf16[144,2048]{1,0:T(8,128)(2,1)S(1)} %get-tuple-element.115), channel_id=1, source_target_pairs={{0,6},{2,4},{4,2},{6,0},{1,7},{3,5},{5,3},{7,1},{8,14},{10,12},{12... | collective-permute-start | bytes 1769480 | tf_op jit(solution)/shard_map/normed0/to_xy/ppermute | solution.py:53
  152.5 24.2 %collective-permute-start.27 = (bf16[144,2048]{1,0:T(8,128)(2,1)}, bf16[144,2048]{1,0:T(8,128)(2,1)}, u32[]{:S(2)}, u32[]{:S(2)}) collective-permute-start(bf16[144,2048]{1,0:T(8,128)(2,1)} %get-tuple-element.125), channel_id=1, source_target_pairs={{0,2},{2,0},{1,3},{3,1},{4,6},{6,4},{5,7},{7,5},{8,10},{10,8},{9,1... | collective-permute-start | bytes 1769480 | tf_op jit(solution)/shard_map/normed1/to_y/ppermute | solution.py:49
  154.0 23.1 %collective-permute-start.28 = (bf16[144,2048]{1,0:T(8,128)(2,1)}, bf16[144,2048]{1,0:T(8,128)(2,1)}, u32[]{:S(2)}, u32[]{:S(2)}) collective-permute-start(bf16[144,2048]{1,0:T(8,128)(2,1)} %get-tuple-element.126), channel_id=1, source_target_pairs={{0,4},{4,0},{1,5},{5,1},{2,6},{6,2},{3,7},{7,3},{8,12},{12,8},{9,1... | collective-permute-start | bytes 1769480 | tf_op jit(solution)/shard_map/normed1/to_x/ppermute | solution.py:49
  155.5 27.7 %collective-permute-start.29 = (bf16[144,2048]{1,0:T(8,128)(2,1)}, bf16[144,2048]{1,0:T(8,128)(2,1)}, u32[]{:S(2)}, u32[]{:S(2)}) collective-permute-start(bf16[144,2048]{1,0:T(8,128)(2,1)} %get-tuple-element.127), channel_id=1, source_target_pairs={{0,6},{2,4},{4,2},{6,0},{1,7},{3,5},{5,3},{7,1},{8,14},{10,12},{12... | collective-permute-start | bytes 1769480 | tf_op jit(solution)/shard_map/normed1/to_xy/ppermute | solution.py:53
  173.6 27.6 %collective-permute-start.30 = (bf16[144,2048]{1,0:T(8,128)(2,1)}, bf16[144,2048]{1,0:T(8,128)(2,1)}, u32[]{:S(2)}, u32[]{:S(2)}) collective-permute-start(bf16[144,2048]{1,0:T(8,128)(2,1)} %get-tuple-element.134), channel_id=1, source_target_pairs={{0,2},{2,0},{1,3},{3,1},{4,6},{6,4},{5,7},{7,5},{8,10},{10,8},{9,1... | collective-permute-start | bytes 1769480 | tf_op jit(solution)/shard_map/row0/to_y/ppermute | solution.py:49
  175.2 26.1 %collective-permute-start.31 = (bf16[144,2048]{1,0:T(8,128)(2,1)}, bf16[144,2048]{1,0:T(8,128)(2,1)}, u32[]{:S(2)}, u32[]{:S(2)}) collective-permute-start(bf16[144,2048]{1,0:T(8,128)(2,1)} %get-tuple-element.135), channel_id=1, source_target_pairs={{0,4},{4,0},{1,5},{5,1},{2,6},{6,2},{3,7},{7,3},{8,12},{12,8},{9,1... | collective-permute-start | bytes 1769480 | tf_op jit(solution)/shard_map/row0/to_x/ppermute | solution.py:49
  176.7 29.5 %collective-permute-start.32 = (bf16[144,2048]{1,0:T(8,128)(2,1)}, bf16[144,2048]{1,0:T(8,128)(2,1)}, u32[]{:S(2)}, u32[]{:S(2)}) collective-permute-start(bf16[144,2048]{1,0:T(8,128)(2,1)} %get-tuple-element.136), channel_id=1, source_target_pairs={{0,6},{2,4},{4,2},{6,0},{1,7},{3,5},{5,3},{7,1},{8,14},{10,12},{12... | collective-permute-start | bytes 1769480 | tf_op jit(solution)/shard_map/row0/to_xy/ppermute | solution.py:53
  212.6 19.0 %collective-permute-start.35 = (bf16[144,2048]{1,0:T(8,128)(2,1)S(1)}, bf16[144,2048]{1,0:T(8,128)(2,1)S(1)}, u32[]{:S(2)}, u32[]{:S(2)}) collective-permute-start(bf16[144,2048]{1,0:T(8,128)(2,1)S(1)} %copy-done.51), channel_id=1, source_target_pairs={{0,2},{2,0},{1,3},{3,1},{4,6},{6,4},{5,7},{7,5},{8,10},{10,8},{9,1... | collective-permute-start | bytes 1769480 | tf_op jit(solution)/shard_map/row1/to_y/ppermute | solution.py:49
  214.2 17.4 %collective-permute-start.36 = (bf16[144,2048]{1,0:T(8,128)(2,1)S(1)}, bf16[144,2048]{1,0:T(8,128)(2,1)S(1)}, u32[]{:S(2)}, u32[]{:S(2)}) collective-permute-start(bf16[144,2048]{1,0:T(8,128)(2,1)S(1)} %copy-done.50), channel_id=1, source_target_pairs={{0,4},{4,0},{1,5},{5,1},{2,6},{6,2},{3,7},{7,3},{8,12},{12,8},{9,1... | collective-permute-start | bytes 1769480 | tf_op jit(solution)/shard_map/row1/to_x/ppermute | solution.py:49
  215.7 26.5 %collective-permute-start.37 = (bf16[144,2048]{1,0:T(8,128)(2,1)S(1)}, bf16[144,2048]{1,0:T(8,128)(2,1)S(1)}, u32[]{:S(2)}, u32[]{:S(2)}) collective-permute-start(bf16[144,2048]{1,0:T(8,128)(2,1)S(1)} %copy-done.49), channel_id=1, source_target_pairs={{0,6},{2,4},{4,2},{6,0},{1,7},{3,5},{5,3},{7,1},{8,14},{10,12},{12... | collective-permute-start | bytes 1769480 | tf_op jit(solution)/shard_map/row1/to_xy/ppermute | solution.py:53
  216.3 15.3 %collective-permute-start.34 = (bf16[128,2048]{1,0:T(8,128)(2,1)S(1)}, bf16[128,2048]{1,0:T(8,128)(2,1)S(1)}, u32[]{:S(2)}, u32[]{:S(2)}) collective-permute-start(bf16[128,2048]{1,0:T(8,128)(2,1)S(1)} %add_convert_fusion.5), channel_id=1, source_target_pairs={{0,8},{8,16},{16,24},{24,0},{1,9},{9,17},{17,25},{25,1},{2,10},{10... | collective-permute-start | bytes 1572872 | tf_op jit(solution)/shard_map/row_hop/ppermute | solution.py:58
  249.5 15.8 %collective-permute-start.39 = (bf16[128,2048]{1,0:T(8,128)(2,1)S(1)}, bf16[128,2048]{1,0:T(8,128)(2,1)S(1)}, u32[]{:S(2)}, u32[]{:S(2)}) collective-permute-start(bf16[128,2048]{1,0:T(8,128)(2,1)S(1)} %add_convert_fusion.4), channel_id=1, source_target_pairs={{0,8},{8,16},{16,24},{24,0},{1,9},{9,17},{17,25},{25,1},{2,10},{10... | collective-permute-start | bytes 1572872 | tf_op jit(solution)/shard_map/row_hop/ppermute | solution.py:58
  250.4 30.1 %collective-permute-start.41 = (bf16[144,2048]{1,0:T(8,128)(2,1)S(1)}, bf16[144,2048]{1,0:T(8,128)(2,1)S(1)}, u32[]{:S(2)}, u32[]{:S(2)}) collective-permute-start(bf16[144,2048]{1,0:T(8,128)(2,1)S(1)} %copy-done.48), channel_id=1, source_target_pairs={{0,2},{2,0},{1,3},{3,1},{4,6},{6,4},{5,7},{7,5},{8,10},{10,8},{9,1... | collective-permute-start | bytes 1769480 | tf_op jit(solution)/shard_map/made1/to_y/ppermute | solution.py:49
  251.9 28.6 %collective-permute-start.42 = (bf16[144,2048]{1,0:T(8,128)(2,1)S(1)}, bf16[144,2048]{1,0:T(8,128)(2,1)S(1)}, u32[]{:S(2)}, u32[]{:S(2)}) collective-permute-start(bf16[144,2048]{1,0:T(8,128)(2,1)S(1)} %copy-done.47), channel_id=1, source_target_pairs={{0,4},{4,0},{1,5},{5,1},{2,6},{6,2},{3,7},{7,3},{8,12},{12,8},{9,1... | collective-permute-start | bytes 1769480 | tf_op jit(solution)/shard_map/made1/to_x/ppermute | solution.py:49
  253.4 28.0 %collective-permute-start.43 = (bf16[144,2048]{1,0:T(8,128)(2,1)S(1)}, bf16[144,2048]{1,0:T(8,128)(2,1)S(1)}, u32[]{:S(2)}, u32[]{:S(2)}) collective-permute-start(bf16[144,2048]{1,0:T(8,128)(2,1)S(1)} %copy-done.46), channel_id=1, source_target_pairs={{0,6},{2,4},{4,2},{6,0},{1,7},{3,5},{5,3},{7,1},{8,14},{10,12},{12... | collective-permute-start | bytes 1769480 | tf_op jit(solution)/shard_map/made1/to_xy/ppermute | solution.py:53
  265.5 15.0 %collective-permute-start.40 = (bf16[128,2048]{1,0:T(8,128)(2,1)S(1)}, bf16[128,2048]{1,0:T(8,128)(2,1)S(1)}, u32[]{:S(2)}, u32[]{:S(2)}) collective-permute-start(bf16[128,2048]{1,0:T(8,128)(2,1)S(1)} %add_convert_fusion.3), channel_id=1, source_target_pairs={{0,8},{8,16},{16,24},{24,0},{1,9},{9,17},{17,25},{25,1},{2,10},{10... | collective-permute-start | bytes 1572872 | tf_op jit(solution)/shard_map/row_hop/ppermute | solution.py:58
  288.6 33.2 %collective-permute-start.48 = (bf16[144,2048]{1,0:T(8,128)(2,1)}, bf16[144,2048]{1,0:T(8,128)(2,1)S(1)}, u32[]{:S(2)}, u32[]{:S(2)}) collective-permute-start(bf16[144,2048]{1,0:T(8,128)(2,1)} %get-tuple-element.176), channel_id=1, source_target_pairs={{0,2},{2,0},{1,3},{3,1},{4,6},{6,4},{5,7},{7,5},{8,10},{10,8},{9,1... | collective-permute-start | bytes 1769480 | tf_op jit(solution)/shard_map/made0/to_y/ppermute | solution.py:49
  290.2 32.5 %collective-permute-start.49 = (bf16[144,2048]{1,0:T(8,128)(2,1)}, bf16[144,2048]{1,0:T(8,128)(2,1)S(1)}, u32[]{:S(2)}, u32[]{:S(2)}) collective-permute-start(bf16[144,2048]{1,0:T(8,128)(2,1)} %get-tuple-element.177), channel_id=1, source_target_pairs={{0,4},{4,0},{1,5},{5,1},{2,6},{6,2},{3,7},{7,3},{8,12},{12,8},{9,1... | collective-permute-start | bytes 1769480 | tf_op jit(solution)/shard_map/made0/to_x/ppermute | solution.py:49
  291.7 31.8 %collective-permute-start.50 = (bf16[144,2048]{1,0:T(8,128)(2,1)}, bf16[144,2048]{1,0:T(8,128)(2,1)}, u32[]{:S(2)}, u32[]{:S(2)}) collective-permute-start(bf16[144,2048]{1,0:T(8,128)(2,1)} %get-tuple-element.178), channel_id=1, source_target_pairs={{0,6},{2,4},{4,2},{6,0},{1,7},{3,5},{5,3},{7,1},{8,14},{10,12},{12... | collective-permute-start | bytes 1769480 | tf_op jit(solution)/shard_map/made0/to_xy/ppermute | solution.py:53
  293.4 39.8 %collective-permute-start.45 = (bf16[128,2176]{1,0:T(8,128)(2,1)}, bf16[128,2176]{1,0:T(8,128)(2,1)}, u32[]{:S(2)}, u32[]{:S(2)}) collective-permute-start(bf16[128,2176]{1,0:T(8,128)(2,1)} %add_convert_fusion.2), channel_id=1, source_target_pairs={{0,24},{8,0},{16,8},{24,16},{1,25},{9,1},{17,9},{25,17},{2,26},{10... | collective-permute-start | bytes 1671176 | tf_op jit(solution)/shard_map/made_hop/ppermute | solution.py:73
  309.5 9.8 %collective-permute-start.46 = (bf16[256,512]{1,0:T(8,128)(2,1)}, bf16[256,512]{1,0:T(8,128)(2,1)S(1)}, u32[]{:S(2)}, u32[]{:S(2)}) collective-permute-start(bf16[256,512]{1,0:T(8,128)(2,1)} %get-tuple-element.167), channel_id=1, source_target_pairs={{8,0},{16,8},{24,16},{9,1},{17,9},{25,17},{10,2},{18,10},{26,18},{... | collective-permute-start | bytes 786440 | tf_op jit(solution)/shard_map/kv_back_hop/ppermute | solution.py:68
  320.4 16.4 %collective-permute-start.53 = (bf16[256,512]{1,0:T(8,128)(2,1)S(1)}, bf16[256,512]{1,0:T(8,128)(2,1)S(1)}, u32[]{:S(2)}, u32[]{:S(2)}) collective-permute-start(bf16[256,512]{1,0:T(8,128)(2,1)S(1)} %add_convert_fusion.7), channel_id=1, source_target_pairs={{8,0},{16,8},{24,16},{9,1},{17,9},{25,17},{10,2},{18,10},{26,18},{... | collective-permute-start | bytes 786440 | tf_op jit(solution)/shard_map/kv_back_hop/ppermute | solution.py:68
  333.1 24.6 %collective-permute-start.51 = (bf16[256,2176]{1,0:T(8,128)(2,1)S(1)}, bf16[256,2176]{1,0:T(8,128)(2,1)S(1)}, u32[]{:S(2)}, u32[]{:S(2)}) collective-permute-start(bf16[256,2176]{1,0:T(8,128)(2,1)S(1)} %get-tuple-element.180), channel_id=1, source_target_pairs={{0,1},{1,0},{2,3},{3,2},{4,5},{5,4},{6,7},{7,6},{8,9},{9,8},{10,11... | collective-permute-start | bytes 3342344 | tf_op jit(solution)/shard_map/made0/sum_flip/ppermute | solution.py:49
  334.5 23.2 %collective-permute-start.47 = (bf16[128,2176]{1,0:T(8,128)(2,1)S(1)}, bf16[128,2176]{1,0:T(8,128)(2,1)S(1)}, u32[]{:S(2)}, u32[]{:S(2)}) collective-permute-start(bf16[128,2176]{1,0:T(8,128)(2,1)S(1)} %add_convert_fusion.1), channel_id=1, source_target_pairs={{0,24},{8,0},{16,8},{24,16},{1,25},{9,1},{17,9},{25,17},{2,26},{10... | collective-permute-start | bytes 1671176 | tf_op jit(solution)/shard_map/made_hop/ppermute | solution.py:73
  337.0 19.1 %collective-permute-start.54 = (bf16[256,512]{1,0:T(8,128)(2,1)S(1)}, bf16[256,512]{1,0:T(8,128)(2,1)S(1)}, u32[]{:S(2)}, u32[]{:S(2)}) collective-permute-start(bf16[256,512]{1,0:T(8,128)(2,1)S(1)} %add_convert_fusion.6), channel_id=1, source_target_pairs={{8,0},{16,8},{24,16},{9,1},{17,9},{25,17},{10,2},{18,10},{26,18},{... | collective-permute-start | bytes 786440 | tf_op jit(solution)/shard_map/kv_back_hop/ppermute | solution.py:68
  356.2 5.4 %collective-permute-start.55 = (bf16[128,512]{1,0:T(8,128)(2,1)S(1)}, bf16[128,512]{1,0:T(8,128)(2,1)}, u32[]{:S(2)}, u32[]{:S(2)}) collective-permute-start(bf16[128,512]{1,0:T(8,128)(2,1)S(1)} %slice.106), channel_id=1, source_target_pairs={{0,4},{4,0},{1,5},{5,1},{2,6},{6,2},{3,7},{7,3},{8,12},{12,8},{9,1... | collective-permute-start | bytes 393224 | tf_op jit(solution)/shard_map/kv_back_flip/ppermute | solution.py:49
  358.9 14.3 %collective-permute-start.52 = (bf16[128,2176]{1,0:T(8,128)(2,1)}, bf16[128,2176]{1,0:T(8,128)(2,1)S(1)}, u32[]{:S(2)}, u32[]{:S(2)}) collective-permute-start(bf16[128,2176]{1,0:T(8,128)(2,1)} %add_convert_fusion), channel_id=1, source_target_pairs={{0,24},{8,0},{16,8},{24,16},{1,25},{9,1},{17,9},{25,17},{2,26},{10... | collective-permute-start | bytes 1671176 | tf_op jit(solution)/shard_map/made_hop/ppermute | solution.py:73
  (60 other events, 532.1 us)
